TPU v7x, 256 devices: a whole 4x4x8 slice. The times are simulated.
256 devices in a mesh: seq: 64 (over z, x, core), section: 4 (over y).
Axes of the slice: x: 4, y: 4, z: 8, core: 2. Of those that a mesh axis runs over, the one named last changes fastest.
Arguments:
- enc_out: bfloat16 [32768, 4096], P('seq'), may hold values from -6 to 6
- span_len: int32 [64, 192], P('seq'), may hold values from 0 to 497, as said below
- skip_rows: bfloat16 [32768, 1024], P('seq', 'section'), may hold values from -6 to 6
- norm_gain: float32 [4096], replicated, may hold values from 0.1 to 1.9
- w_query: bfloat16 [4096, 2048], P(None, 'section'), may hold values from -3 to 3
- w_key: bfloat16 [4096, 512], P(None, 'section'), may hold values from -3 to 3
- w_value: bfloat16 [4096, 512], P(None, 'section'), may hold values from -0.09375 to 0.09375
- w_out: bfloat16 [2048, 1024], P('section'), may hold values from -0.125 to 0.125
- conv_kernel: float32 [31, 1024], P(None, 'section'), may hold values from -1 to 1
Outputs:
- decoded: bfloat16 [32768, 1024], P('seq', 'section')
Inputs may be any that keep to these rules, and one draw needn't show every extreme that they name: `span_len`: row d lists the lengths of the spans that start in the bytes of index d of seq: its first entries are positive and sum to 512, the rest are 0. Rows hold between 16 and 192 spans and some row holds exactly 192; all rows together hold 4096 spans. Some row holds exactly 16 spans, the first of them as long as the maximum.
All inputs are finite; a program needn't handle non-finite values.
Results may differ from a plain program's by a relative error of at most 0.015.
Values may be sent and summed in bfloat16 or wider, within the bound.
No kernel may reach another device: no remote copies, remote signals or barrier semaphores. Data moves between devices by JAX's collectives and lax.ppermute only.
A program may use at most 64 MiB of HBM per device.

v0:
```python
import math

import jax
import jax.numpy as jnp
from jax import lax
from jax.experimental import pallas as pl
from jax.experimental.pallas import tpu as pltpu
from jax.sharding import PartitionSpec as P

HD = 128
CAP = 192
TILE = 16
ROWS = CAP + TILE
NX = 4
NZ = 8
HALF = 384
UPPER = HALF + TILE
PIECE = UPPER + HALF
QT = 96
KEYS = 512
POOL_STEPS = 4
FULL = 63
QUERY_LIMIT = 62
HALO = 32
LOG2E = math.log2(math.e)
NEG = -1e30
MIB = 1 << 20
BF = jnp.bfloat16
F32 = jnp.float32


def vmem():
    return pl.BlockSpec(memory_space=pltpu.VMEM)


def anywhere():
    return pl.BlockSpec(memory_space=pl.ANY)


def params(limit=48):
    return pltpu.CompilerParams(vmem_limit_bytes=limit * MIB)


def iota(shape, dim):
    return lax.broadcasted_iota(jnp.int32, shape, dim)


def pool_kernel(len_hbm, gain_hbm, enc_hbm, wk_hbm, wv_hbm, kv_ref, x_hbm, scale_ref, lengths, gain, enc, wkv, x, sems):
    byte_rows, width = enc.shape
    block = width // POOL_STEPS
    small = [
        pltpu.make_async_copy(len_hbm, lengths, sems.at[0]),
        pltpu.make_async_copy(gain_hbm, gain, sems.at[1]),
    ]
    for copy in small:
        copy.start()
    copies = []
    for step in range(POOL_STEPS):
        part = pl.ds(step * block, block)
        at = 2 + 3 * step
        group = [
            pltpu.make_async_copy(enc_hbm.at[:, part], enc.at[:, part], sems.at[at]),
            pltpu.make_async_copy(wk_hbm.at[part], wkv.at[part, pl.ds(0, HD)], sems.at[at + 1]),
            pltpu.make_async_copy(wv_hbm.at[part], wkv.at[part, pl.ds(HD, HD)], sems.at[at + 2]),
        ]
        for copy in group:
            copy.start()
        copies.append(group)
    for copy in small:
        copy.wait()
    before = iota((CAP, CAP), 1) < iota((CAP, CAP), 0)
    start = jnp.sum(jnp.where(before, lengths[...], 0).astype(F32), axis=1, keepdims=True)
    hot = jnp.where(iota((CAP, byte_rows), 1).astype(F32) == start, 1.0, 0.0).astype(BF)
    total = jnp.zeros((CAP, 2 * HD), F32)
    squares = jnp.zeros((CAP, HD), F32)
    leaving = []
    held = None
    for step in range(POOL_STEPS + 1):
        if step < POOL_STEPS:
            for copy in copies[step]:
                copy.wait()
        if held is not None:
            last = slice((step - 1) * block, step * block)
            total += jnp.dot(held, wkv[last, :], preferred_element_type=F32)
        if step < POOL_STEPS:
            part = slice(step * block, (step + 1) * block)
            pooled = jnp.dot(hot, enc[:, part], preferred_element_type=F32)
            for k in range(block // HD):
                piece = pooled[:, k * HD : (k + 1) * HD]
                squares += piece * piece
            held = (pooled * gain[:, part]).astype(BF)
            x[:, part] = held
            leaving.append(
                pltpu.make_async_copy(
                    x.at[:, pl.ds(step * block, block)],
                    x_hbm.at[:, pl.ds(step * block, block)],
                    sems.at[2 + 3 * POOL_STEPS + step],
                )
            )
            leaving[-1].start()
    scale = lax.rsqrt(jnp.sum(squares, axis=1, keepdims=True) / width + 1e-5)
    scale_ref[...] = jnp.broadcast_to(scale, scale_ref.shape)
    kv_ref[:CAP, :] = (total * scale).astype(BF)
    count = jnp.sum((lengths[...] > 0).astype(F32), axis=1, keepdims=True)
    kv_ref[CAP:, :] = jnp.broadcast_to(count, (TILE, 2 * HD)).astype(BF)
    for copy in leaving:
        copy.wait()


def pool(lengths, enc, gain, wk, wv):
    byte_rows, width = enc.shape
    return pl.pallas_call(
        pool_kernel,
        in_specs=[anywhere()] * 5,
        out_specs=[vmem(), anywhere(), vmem()],
        out_shape=[
            jax.ShapeDtypeStruct((ROWS, 2 * HD), BF),
            jax.ShapeDtypeStruct((CAP, width), BF),
            jax.ShapeDtypeStruct((CAP, HD), F32),
        ],
        scratch_shapes=[
            pltpu.VMEM(lengths.shape, jnp.int32),
            pltpu.VMEM(gain.shape, F32),
            pltpu.VMEM((byte_rows, width), BF),
            pltpu.VMEM((width, 2 * HD), BF),
            pltpu.VMEM((CAP, width), BF),
            pltpu.SemaphoreType.DMA((4 * POOL_STEPS + 2,)),
        ],
        compiler_params=params(FULL),
        cost_estimate=pl.CostEstimate(
            flops=2 * CAP * width * (byte_rows + 2 * HD),
            bytes_accessed=2 * width * (byte_rows + CAP + 2 * HD),
            transcendentals=0,
        ),
        name="pool",
    )(lengths, gain, enc, wk, wv)


def query_kernel(x_hbm, scale_ref, wq_hbm, q_ref, x, wq, sems):
    width = wq.shape[0]
    block = width // POOL_STEPS
    copies = []
    for step in range(POOL_STEPS):
        part = pl.ds(step * block, block)
        copies.append(
            [
                pltpu.make_async_copy(wq_hbm.at[part], wq.at[part], sems.at[2 * step]),
                pltpu.make_async_copy(x_hbm.at[:, part], x.at[:, part], sems.at[2 * step + 1]),
            ]
        )
        for copy in copies[-1]:
            copy.start()
    total = jnp.zeros(q_ref.shape, F32)
    for step in range(POOL_STEPS):
        for copy in copies[step]:
            copy.wait()
        part = slice(step * block, (step + 1) * block)
        total += jnp.dot(x[:, part], wq[part, :], preferred_element_type=F32)
    q_ref[...] = (total * (scale_ref[:, :1] * (LOG2E * HD**-0.5))).astype(BF)


def query(x, wq, scale):
    width, out = wq.shape
    return pl.pallas_call(
        query_kernel,
        in_specs=[anywhere(), vmem(), anywhere()],
        out_specs=vmem(),
        out_shape=jax.ShapeDtypeStruct((CAP, out), BF),
        scratch_shapes=[
            pltpu.VMEM((CAP, width), BF),
            pltpu.VMEM((width, out), BF),
            pltpu.SemaphoreType.DMA((2 * POOL_STEPS,)),
        ],
        compiler_params=params(QUERY_LIMIT),
        cost_estimate=pl.CostEstimate(
            flops=2 * CAP * width * out, bytes_accessed=2 * width * (out + CAP), transcendentals=0
        ),
        name="query",
    )(x, scale, wq)


def compact_kernel(index_ref, *refs):
    blocks, out_ref = refs[:8], refs[8]
    x, core = index_ref[1], index_ref[2]
    shifts = (0, 1, 3, 2)
    order = [
        ((x + NX - shift) % NX) * 2 + (core if side == 0 else 1 - core)
        for side in range(2)
        for shift in shifts
    ]
    counts = [ref[CAP : CAP + TILE, :].astype(F32)[:1, :] for ref in blocks]
    lane = iota((1, CAP), 1).astype(F32)
    targets = []
    for i in range(8):
        first = jnp.zeros((1, 2 * HD), F32)
        for k in range(8):
            if k != i:
                first += jnp.where(order[k] < order[i], counts[k], 0.0)
        targets.append(jnp.where(lane < counts[i][:, :CAP], first[:, :CAP] + lane, -1.0))
    sub = iota((TILE, 2 * HD), 0)
    table = jnp.zeros((TILE, 2 * HD), F32)
    for i in range(8):
        table += jnp.where(sub == order[i], counts[i], 0.0)
    out_ref[HALF:UPPER, :] = table.astype(BF)
    for half in range(2):
        row = (iota((HALF, CAP), 0) + half * HALF).astype(F32)
        total = jnp.zeros((HALF, 2 * HD), F32)
        for i in range(8):
            hot = jnp.where(row == targets[i], 1.0, 0.0).astype(BF)
            total += jnp.dot(hot, blocks[i][:CAP, :], preferred_element_type=F32)
        out_ref[half * UPPER : half * UPPER + HALF, :] = total.astype(BF)


def compact(index, blocks):
    return pl.pallas_call(
        compact_kernel,
        in_specs=[pl.BlockSpec(memory_space=pltpu.SMEM)] + [vmem()] * 8,
        out_specs=vmem(),
        out_shape=jax.ShapeDtypeStruct((PIECE, 2 * HD), BF),
        compiler_params=params(),
        name="compact",
    )(index, *blocks)


def attend_kernel(index_ref, len_ref, q_ref, wout_ref, *refs):
    n_in = 9
    pieces, outs, flag_ref = refs[:n_in], refs[n_in : n_in + 4], refs[n_in + 4]
    keys, values, scores, top, acc, lsum = refs[n_in + 5 :]
    z, x, core, y = index_ref[0], index_ref[1], index_ref[2], index_ref[3]
    own = x * 2 + core
    for out in outs:
        out[...] = jnp.zeros_like(out)

    own_piece, came, swapped = pieces[0], pieces[1:5], pieces[5:9]
    upward, downward = (came, swapped), (swapped, came)

    def plain(refs):
        return [[(ref, 0, 0), (ref, UPPER, HALF)] for ref in refs]

    planes = [(8 - s, plain([downward[c][s - 1] for c in range(2)])) for s in (1, 2, 3)]
    planes.append((4, [[(upward[c][3], 0, 0), (downward[c][3], TILE, HALF)] for c in range(2)]))
    planes += [(s, plain([upward[c][s - 1] for c in range(2)])) for s in (3, 2, 1)]
    planes.append((0, plain([own_piece, own_piece])))

    def table(back, halves):
        found = [ref[HALF:UPPER, :HD].astype(F32) for (ref, _, _), _ in halves]
        return jnp.where(core == 0, found[0], found[1]) if back else found[0]

    def single(value):
        return jnp.max(jnp.sum(value, axis=0, keepdims=True)).astype(jnp.int32)

    lives = [single(table(back, halves)) for back, halves in planes]
    most = lives[0]
    for live in lives[1:]:
        most = jnp.maximum(most, live)
    flag_ref[0] = (most > 2 * HALF).astype(jnp.int32)
    own_table = table(*planes[-1])
    row = iota((TILE, HD), 0)
    before = single(jnp.where(row < own, own_table, 0.0))
    count = single(jnp.where(row == own, own_table, 0.0))

    first = jnp.int32(0)
    half_row = iota((HALF, HD), 0)
    for (back, halves), live in zip(planes, lives):
        here = jnp.minimum(live, 2 * HALF)
        for c in range(2 if back else 1):
            wanted = (z >= back) & (core == c) if back else z >= 0

            @pl.when(wanted)
            def _(moves=halves[c], here=here, first=first):
                for ref, low, to_row in moves:
                    to = pl.ds(pl.multiple_of(first + to_row, TILE), HALF)
                    keys[to, :HD] = ref[low : low + HALF, :HD]
                    values[to, :] = ref[low : low + HALF, HD:]
                    dead = jnp.where(half_row + to_row < here, 0.0, NEG)
                    keys[to, HD:] = dead.astype(BF)

        if back:
            first = first + jnp.where(z >= back, (here + TILE - 1) // TILE * TILE, 0)
    end = pl.ds(pl.multiple_of(first + 2 * HALF, TILE), KEYS)
    keys[end, :] = jnp.zeros((KEYS, 2 * HD), BF)
    values[end, :] = jnp.zeros((KEYS, HD), BF)
    free = first // KEYS
    chunks = (first + before + count + KEYS - 1) // KEYS
    ones = jnp.where(iota((4 * QT, HD), 1) == 0, 1.0, 0.0).astype(BF)

    def per_tile(tile, _):
        slots = pl.ds(pl.multiple_of(tile * QT, QT), QT)
        q = jnp.concatenate([q_ref[slots, h * HD : (h + 1) * HD] for h in range(4)], axis=0)
        q = jnp.concatenate([q, ones], axis=1)
        top[...] = jnp.full(top.shape, NEG, F32)
        acc[...] = jnp.zeros_like(acc)
        lsum[...] = jnp.zeros_like(lsum)

        def score(c):
            rows = pl.ds(pl.multiple_of(c * KEYS, KEYS), KEYS)
            return lax.dot_general(
                q, keys[rows, :], (((1,), (1,)), ((), ())), preferred_element_type=F32
            )

        def keep(c, s):
            scores[c] = s
            best = top[...]
            for k in range(KEYS // HD):
                best = jnp.maximum(best, s[:, k * HD : (k + 1) * HD])
            top[...] = best

        def open_chunk(c, _):
            keep(c, score(c))
            return 0

        query_pos = first + before + tile * QT + iota((4 * QT, 1), 0) % QT

        def masked_chunk(c, _):
            allowed = c * KEYS + iota((4 * QT, KEYS), 1) <= query_pos
            keep(c, jnp.where(allowed, score(c), NEG))
            return 0

        lax.fori_loop(0, free, open_chunk, 0)
        lax.fori_loop(free, chunks, masked_chunk, 0)
        top[...] = jnp.broadcast_to(jnp.max(top[...], axis=1, keepdims=True), top.shape)

        def weigh(c, _):
            best = top[...]
            parts = [
                jnp.exp2(scores[c, :, k * HD : (k + 1) * HD] - best) for k in range(KEYS // HD)
            ]
            total = parts[0]
            for part in parts[1:]:
                total = total + part
            lsum[...] += total
            p = jnp.concatenate([part.astype(BF) for part in parts], axis=1)
            rows = pl.ds(pl.multiple_of(c * KEYS, KEYS), KEYS)
            acc[...] += jnp.dot(p, values[rows, :], preferred_element_type=F32)
            return 0

        lax.fori_loop(0, chunks, weigh, 0)
        a = (acc[...] / jnp.sum(lsum[...], axis=1, keepdims=True)).astype(BF)
        a = jnp.concatenate([a[h * QT : (h + 1) * QT, :] for h in range(4)], axis=1)
        for k in range(4):
            cols = pl.ds(pl.multiple_of(((y + k) % 4) * 256, 256), 256)
            outs[k][slots, :] = jnp.dot(
                a, wout_ref[:, cols], preferred_element_type=F32
            ).astype(BF)
        return 0

    lax.fori_loop(0, (count + QT - 1) // QT, per_tile, 0)


def attend(index, lengths, q, wout, pieces):
    most = 2 * NZ * HALF + KEYS
    *parts, flag = pl.pallas_call(
        attend_kernel,
        in_specs=[pl.BlockSpec(memory_space=pltpu.SMEM)] + [vmem()] * (3 + len(pieces)),
        out_specs=[vmem()] * 4 + [pl.BlockSpec(memory_space=pltpu.SMEM)],
        out_shape=[jax.ShapeDtypeStruct((CAP, 256), BF)] * 4
        + [jax.ShapeDtypeStruct((1,), jnp.int32)],
        scratch_shapes=[
            pltpu.VMEM((most, 2 * HD), BF),
            pltpu.VMEM((most, HD), BF),
            pltpu.VMEM((most // KEYS, 4 * QT, KEYS), F32),
            pltpu.VMEM((4 * QT, HD), F32),
            pltpu.VMEM((4 * QT, HD), F32),
            pltpu.VMEM((4 * QT, HD), F32),
        ],
        compiler_params=params(),
        name="attend",
    )(index, lengths, q, wout, *pieces)
    return parts, flag[0]


def attend_any(kv, q, lengths, wout, y):
    everyone = lax.all_gather(kv, "seq", axis=0)
    device = lax.axis_index("seq")
    queries = q.reshape(CAP, 4, HD)
    slot = jnp.arange(CAP, dtype=jnp.int32)

    def step(carry, part):
        top, total, weighted = carry
        block, source = part
        keys, values = block[:CAP, :HD], block[:CAP, HD:]
        live = block[CAP, 0].astype(jnp.int32)
        s = jnp.einsum("wgd,rd->wgr", queries, keys, preferred_element_type=F32)
        later = (source == device) & (slot[None, :] > slot[:, None])
        allowed = ((slot < live)[None, :] & (source <= device) & ~later)[:, None, :]
        s = jnp.where(allowed, s, NEG)
        new = jnp.maximum(top, jnp.max(s, axis=2))
        factor = jnp.exp2(top - new)
        w = jnp.where(allowed, jnp.exp2(s - new[..., None]), 0.0)
        total = total * factor + jnp.sum(w, axis=2)
        weighted = weighted * factor[..., None] + jnp.einsum(
            "wgr,rd->wgd", w.astype(BF), values, preferred_element_type=F32
        )
        return (new, total, weighted), None

    start = (
        jnp.full((CAP, 4), NEG, F32),
        jnp.zeros((CAP, 4), F32),
        jnp.zeros((CAP, 4, HD), F32),
    )
    sources = jnp.arange(everyone.shape[0], dtype=jnp.int32)
    (_, total, weighted), _ = lax.scan(step, start, (everyone, sources))
    a = (weighted / total[..., None]).reshape(CAP, 4 * HD).astype(BF)
    part = jnp.dot(a, wout, preferred_element_type=F32).astype(BF)
    return [lax.dynamic_slice_in_dim(part, ((y + k) % 4) * 256, 256, 1) for k in range(4)]


def mix_kernel(len_ref, skip_ref, p0, p1, p2, p3, mixed_ref, tail_ref):
    byte_rows = skip_ref.shape[0]
    lengths = len_ref[...].astype(F32)
    inner = p0[...].astype(F32) + p1[...].astype(F32) + p2[...].astype(F32) + p3[...].astype(F32)
    i, j = iota((CAP, CAP), 0), iota((CAP, CAP), 1)
    column = jnp.sum(jnp.where(i == j, lengths, 0.0), axis=1, keepdims=True)
    start = jnp.sum(jnp.where(i < j, column, 0.0), axis=0, keepdims=True)
    at = iota((byte_rows, CAP), 0).astype(F32)
    hot = jnp.where((at >= start) & (at < start + lengths), 1.0, 0.0).astype(BF)
    up = jnp.dot(hot, inner.astype(BF), preferred_element_type=F32)
    mixed = (skip_ref[...].astype(F32) + up).astype(BF)
    mixed_ref[...] = mixed
    tail_ref[...] = mixed[byte_rows - HALO :, :]


def mix(lengths, skip, parts):
    return pl.pallas_call(
        mix_kernel,
        in_specs=[vmem()] * 6,
        out_specs=[vmem()] * 2,
        out_shape=[
            jax.ShapeDtypeStruct(skip.shape, BF),
            jax.ShapeDtypeStruct((HALO, skip.shape[1]), BF),
        ],
        compiler_params=params(),
        name="mix",
    )(lengths, skip, *parts)


def filtered(window, taps):
    rows = window.shape[0] - HALO
    total = jnp.zeros((rows, window.shape[1]), F32)
    lags = taps.shape[0]
    for r in range(8):
        moved = window[8 - r : rows + HALO - r, :]
        for lag in range(r, lags, 8):
            low = HALO - 8 - (lag - r)
            total += taps[lag : lag + 1, :] * moved[low : low + rows, :]
    return (window[HALO:, :] + total / (1.0 + jnp.exp(-total))).astype(BF)


def conv_kernel(mixed_ref, taps_ref, out_ref, ext):
    byte_rows, channels = mixed_ref.shape
    ext[:HALO, :] = jnp.zeros((HALO, channels), F32)
    ext[HALO:, :] = mixed_ref[...].astype(F32)
    block = 64

    def per_block(i, _):
        first = pl.multiple_of(i * block, block)
        for low in range(0, channels, 128):
            part = slice(low, low + 128)
            window = ext[pl.ds(first, block + HALO), part]
            out_ref[pl.ds(first, block), part] = filtered(window, taps_ref[:, part])
        return 0

    lax.fori_loop(0, byte_rows // block, per_block, 0)


def rim_kernel(given_hbm, rim_ref, mixed_ref, taps_ref, out_hbm, rows, sem):
    del given_hbm
    for low in range(0, mixed_ref.shape[1], 128):
        part = slice(low, low + 128)
        window = jnp.concatenate([rim_ref[:, part], mixed_ref[:HALO, part]], axis=0).astype(F32)
        rows[:, part] = filtered(window, taps_ref[:, part])
    copy = pltpu.make_async_copy(rows, out_hbm.at[pl.ds(0, HALO)], sem)
    copy.start()
    copy.wait()


def convolve(mixed, taps):
    return pl.pallas_call(
        conv_kernel,
        in_specs=[vmem()] * 2,
        out_specs=vmem(),
        out_shape=jax.ShapeDtypeStruct(mixed.shape, BF),
        scratch_shapes=[pltpu.VMEM((HALO + mixed.shape[0], mixed.shape[1]), F32)],
        compiler_params=params(),
        cost_estimate=pl.CostEstimate(
            flops=2 * mixed.size * taps.shape[0], bytes_accessed=16 * mixed.size, transcendentals=0
        ),
        name="convolve",
    )(mixed, taps)


def first_rows(given, rim, mixed, taps):
    return pl.pallas_call(
        rim_kernel,
        in_specs=[anywhere()] + [vmem()] * 3,
        out_specs=anywhere(),
        out_shape=jax.ShapeDtypeStruct(given.shape, BF),
        input_output_aliases={0: 0},
        scratch_shapes=[pltpu.VMEM((HALO, mixed.shape[1]), BF), pltpu.SemaphoreType.DMA],
        compiler_params=params(),
        name="first_rows",
    )(given, rim, mixed, taps)


def seq_permute(value, move):
    pairs = []
    for z in range(NZ):
        for x in range(NX):
            for core in range(2):
                tz, tx, tc = move(z, x, core)
                target = ((tz % NZ) * NX + tx % NX) * 2 + tc
                pairs.append(((z * NX + x) * 2 + core, target))
    return lax.ppermute(value, "seq", pairs)


def along_x(value, steps):
    return seq_permute(value, lambda z, x, c: (z, x + steps, c))


def round_z(value):
    return seq_permute(value, lambda z, x, c: (z + 1 - 2 * c, x, c))


def swap(value):
    return seq_permute(value, lambda z, x, c: (z, x, 1 - c))


def per_device(enc, span_len, skip, gain, wq, wk, wv, wout, taps):
    seq = lax.axis_index("seq")
    y = lax.axis_index("section")
    index = jnp.stack([seq // (2 * NX), (seq // 2) % NX, seq % 2, y]).astype(jnp.int32)
    kv, x, scale = pool(span_len, enc, gain.reshape(1, -1), wk, wv)
    there = [along_x(kv, 1), along_x(kv, -1), along_x(kv, 2)]
    there, q = lax.optimization_barrier((there, query(x, wq, scale)))
    column = [kv] + there
    plane = compact(index, column + [swap(v) for v in column])
    came = [round_z(plane)]
    came.append(round_z(came[-1]))
    came.append(round_z(came[-1]))
    came.append(round_z(lax.dynamic_slice_in_dim(came[-1], (seq % 2) * HALF, UPPER, 0)))
    pieces = [plane] + came + [swap(piece) for piece in came]
    parts, crowded = attend(index, span_len, q, wout, pieces)
    parts = lax.cond(
        crowded > 0, lambda _: attend_any(kv, q, span_len, wout, y), lambda given: given, parts
    )
    sent = [
        lax.ppermute(parts[k], "section", [(i, (i + k) % 4) for i in range(4)]) for k in (1, 2, 3)
    ]
    mixed, tail = mix(span_len, skip, [parts[0]] + sent)
    rim = lax.ppermute(tail, "seq", [(i, i + 1) for i in range(2 * NX * NZ - 1)])
    return first_rows(convolve(mixed, taps), rim, mixed, taps)


def solution(mesh):
    return jax.shard_map(
        per_device,
        mesh=mesh,
        in_specs=(
            P("seq", None),
            P("seq", None),
            P("seq", "section"),
            P(),
            P(None, "section"),
            P(None, "section"),
            P(None, "section"),
            P("section", None),
            P(None, "section"),
        ),
        out_specs=P("seq", "section"),
        check_vma=False,
    )
```

profile of v0, /device:TPU:128, one launch (start us, length us, event | category | flops | bytes accessed | tf_op | source)
XLA Modules:
  0.0 93.0 jit_solution(16221207013013212374)
XLA Ops:
  6.5 5.0 %pool.1 = (bf16[208,256]{1,0:T(8,128)(2,1)S(1)}, bf16[192,4096]{1,0:T(8,128)(2,1)}, f32[192,128]{1,0:T(8,128)}) custom-call(s32[1,192]{1,0:T(1,128)} %len_ref.3, f32[1,4096]{1,0:T(1,128)} %bitcast.51, bf16[512,4096]{1,0:T(8,128)(2,1)} %enc_hbm.1, bf16[4096,128]{1,0:T(8,128)(2,1)} %wk_hbm.1, bf16[4096,128]{1,0:T(8,128)(2,1)} %wv_hbm.1), custom_call_target="tpu_custom_call" | custom-call | flops 1207959552 | bytes 7864320 | tf_op jit(solution)/shard_map/pool/pallas_call | solution.py:112
  11.6 3.1 %collective-permute-start.2 = (bf16[208,256]{1,0:T(8,128)(2,1)S(1)}, bf16[208,256]{1,0:T(8,128)(2,1)S(1)}, u32[]{:S(2)}, u32[]{:S(2)}) collective-permute-start(bf16[208,256]{1,0:T(8,128)(2,1)S(1)} %get-tuple-element.94.refs_0_), channel_id=1, source_target_pairs={{0,16},{4,20},{8,24},{12,28},{16,0},{20,4},{24,8},{28,12},{32,48},... | collective-permute-start | bytes 319496 | tf_op jit(solution)/shard_map/ppermute | solution.py:513
  14.7 1.1 %collective-permute-start.1 = (bf16[208,256]{1,0:T(8,128)(2,1)S(1)}, bf16[208,256]{1,0:T(8,128)(2,1)S(1)}, u32[]{:S(2)}, u32[]{:S(2)}) collective-permute-start(bf16[208,256]{1,0:T(8,128)(2,1)S(1)} %get-tuple-element.94.refs_0_), channel_id=1, source_target_pairs={{0,24},{4,28},{8,0},{12,4},{16,8},{20,12},{24,16},{28,20},{32,56},... | collective-permute-start | bytes 319496 | tf_op jit(solution)/shard_map/ppermute | solution.py:513
  15.8 0.9 collective-permute-start
  16.7 4.0 %query.1.q_ref = bf16[192,512]{1,0:T(8,128)(2,1)S(1)} custom-call(bf16[192,4096]{1,0:T(8,128)(2,1)} %get-tuple-element.95.x_hbm, f32[192,128]{1,0:T(8,128)} %get-tuple-element.96.scale_ref, bf16[4096,512]{1,0:T(8,128)(2,1)} %wq_hbm.1), custom_call_target="tpu_custom_call" | custom-call | flops 805306368 | bytes 5767168 | tf_op jit(solution)/shard_map/query/pallas_call | solution.py:164
  20.7 1.0 %collective-permute-done.refs_1_ = bf16[208,256]{1,0:T(8,128)(2,1)S(1)} collective-permute-done((bf16[208,256]{1,0:T(8,128)(2,1)S(1)}, bf16[208,256]{1,0:T(8,128)(2,1)S(1)}, u32[]{:S(2)}, u32[]{:S(2)}) %collective-permute-start) | collective-permute-done | bytes 106528 | tf_op jit(solution)/shard_map/ppermute | solution.py:513
  21.7 0.5 collective-permute-start.5
  22.3 0.7 collective-permute-done.4.refs_5_
  23.1 0.2 collective-permute-done.5.refs_6_
  23.2 0.4 collective-permute-done.6.refs_7_
  23.6 1.5 %compact.1.refs_0_ = bf16[784,256]{1,0:T(8,128)(2,1)S(1)} custom-call(s32[4]{0:T(128)S(1)} %pad_add_fusion.index_ref, bf16[208,256]{1,0:T(8,128)(2,1)S(1)} %get-tuple-element.94.refs_0_, bf16[208,256]{1,0:T(8,128)(2,1)S(1)} %collective-permute-done.refs_1_, bf16[208,256]{1,0:T(8,128)(2,1)S(1)} %collective-permute-done.1.refs_2_, ...), custom_call_target="tpu_custom_call" | custom-call | tf_op jit(solution)/shard_map/compact/pallas_call | solution.py:215
  25.1 1.1 %collective-permute-start.7 = (bf16[784,256]{1,0:T(8,128)(2,1)S(1)}, bf16[784,256]{1,0:T(8,128)(2,1)S(1)}, u32[]{:S(2)}, u32[]{:S(2)}) collective-permute-start(bf16[784,256]{1,0:T(8,128)(2,1)S(1)} %compact.1.refs_0_), channel_id=1, source_target_pairs={{0,32},{4,228},{8,40},{12,236},{16,48},{20,244},{24,56},{28,252},{... | collective-permute-start | bytes 1204232 | tf_op jit(solution)/shard_map/ppermute | solution.py:513
  26.2 8.1 %collective-permute-done.7.refs_1_ = bf16[784,256]{1,0:T(8,128)(2,1)S(1)} collective-permute-done((bf16[784,256]{1,0:T(8,128)(2,1)S(1)}, bf16[784,256]{1,0:T(8,128)(2,1)S(1)}, u32[]{:S(2)}, u32[]{:S(2)}) %collective-permute-start.7) | collective-permute-done | bytes 401440 | tf_op jit(solution)/shard_map/ppermute | solution.py:513
  34.3 9.1 %collective-permute-done.8.refs_2_ = bf16[784,256]{1,0:T(8,128)(2,1)S(1)} collective-permute-done((bf16[784,256]{1,0:T(8,128)(2,1)S(1)}, bf16[784,256]{1,0:T(8,128)(2,1)S(1)}, u32[]{:S(2)}, u32[]{:S(2)}) %collective-permute-start.8) | collective-permute-done | bytes 401440 | tf_op jit(solution)/shard_map/ppermute | solution.py:513
  43.3 9.1 %collective-permute-done.9.refs_3_ = bf16[784,256]{1,0:T(8,128)(2,1)S(1)} collective-permute-done((bf16[784,256]{1,0:T(8,128)(2,1)S(1)}, bf16[784,256]{1,0:T(8,128)(2,1)S(1)}, u32[]{:S(2)}, u32[]{:S(2)}) %collective-permute-start.9) | collective-permute-done | bytes 401440 | tf_op jit(solution)/shard_map/ppermute | solution.py:513
  52.4 0.1 collective-permute-start.10
  52.5 0.1 collective-permute-start.11
  52.6 0.5 collective-permute-start.12
  53.1 0.1 collective-permute-start.13
  53.2 6.3 %collective-permute-done.10.refs_4_ = bf16[400,256]{1,0:T(8,128)(2,1)S(1)} collective-permute-done((bf16[400,256]{1,0:T(8,128)(2,1)S(1)}, bf16[400,256]{1,0:T(8,128)(2,1)S(1)}, u32[]{:S(2)}, u32[]{:S(2)}) %collective-permute-start.10) | collective-permute-done | bytes 204832 | tf_op jit(solution)/shard_map/ppermute | solution.py:513
  59.5 1.4 %collective-permute-done.14.refs_8_ = bf16[400,256]{1,0:T(8,128)(2,1)S(1)} collective-permute-done((bf16[400,256]{1,0:T(8,128)(2,1)S(1)}, bf16[400,256]{1,0:T(8,128)(2,1)S(1)}, u32[]{:S(2)}, u32[]{:S(2)}) %collective-permute-start.14) | collective-permute-done | bytes 204832 | tf_op jit(solution)/shard_map/ppermute | solution.py:513
  60.9 5.5 %attend.1 = (bf16[192,256]{1,0:T(8,128)(2,1)S(1)}, bf16[192,256]{1,0:T(8,128)(2,1)S(1)}, bf16[192,256]{1,0:T(8,128)(2,1)S(1)}, bf16[192,256]{1,0:T(8,128)(2,1)S(1)}, s32[1]{0:T(128)}) custom-call(s32[4]{0:T(128)S(1)} %pad_add_fusion.index_ref, s32[1,192]{1,0:T(1,128)S(1)} %copy-done.2, bf16[192,512]{1,0:T(8,128)(2,1)S(1)} %query.1.q_ref, ...), custom_call_target="tpu_custom_call" | custom-call | tf_op jit(solution)/shard_map/attend/pallas_call | solution.py:352
  67.1 1.6 %collective-permute-start.15 = (bf16[192,256]{1,0:T(8,128)(2,1)S(1)}, bf16[192,256]{1,0:T(8,128)(2,1)S(1)}, u32[]{:S(2)}, u32[]{:S(2)}) collective-permute-start(bf16[192,256]{1,0:T(8,128)(2,1)S(1)} %get-tuple-element.107), channel_id=1, source_target_pairs={{0,1},{1,2},{2,3},{3,0},{4,5},{5,6},{6,7},{7,4},{8,9},{9,10},{10,1... | collective-permute-start | bytes 294920 | tf_op jit(solution)/shard_map/ppermute | solution.py:547
  68.7 2.9 %collective-permute-start.16 = (bf16[192,256]{1,0:T(8,128)(2,1)S(1)}, bf16[192,256]{1,0:T(8,128)(2,1)S(1)}, u32[]{:S(2)}, u32[]{:S(2)}) collective-permute-start(bf16[192,256]{1,0:T(8,128)(2,1)S(1)} %get-tuple-element.108), channel_id=1, source_target_pairs={{0,2},{1,3},{2,0},{3,1},{4,6},{5,7},{6,4},{7,5},{8,10},{9,11},{10,... | collective-permute-start | bytes 294920 | tf_op jit(solution)/shard_map/ppermute | solution.py:547
  71.6 1.3 %collective-permute-start.17 = (bf16[192,256]{1,0:T(8,128)(2,1)S(1)}, bf16[192,256]{1,0:T(8,128)(2,1)S(1)}, u32[]{:S(2)}, u32[]{:S(2)}) collective-permute-start(bf16[192,256]{1,0:T(8,128)(2,1)S(1)} %get-tuple-element.109), channel_id=1, source_target_pairs={{0,3},{1,0},{2,1},{3,2},{4,7},{5,4},{6,5},{7,6},{8,11},{9,8},{10,9... | collective-permute-start | bytes 294920 | tf_op jit(solution)/shard_map/ppermute | solution.py:547
  73.0 0.3 collective-permute-done.15.p1
  73.3 3.3 %collective-permute-done.16.p2 = bf16[192,256]{1,0:T(8,128)(2,1)S(1)} collective-permute-done((bf16[192,256]{1,0:T(8,128)(2,1)S(1)}, bf16[192,256]{1,0:T(8,128)(2,1)S(1)}, u32[]{:S(2)}, u32[]{:S(2)}) %collective-permute-start.16) | collective-permute-done | bytes 98336 | tf_op jit(solution)/shard_map/ppermute | solution.py:547
  76.6 0.3 mix.1
  76.9 1.9 %collective-permute-start.18 = (bf16[32,256]{1,0:T(8,128)(2,1)S(1)}, bf16[32,256]{1,0:T(8,128)(2,1)S(1)}, u32[]{:S(2)}, u32[]{:S(2)}) collective-permute-start(bf16[32,256]{1,0:T(8,128)(2,1)S(1)} %get-tuple-element.111), channel_id=1, source_target_pairs={{0,4},{4,8},{8,12},{12,16},{16,20},{20,24},{24,28},{28,32},{32,36}... | collective-permute-start | bytes 49160 | tf_op jit(solution)/shard_map/ppermute | solution.py:550
  78.8 3.6 %convolve.1.given_hbm = bf16[512,256]{1,0:T(8,128)(2,1)} custom-call(bf16[512,256]{1,0:T(8,128)(2,1)S(1)} %get-tuple-element.110.mixed_ref, f32[31,256]{1,0:T(8,128)S(1)} %copy-done.1), custom_call_target="tpu_custom_call" | custom-call | flops 8126464 | bytes 2097152 | tf_op jit(solution)/shard_map/convolve/pallas_call | solution.py:478
  82.4 2.9 %collective-permute-done.18.rim_ref = bf16[32,256]{1,0:T(8,128)(2,1)S(1)} collective-permute-done((bf16[32,256]{1,0:T(8,128)(2,1)S(1)}, bf16[32,256]{1,0:T(8,128)(2,1)S(1)}, u32[]{:S(2)}, u32[]{:S(2)}) %collective-permute-start.18) | collective-permute-done | bytes 16416 | tf_op jit(solution)/shard_map/ppermute | solution.py:550
  85.3 0.8 first_rows.1
  (24 shorter events, 0.2 us)
Async XLA Ops:
  11.5 49.4 %copy-start.2 = (s32[1,192]{1,0:T(1,128)S(1)}, s32[1,192]{1,0:T(1,128)}, u32[]{:S(2)}) copy-start(s32[1,192]{1,0:T(1,128)} %len_ref.3) | copy-start | bytes 2308
  11.6 49.4 %copy-start.3 = (bf16[512,1024]{1,0:T(8,128)(2,1)S(1)}, bf16[512,1024]{1,0:T(8,128)(2,1)}, u32[]{:S(2)}) copy-start(bf16[512,1024]{1,0:T(8,128)(2,1)} %wout_ref.1) | copy-start | bytes 3145732
  11.6 9.1 %collective-permute-start.2 = (bf16[208,256]{1,0:T(8,128)(2,1)S(1)}, bf16[208,256]{1,0:T(8,128)(2,1)S(1)}, u32[]{:S(2)}, u32[]{:S(2)}) collective-permute-start(bf16[208,256]{1,0:T(8,128)(2,1)S(1)} %get-tuple-element.94.refs_0_), channel_id=1, source_target_pairs={{0,16},{4,20},{8,24},{12,28},{16,0},{20,4},{24,8},{28,12},{32,48},... | collective-permute-start | bytes 319496 | tf_op jit(solution)/shard_map/ppermute | solution.py:513
  14.7 6.0 %collective-permute-start.1 = (bf16[208,256]{1,0:T(8,128)(2,1)S(1)}, bf16[208,256]{1,0:T(8,128)(2,1)S(1)}, u32[]{:S(2)}, u32[]{:S(2)}) collective-permute-start(bf16[208,256]{1,0:T(8,128)(2,1)S(1)} %get-tuple-element.94.refs_0_), channel_id=1, source_target_pairs={{0,24},{4,28},{8,0},{12,4},{16,8},{20,12},{24,16},{28,20},{32,56},... | collective-permute-start | bytes 319496 | tf_op jit(solution)/shard_map/ppermute | solution.py:513
  15.8 5.9 %collective-permute-start = (bf16[208,256]{1,0:T(8,128)(2,1)S(1)}, bf16[208,256]{1,0:T(8,128)(2,1)S(1)}, u32[]{:S(2)}, u32[]{:S(2)}) collective-permute-start(bf16[208,256]{1,0:T(8,128)(2,1)S(1)} %get-tuple-element.94.refs_0_), channel_id=1, source_target_pairs={{0,8},{4,12},{8,16},{12,20},{16,24},{20,28},{24,0},{28,4},{32,40},... | collective-permute-start | bytes 319496 | tf_op jit(solution)/shard_map/ppermute | solution.py:513
  16.7 5.6 %collective-permute-start.3 = (bf16[208,256]{1,0:T(8,128)(2,1)S(1)}, bf16[208,256]{1,0:T(8,128)(2,1)S(1)}, u32[]{:S(2)}, u32[]{:S(2)}) collective-permute-start(bf16[208,256]{1,0:T(8,128)(2,1)S(1)} %get-tuple-element.94.refs_0_), channel_id=1, source_target_pairs={{0,4},{4,0},{8,12},{12,8},{16,20},{20,16},{24,28},{28,24},{32,36},... | collective-permute-start | bytes 319496 | tf_op jit(solution)/shard_map/ppermute | solution.py:513
  21.7 1.3 %collective-permute-start.4 = (bf16[208,256]{1,0:T(8,128)(2,1)S(1)}, bf16[208,256]{1,0:T(8,128)(2,1)S(1)}, u32[]{:S(2)}, u32[]{:S(2)}) collective-permute-start(bf16[208,256]{1,0:T(8,128)(2,1)S(1)} %collective-permute-done.refs_1_), channel_id=1, source_target_pairs={{0,4},{4,0},{8,12},{12,8},{16,20},{20,16},{24,28},{28,24},{32,36},... | collective-permute-start | bytes 319496 | tf_op jit(solution)/shard_map/ppermute | solution.py:513
  21.7 1.5 %collective-permute-start.5 = (bf16[208,256]{1,0:T(8,128)(2,1)S(1)}, bf16[208,256]{1,0:T(8,128)(2,1)S(1)}, u32[]{:S(2)}, u32[]{:S(2)}) collective-permute-start(bf16[208,256]{1,0:T(8,128)(2,1)S(1)} %collective-permute-done.1.refs_2_), channel_id=1, source_target_pairs={{0,4},{4,0},{8,12},{12,8},{16,20},{20,16},{24,28},{28,24},{32,36},... | collective-permute-start | bytes 319496 | tf_op jit(solution)/shard_map/ppermute | solution.py:513
  22.2 1.3 %collective-permute-start.6 = (bf16[208,256]{1,0:T(8,128)(2,1)S(1)}, bf16[208,256]{1,0:T(8,128)(2,1)S(1)}, u32[]{:S(2)}, u32[]{:S(2)}) collective-permute-start(bf16[208,256]{1,0:T(8,128)(2,1)S(1)} %collective-permute-done.2.refs_3_), channel_id=1, source_target_pairs={{0,4},{4,0},{8,12},{12,8},{16,20},{20,16},{24,28},{28,24},{32,36},... | collective-permute-start | bytes 319496 | tf_op jit(solution)/shard_map/ppermute | solution.py:513
  25.1 9.2 %collective-permute-start.7 = (bf16[784,256]{1,0:T(8,128)(2,1)S(1)}, bf16[784,256]{1,0:T(8,128)(2,1)S(1)}, u32[]{:S(2)}, u32[]{:S(2)}) collective-permute-start(bf16[784,256]{1,0:T(8,128)(2,1)S(1)} %compact.1.refs_0_), channel_id=1, source_target_pairs={{0,32},{4,228},{8,40},{12,236},{16,48},{20,244},{24,56},{28,252},{... | collective-permute-start | bytes 1204232 | tf_op jit(solution)/shard_map/ppermute | solution.py:513
  34.3 9.1 %collective-permute-start.8 = (bf16[784,256]{1,0:T(8,128)(2,1)S(1)}, bf16[784,256]{1,0:T(8,128)(2,1)S(1)}, u32[]{:S(2)}, u32[]{:S(2)}) collective-permute-start(bf16[784,256]{1,0:T(8,128)(2,1)S(1)} %collective-permute-done.7.refs_1_), channel_id=1, source_target_pairs={{0,32},{4,228},{8,40},{12,236},{16,48},{20,244},{24,56},{28,252},{... | collective-permute-start | bytes 1204232 | tf_op jit(solution)/shard_map/ppermute | solution.py:513
  43.3 9.1 %collective-permute-start.9 = (bf16[784,256]{1,0:T(8,128)(2,1)S(1)}, bf16[784,256]{1,0:T(8,128)(2,1)S(1)}, u32[]{:S(2)}, u32[]{:S(2)}) collective-permute-start(bf16[784,256]{1,0:T(8,128)(2,1)S(1)} %collective-permute-done.8.refs_2_), channel_id=1, source_target_pairs={{0,32},{4,228},{8,40},{12,236},{16,48},{20,244},{24,56},{28,252},{... | collective-permute-start | bytes 1204232 | tf_op jit(solution)/shard_map/ppermute | solution.py:513
  52.4 7.0 %collective-permute-start.10 = (bf16[400,256]{1,0:T(8,128)(2,1)S(1)}, bf16[400,256]{1,0:T(8,128)(2,1)S(1)}, u32[]{:S(2)}, u32[]{:S(2)}) collective-permute-start(bf16[400,256]{1,0:T(8,128)(2,1)S(1)} %constant_dynamic-slice_fusion.4), channel_id=1, source_target_pairs={{0,32},{4,228},{8,40},{12,236},{16,48},{20,244},{24,56},{28,252},{... | collective-permute-start | bytes 614408 | tf_op jit(solution)/shard_map/ppermute | solution.py:513
  52.5 7.0 %collective-permute-start.11 = (bf16[784,256]{1,0:T(8,128)(2,1)S(1)}, bf16[784,256]{1,0:T(8,128)(2,1)S(1)}, u32[]{:S(2)}, u32[]{:S(2)}) collective-permute-start(bf16[784,256]{1,0:T(8,128)(2,1)S(1)} %collective-permute-done.7.refs_1_), channel_id=1, source_target_pairs={{0,4},{4,0},{8,12},{12,8},{16,20},{20,16},{24,28},{28,24},{32,36},... | collective-permute-start | bytes 1204232 | tf_op jit(solution)/shard_map/ppermute | solution.py:513
  52.6 6.9 %collective-permute-start.12 = (bf16[784,256]{1,0:T(8,128)(2,1)S(1)}, bf16[784,256]{1,0:T(8,128)(2,1)S(1)}, u32[]{:S(2)}, u32[]{:S(2)}) collective-permute-start(bf16[784,256]{1,0:T(8,128)(2,1)S(1)} %collective-permute-done.8.refs_2_), channel_id=1, source_target_pairs={{0,4},{4,0},{8,12},{12,8},{16,20},{20,16},{24,28},{28,24},{32,36},... | collective-permute-start | bytes 1204232 | tf_op jit(solution)/shard_map/ppermute | solution.py:513
  53.1 6.4 %collective-permute-start.13 = (bf16[784,256]{1,0:T(8,128)(2,1)S(1)}, bf16[784,256]{1,0:T(8,128)(2,1)S(1)}, u32[]{:S(2)}, u32[]{:S(2)}) collective-permute-start(bf16[784,256]{1,0:T(8,128)(2,1)S(1)} %collective-permute-done.9.refs_3_), channel_id=1, source_target_pairs={{0,4},{4,0},{8,12},{12,8},{16,20},{20,16},{24,28},{28,24},{32,36},... | collective-permute-start | bytes 1204232 | tf_op jit(solution)/shard_map/ppermute | solution.py:513
  59.5 1.5 %collective-permute-start.14 = (bf16[400,256]{1,0:T(8,128)(2,1)S(1)}, bf16[400,256]{1,0:T(8,128)(2,1)S(1)}, u32[]{:S(2)}, u32[]{:S(2)}) collective-permute-start(bf16[400,256]{1,0:T(8,128)(2,1)S(1)} %collective-permute-done.10.refs_4_), channel_id=1, source_target_pairs={{0,4},{4,0},{8,12},{12,8},{16,20},{20,16},{24,28},{28,24},{32,36},... | collective-permute-start | bytes 614408 | tf_op jit(solution)/shard_map/ppermute | solution.py:513
  67.1 9.5 %copy-start = (bf16[512,256]{1,0:T(8,128)(2,1)S(1)}, bf16[512,256]{1,0:T(8,128)(2,1)}, u32[]{:S(2)}) copy-start(bf16[512,256]{1,0:T(8,128)(2,1)} %skip_ref.1) | copy-start | bytes 786436
  67.1 11.8 %copy-start.1 = (f32[31,256]{1,0:T(8,128)S(1)}, f32[31,256]{1,0:T(8,128)}, u32[]{:S(2)}) copy-start(f32[31,256]{1,0:T(8,128)} %taps_ref.3) | copy-start | bytes 95236
  67.1 6.2 %collective-permute-start.15 = (bf16[192,256]{1,0:T(8,128)(2,1)S(1)}, bf16[192,256]{1,0:T(8,128)(2,1)S(1)}, u32[]{:S(2)}, u32[]{:S(2)}) collective-permute-start(bf16[192,256]{1,0:T(8,128)(2,1)S(1)} %get-tuple-element.107), channel_id=1, source_target_pairs={{0,1},{1,2},{2,3},{3,0},{4,5},{5,6},{6,7},{7,4},{8,9},{9,10},{10,1... | collective-permute-start | bytes 294920 | tf_op jit(solution)/shard_map/ppermute | solution.py:547
  68.7 7.8 %collective-permute-start.16 = (bf16[192,256]{1,0:T(8,128)(2,1)S(1)}, bf16[192,256]{1,0:T(8,128)(2,1)S(1)}, u32[]{:S(2)}, u32[]{:S(2)}) collective-permute-start(bf16[192,256]{1,0:T(8,128)(2,1)S(1)} %get-tuple-element.108), channel_id=1, source_target_pairs={{0,2},{1,3},{2,0},{3,1},{4,6},{5,7},{6,4},{7,5},{8,10},{9,11},{10,... | collective-permute-start | bytes 294920 | tf_op jit(solution)/shard_map/ppermute | solution.py:547
  71.6 4.9 %collective-permute-start.17 = (bf16[192,256]{1,0:T(8,128)(2,1)S(1)}, bf16[192,256]{1,0:T(8,128)(2,1)S(1)}, u32[]{:S(2)}, u32[]{:S(2)}) collective-permute-start(bf16[192,256]{1,0:T(8,128)(2,1)S(1)} %get-tuple-element.109), channel_id=1, source_target_pairs={{0,3},{1,0},{2,1},{3,2},{4,7},{5,4},{6,5},{7,6},{8,11},{9,8},{10,9... | collective-permute-start | bytes 294920 | tf_op jit(solution)/shard_map/ppermute | solution.py:547
  76.9 8.4 %collective-permute-start.18 = (bf16[32,256]{1,0:T(8,128)(2,1)S(1)}, bf16[32,256]{1,0:T(8,128)(2,1)S(1)}, u32[]{:S(2)}, u32[]{:S(2)}) collective-permute-start(bf16[32,256]{1,0:T(8,128)(2,1)S(1)} %get-tuple-element.111), channel_id=1, source_target_pairs={{0,4},{4,8},{8,12},{12,16},{16,20},{20,24},{24,28},{28,32},{32,36}... | collective-permute-start | bytes 49160 | tf_op jit(solution)/shard_map/ppermute | solution.py:550
where the time goes:
time: 93.6 us; the launch traced here: 93 us
  waiting for transfers between devices  42.6 us (46%)
  Pallas kernels  20.7 us (22%)
  starting transfers between devices  15.3 us (16%)
  between operations  14.2 us (15%)
    ppermute x15, waiting for transfers between devices, seq_permute(): return lax.ppermute(value, 'seq', pairs)  36.2 us
    ppermute x15, starting transfers between devices, seq_permute(): return lax.ppermute(value, 'seq', pairs)  7.53 us
    ppermute x3, starting transfers between devices, per_device(): lax.ppermute(parts[k], 'section', [(i, (i + k) % 4) for i in range(4)])  5.88 us
    pallas_call x1, Pallas kernels, attend(): pl.pallas_call(attend_kernel, in_specs=[pl.BlockSpec(memory_space=pltpu.S...  5.47 us
    pallas_call x1, Pallas kernels, pool(): pl.pallas_call(pool_kernel, in_specs=[anywhere()] * 5, out_specs=[vmem(),...  5 us
    pallas_call x1, Pallas kernels, query(): pl.pallas_call(query_kernel, in_specs=[anywhere(), vmem(), anywhere()], o...  3.95 us
    ppermute x3, waiting for transfers between devices, per_device(): lax.ppermute(parts[k], 'section', [(i, (i + k) % 4) for i in range(4)])  3.59 us
    pallas_call x1, Pallas kernels, convolve(): pl.pallas_call(conv_kernel, in_specs=[vmem()] * 2, out_specs=vmem(), out_...  3.56 us
  transfers between devices with their start and end apart: 19, of which 12 were waited for; matrix products, arithmetic and copies ran while one was open for 0% of the time, Pallas kernels for 8%

commit v1 on v0

--- a/solution.py
+++ b/solution.py
@@ -19,6 +19,7 @@
 QT = 96
 KEYS = 512
 POOL_STEPS = 4
+DEPTH = 2
 FULL = 63
 QUERY_LIMIT = 62
 HALO = 32
@@ -63,9 +64,10 @@
             pltpu.make_async_copy(wk_hbm.at[part], wkv.at[part, pl.ds(0, HD)], sems.at[at + 1]),
             pltpu.make_async_copy(wv_hbm.at[part], wkv.at[part, pl.ds(HD, HD)], sems.at[at + 2]),
         ]
-        for copy in group:
-            copy.start()
         copies.append(group)
+        if step < DEPTH:
+            for copy in group:
+                copy.start()
     for copy in small:
         copy.wait()
     before = iota((CAP, CAP), 1) < iota((CAP, CAP), 0)
@@ -79,6 +81,9 @@
         if step < POOL_STEPS:
             for copy in copies[step]:
                 copy.wait()
+            if step + DEPTH < POOL_STEPS:
+                for copy in copies[step + DEPTH]:
+                    copy.start()
         if held is not None:
             last = slice((step - 1) * block, step * block)
             total += jnp.dot(held, wkv[last, :], preferred_element_type=F32)
@@ -222,120 +227,188 @@
     )(index, *blocks)
 
 
-def attend_kernel(index_ref, len_ref, q_ref, wout_ref, *refs):
-    n_in = 9
-    pieces, outs, flag_ref = refs[:n_in], refs[n_in : n_in + 4], refs[n_in + 4]
-    keys, values, scores, top, acc, lsum = refs[n_in + 5 :]
-    z, x, core, y = index_ref[0], index_ref[1], index_ref[2], index_ref[3]
+def single(value):
+    return jnp.max(jnp.sum(value, axis=0, keepdims=True)).astype(jnp.int32)
+
+
+def table_of(ref):
+    return ref[HALF:UPPER, :HD].astype(F32)
+
+
+def heads_of(q_ref, slots):
+    q = jnp.concatenate([q_ref[slots, h * HD : (h + 1) * HD] for h in range(4)], axis=0)
+    ones = jnp.where(iota((4 * QT, HD), 1) == 0, 1.0, 0.0).astype(BF)
+    return jnp.concatenate([q, ones], axis=1)
+
+
+def place(keys, values, ref, low, to_row, first, live):
+    to = pl.ds(pl.multiple_of(first + to_row, TILE), HALF)
+    keys[to, :HD] = ref[low : low + HALF, :HD]
+    values[to, :] = ref[low : low + HALF, HD:]
+    dead = jnp.where(iota((HALF, HD), 0) + to_row < live, 0.0, NEG)
+    keys[to, HD:] = dead.astype(BF)
+
+
+def fill(keys, values, start, rows, bias):
+    end = pl.ds(pl.multiple_of(start, TILE), rows)
+    keys[end, :HD] = jnp.zeros((rows, HD), BF)
+    keys[end, HD:] = jnp.full((rows, HD), bias, BF)
+    values[end, :] = jnp.zeros((rows, HD), BF)
+
+
+def softmax_chunks(q, query_pos, free, chunks, keys, values, scores, top, lsum, acc):
+    def score(c):
+        rows = pl.ds(pl.multiple_of(c * KEYS, KEYS), KEYS)
+        return lax.dot_general(
+            q, keys[rows, :], (((1,), (1,)), ((), ())), preferred_element_type=F32
+        )
+
+    def keep(c, s):
+        scores[c] = s
+        best = top[...]
+        for k in range(KEYS // HD):
+            best = jnp.maximum(best, s[:, k * HD : (k + 1) * HD])
+        top[...] = best
+
+    def open_chunk(c, _):
+        keep(c, score(c))
+        return 0
+
+    def masked_chunk(c, _):
+        allowed = c * KEYS + iota((4 * QT, KEYS), 1) <= query_pos
+        keep(c, jnp.where(allowed, score(c), NEG))
+        return 0
+
+    lax.fori_loop(0, free, open_chunk, 0)
+    if query_pos is not None:
+        lax.fori_loop(free, chunks, masked_chunk, 0)
+    top[...] = jnp.broadcast_to(jnp.max(top[...], axis=1, keepdims=True), top.shape)
+
+    def weigh(c, _):
+        best = top[...]
+        parts = [jnp.exp2(scores[c, :, k * HD : (k + 1) * HD] - best) for k in range(KEYS // HD)]
+        total = parts[0]
+        for part in parts[1:]:
+            total = total + part
+        lsum[...] += total
+        p = jnp.concatenate([part.astype(BF) for part in parts], axis=1)
+        rows = pl.ds(pl.multiple_of(c * KEYS, KEYS), KEYS)
+        acc[...] += jnp.dot(p, values[rows, :], preferred_element_type=F32)
+        return 0
+
+    return weigh
+
+
+def attend_near_kernel(index_ref, q_ref, *refs):
+    pieces, (top, lsum, acc, info_ref) = refs[:7], refs[7:11]
+    keys, values, scores = refs[11:]
+    z, x, core = index_ref[0], index_ref[1], index_ref[2]
     own = x * 2 + core
-    for out in outs:
-        out[...] = jnp.zeros_like(out)
-
-    own_piece, came, swapped = pieces[0], pieces[1:5], pieces[5:9]
+
+    own_piece, came, swapped = pieces[0], pieces[1:4], pieces[4:7]
     upward, downward = (came, swapped), (swapped, came)
-
-    def plain(refs):
-        return [[(ref, 0, 0), (ref, UPPER, HALF)] for ref in refs]
-
-    planes = [(8 - s, plain([downward[c][s - 1] for c in range(2)])) for s in (1, 2, 3)]
-    planes.append((4, [[(upward[c][3], 0, 0), (downward[c][3], TILE, HALF)] for c in range(2)]))
-    planes += [(s, plain([upward[c][s - 1] for c in range(2)])) for s in (3, 2, 1)]
-    planes.append((0, plain([own_piece, own_piece])))
-
-    def table(back, halves):
-        found = [ref[HALF:UPPER, :HD].astype(F32) for (ref, _, _), _ in halves]
-        return jnp.where(core == 0, found[0], found[1]) if back else found[0]
-
-    def single(value):
-        return jnp.max(jnp.sum(value, axis=0, keepdims=True)).astype(jnp.int32)
-
-    lives = [single(table(back, halves)) for back, halves in planes]
-    most = lives[0]
-    for live in lives[1:]:
-        most = jnp.maximum(most, live)
-    flag_ref[0] = (most > 2 * HALF).astype(jnp.int32)
-    own_table = table(*planes[-1])
+    planes = [(8 - s, [downward[c][s - 1] for c in range(2)]) for s in (1, 2, 3)]
+    planes += [(s, [upward[c][s - 1] for c in range(2)]) for s in (3, 2, 1)]
+    planes.append((0, [own_piece, own_piece]))
+
+    lives, most = [], jnp.int32(0)
+    for back, (a, b) in planes:
+        table = jnp.where(core == 0, table_of(a), table_of(b)) if back else table_of(a)
+        lives.append(single(table))
+        most = jnp.maximum(most, lives[-1])
     row = iota((TILE, HD), 0)
+    own_table = table_of(own_piece)
     before = single(jnp.where(row < own, own_table, 0.0))
     count = single(jnp.where(row == own, own_table, 0.0))
+    info_ref[0] = most
+    info_ref[1] = count
 
     first = jnp.int32(0)
-    half_row = iota((HALF, HD), 0)
-    for (back, halves), live in zip(planes, lives):
+    for (back, where), live in zip(planes, lives):
         here = jnp.minimum(live, 2 * HALF)
         for c in range(2 if back else 1):
             wanted = (z >= back) & (core == c) if back else z >= 0
 
             @pl.when(wanted)
-            def _(moves=halves[c], here=here, first=first):
-                for ref, low, to_row in moves:
-                    to = pl.ds(pl.multiple_of(first + to_row, TILE), HALF)
-                    keys[to, :HD] = ref[low : low + HALF, :HD]
-                    values[to, :] = ref[low : low + HALF, HD:]
-                    dead = jnp.where(half_row + to_row < here, 0.0, NEG)
-                    keys[to, HD:] = dead.astype(BF)
+            def _(ref=where[c], here=here, first=first):
+                place(keys, values, ref, 0, 0, first, here)
+                place(keys, values, ref, UPPER, HALF, first, here)
 
         if back:
             first = first + jnp.where(z >= back, (here + TILE - 1) // TILE * TILE, 0)
-    end = pl.ds(pl.multiple_of(first + 2 * HALF, TILE), KEYS)
-    keys[end, :] = jnp.zeros((KEYS, 2 * HD), BF)
-    values[end, :] = jnp.zeros((KEYS, HD), BF)
+    fill(keys, values, first + 2 * HALF, KEYS, 0.0)
     free = first // KEYS
-    chunks = (first + before + count + KEYS - 1) // KEYS
-    ones = jnp.where(iota((4 * QT, HD), 1) == 0, 1.0, 0.0).astype(BF)
+    chunks = (first + jnp.minimum(before + count, 2 * HALF) + KEYS - 1) // KEYS
 
     def per_tile(tile, _):
         slots = pl.ds(pl.multiple_of(tile * QT, QT), QT)
-        q = jnp.concatenate([q_ref[slots, h * HD : (h + 1) * HD] for h in range(4)], axis=0)
-        q = jnp.concatenate([q, ones], axis=1)
-        top[...] = jnp.full(top.shape, NEG, F32)
-        acc[...] = jnp.zeros_like(acc)
-        lsum[...] = jnp.zeros_like(lsum)
-
-        def score(c):
-            rows = pl.ds(pl.multiple_of(c * KEYS, KEYS), KEYS)
-            return lax.dot_general(
-                q, keys[rows, :], (((1,), (1,)), ((), ())), preferred_element_type=F32
-            )
-
-        def keep(c, s):
-            scores[c] = s
-            best = top[...]
-            for k in range(KEYS // HD):
-                best = jnp.maximum(best, s[:, k * HD : (k + 1) * HD])
-            top[...] = best
-
-        def open_chunk(c, _):
-            keep(c, score(c))
-            return 0
-
+        mine = [ref.at[tile] for ref in (top, lsum, acc)]
+        mine[0][...] = jnp.full((4 * QT, HD), NEG, F32)
+        mine[1][...] = jnp.zeros((4 * QT, HD), F32)
+        mine[2][...] = jnp.zeros((4 * QT, HD), F32)
         query_pos = first + before + tile * QT + iota((4 * QT, 1), 0) % QT
-
-        def masked_chunk(c, _):
-            allowed = c * KEYS + iota((4 * QT, KEYS), 1) <= query_pos
-            keep(c, jnp.where(allowed, score(c), NEG))
-            return 0
-
-        lax.fori_loop(0, free, open_chunk, 0)
-        lax.fori_loop(free, chunks, masked_chunk, 0)
-        top[...] = jnp.broadcast_to(jnp.max(top[...], axis=1, keepdims=True), top.shape)
-
-        def weigh(c, _):
-            best = top[...]
-            parts = [
-                jnp.exp2(scores[c, :, k * HD : (k + 1) * HD] - best) for k in range(KEYS // HD)
-            ]
-            total = parts[0]
-            for part in parts[1:]:
-                total = total + part
-            lsum[...] += total
-            p = jnp.concatenate([part.astype(BF) for part in parts], axis=1)
-            rows = pl.ds(pl.multiple_of(c * KEYS, KEYS), KEYS)
-            acc[...] += jnp.dot(p, values[rows, :], preferred_element_type=F32)
-            return 0
-
+        weigh = softmax_chunks(
+            heads_of(q_ref, slots), query_pos, free, chunks, keys, values, scores, *mine
+        )
         lax.fori_loop(0, chunks, weigh, 0)
-        a = (acc[...] / jnp.sum(lsum[...], axis=1, keepdims=True)).astype(BF)
+        return 0
+
+    lax.fori_loop(0, (count + QT - 1) // QT, per_tile, 0)
+
+
+def attend_near(index, q, pieces):
+    most = 7 * 2 * HALF + KEYS
+    most = (most + KEYS - 1) // KEYS * KEYS
+    return pl.pallas_call(
+        attend_near_kernel,
+        in_specs=[pl.BlockSpec(memory_space=pltpu.SMEM)] + [vmem()] * (1 + len(pieces)),
+        out_specs=[vmem()] * 3 + [pl.BlockSpec(memory_space=pltpu.SMEM)],
+        out_shape=[jax.ShapeDtypeStruct((CAP // QT, 4 * QT, HD), F32)] * 3
+        + [jax.ShapeDtypeStruct((2,), jnp.int32)],
+        scratch_shapes=[
+            pltpu.VMEM((most, 2 * HD), BF),
+            pltpu.VMEM((most, HD), BF),
+            pltpu.VMEM((most // KEYS, 4 * QT, KEYS), F32),
+        ],
+        compiler_params=params(),
+        cost_estimate=pl.CostEstimate(
+            flops=12 * QT * most * 3 * HD * 2, bytes_accessed=1 << 23, transcendentals=8 * QT * most
+        ),
+        name="attend_near",
+    )(index, q, *pieces)
+
+
+def attend_far_kernel(index_ref, info_ref, q_ref, wout_ref, came, swapped, top, lsum, acc, *refs):
+    outs, flag_ref = refs[:4], refs[4]
+    keys, values, scores, peak, total, sums = refs[5:]
+    z, core, y = index_ref[0], index_ref[2], index_ref[3]
+    for out in outs:
+        out[...] = jnp.zeros_like(out)
+    live = single(table_of_far(came, core))
+    flag_ref[0] = (jnp.maximum(info_ref[0], live) > 2 * HALF).astype(jnp.int32)
+    count = info_ref[1]
+    here = jnp.minimum(live, 2 * HALF)
+    for c, lower, upper in ((0, came, swapped), (1, swapped, came)):
+
+        @pl.when(core == c)
+        def _(lower=lower, upper=upper):
+            place(keys, values, lower, 0, 0, 0, here)
+            place(keys, values, upper, TILE, HALF, 0, here)
+
+    fill(keys, values, 2 * HALF, 2 * KEYS - 2 * HALF, NEG)
+    chunks = jnp.where(z >= 4, (here + KEYS - 1) // KEYS, 0)
+
+    def per_tile(tile, _):
+        slots = pl.ds(pl.multiple_of(tile * QT, QT), QT)
+        peak[...] = top[tile]
+        weigh = softmax_chunks(
+            heads_of(q_ref, slots), None, chunks, chunks, keys, values, scores, peak, total, sums
+        )
+        factor = jnp.exp2(top[tile] - peak[...])
+        total[...] = lsum[tile] * factor
+        sums[...] = acc[tile] * factor
+        lax.fori_loop(0, chunks, weigh, 0)
+        a = (sums[...] / jnp.sum(total[...], axis=1, keepdims=True)).astype(BF)
         a = jnp.concatenate([a[h * QT : (h + 1) * QT, :] for h in range(4)], axis=1)
         for k in range(4):
             cols = pl.ds(pl.multiple_of(((y + k) % 4) * 256, 256), 256)
@@ -347,37 +420,39 @@
     lax.fori_loop(0, (count + QT - 1) // QT, per_tile, 0)
 
 
-def attend(index, lengths, q, wout, pieces):
-    most = 2 * NZ * HALF + KEYS
+def table_of_far(came, core):
+    low, high = came[:TILE, :HD].astype(F32), came[HALF:UPPER, :HD].astype(F32)
+    return jnp.where(core == 0, high, low)
+
+
+def attend_far(index, info, q, wout, came, swapped, state):
     *parts, flag = pl.pallas_call(
-        attend_kernel,
-        in_specs=[pl.BlockSpec(memory_space=pltpu.SMEM)] + [vmem()] * (3 + len(pieces)),
+        attend_far_kernel,
+        in_specs=[pl.BlockSpec(memory_space=pltpu.SMEM)] * 2 + [vmem()] * 7,
         out_specs=[vmem()] * 4 + [pl.BlockSpec(memory_space=pltpu.SMEM)],
         out_shape=[jax.ShapeDtypeStruct((CAP, 256), BF)] * 4
         + [jax.ShapeDtypeStruct((1,), jnp.int32)],
         scratch_shapes=[
-            pltpu.VMEM((most, 2 * HD), BF),
-            pltpu.VMEM((most, HD), BF),
-            pltpu.VMEM((most // KEYS, 4 * QT, KEYS), F32),
-            pltpu.VMEM((4 * QT, HD), F32),
-            pltpu.VMEM((4 * QT, HD), F32),
-            pltpu.VMEM((4 * QT, HD), F32),
-        ],
+            pltpu.VMEM((2 * KEYS, 2 * HD), BF),
+            pltpu.VMEM((2 * KEYS, HD), BF),
+            pltpu.VMEM((2, 4 * QT, KEYS), F32),
+        ]
+        + [pltpu.VMEM((4 * QT, HD), F32)] * 3,
         compiler_params=params(),
-        name="attend",
-    )(index, lengths, q, wout, *pieces)
+        name="attend_far",
+    )(index, info, q, wout, came, swapped, *state)
     return parts, flag[0]
 
 
 def attend_any(kv, q, lengths, wout, y):
-    everyone = lax.all_gather(kv, "seq", axis=0)
     device = lax.axis_index("seq")
+    devices = lax.axis_size("seq")
     queries = q.reshape(CAP, 4, HD)
     slot = jnp.arange(CAP, dtype=jnp.int32)
 
-    def step(carry, part):
-        top, total, weighted = carry
-        block, source = part
+    def step(turn, carry):
+        block, top, total, weighted = carry
+        source = (device - turn) % devices
         keys, values = block[:CAP, :HD], block[:CAP, HD:]
         live = block[CAP, 0].astype(jnp.int32)
         s = jnp.einsum("wgd,rd->wgr", queries, keys, preferred_element_type=F32)
@@ -391,15 +466,16 @@
         weighted = weighted * factor[..., None] + jnp.einsum(
             "wgr,rd->wgd", w.astype(BF), values, preferred_element_type=F32
         )
-        return (new, total, weighted), None
+        block = lax.ppermute(block, "seq", [(i, (i + 1) % devices) for i in range(devices)])
+        return block, new, total, weighted
 
     start = (
+        kv,
         jnp.full((CAP, 4), NEG, F32),
         jnp.zeros((CAP, 4), F32),
         jnp.zeros((CAP, 4, HD), F32),
     )
-    sources = jnp.arange(everyone.shape[0], dtype=jnp.int32)
-    (_, total, weighted), _ = lax.scan(step, start, (everyone, sources))
+    _, _, total, weighted = lax.fori_loop(0, devices, step, start)
     a = (weighted / total[..., None]).reshape(CAP, 4 * HD).astype(BF)
     part = jnp.dot(a, wout, preferred_element_type=F32).astype(BF)
     return [lax.dynamic_slice_in_dim(part, ((y + k) % 4) * 256, 256, 1) for k in range(4)]
@@ -530,16 +606,16 @@
     y = lax.axis_index("section")
     index = jnp.stack([seq // (2 * NX), (seq // 2) % NX, seq % 2, y]).astype(jnp.int32)
     kv, x, scale = pool(span_len, enc, gain.reshape(1, -1), wk, wv)
-    there = [along_x(kv, 1), along_x(kv, -1), along_x(kv, 2)]
-    there, q = lax.optimization_barrier((there, query(x, wq, scale)))
-    column = [kv] + there
+    column = [kv, along_x(kv, 1), along_x(kv, -1), along_x(kv, 2)]
     plane = compact(index, column + [swap(v) for v in column])
-    came = [round_z(plane)]
+    first, q = lax.optimization_barrier((round_z(plane), query(x, wq, scale)))
+    came = [first]
     came.append(round_z(came[-1]))
     came.append(round_z(came[-1]))
-    came.append(round_z(lax.dynamic_slice_in_dim(came[-1], (seq % 2) * HALF, UPPER, 0)))
-    pieces = [plane] + came + [swap(piece) for piece in came]
-    parts, crowded = attend(index, span_len, q, wout, pieces)
+    far = round_z(lax.dynamic_slice_in_dim(came[-1], (seq % 2) * HALF, UPPER, 0))
+    near = attend_near(index, q, [plane] + came + [swap(piece) for piece in came])
+    far, (*state, info) = lax.optimization_barrier((far, near))
+    parts, crowded = attend_far(index, info, q, wout, far, swap(far), state)
     parts = lax.cond(
         crowded > 0, lambda _: attend_any(kv, q, span_len, wout, y), lambda given: given, parts
     )

time: 93.6 us -> 78.7 us (0.84)
  between operations: 14.2 us -> 0.96 us
  waiting for transfers between devices: 42.6 us -> 37.8 us
  Pallas kernels: 20.7 us -> 23.9 us
    ppermute x15, waiting for transfers between devices: 36.2 us -> 31.3 us  [seq_permute(): return lax.ppermute(value, 'seq', pairs)]
    pallas_call x1 -> x2, Pallas kernels: 5.47 us -> 8.12 us  [the longest x1 4.47 us: attend_near(): pl.pallas_call(attend_near_kernel, in_specs=[pl.BlockSpec(memory_space=pl...]
  transfers between devices with their start and end apart: 19 -> 19, of which waited for: 12 -> 13; matrix products, arithmetic and copies ran while one was open for 0% -> 0% of each run, Pallas kernels for 8% -> 15%
where the time goes in v1:
time: 78.7 us; the launch traced here: 77.6 us
  waiting for transfers between devices  37.8 us (48%)
  Pallas kernels  23.9 us (30%)
  starting transfers between devices  14.8 us (19%)
  between operations  0.96 us (1%)
    ppermute x15, waiting for transfers between devices, seq_permute(): return lax.ppermute(value, 'seq', pairs)  31.3 us
    ppermute x15, starting transfers between devices, seq_permute(): return lax.ppermute(value, 'seq', pairs)  7 us
    ppermute x3, starting transfers between devices, per_device(): lax.ppermute(parts[k], 'section', [(i, (i + k) % 4) for i in range(4)])  5.9 us
    pallas_call x1, Pallas kernels, pool(): pl.pallas_call(pool_kernel, in_specs=[anywhere()] * 5, out_specs=[vmem(),...  5.63 us
    pallas_call x1, Pallas kernels, attend_near(): pl.pallas_call(attend_near_kernel, in_specs=[pl.BlockSpec(memory_space=pl...  4.47 us
    pallas_call x1, Pallas kernels, query(): pl.pallas_call(query_kernel, in_specs=[anywhere(), vmem(), anywhere()], o...  3.96 us
    pallas_call x1, Pallas kernels, attend_far(): pl.pallas_call(attend_far_kernel, in_specs=[pl.BlockSpec(memory_space=plt...  3.65 us
    ppermute x3, waiting for transfers between devices, per_device(): lax.ppermute(parts[k], 'section', [(i, (i + k) % 4) for i in range(4)])  3.61 us
  transfers between devices with their start and end apart: 19, of which 13 were waited for; matrix products, arithmetic and copies ran while one was open for 0% of the time, Pallas kernels for 15%

profile of v1, /device:TPU:128, one launch (start us, length us, event | category | flops | bytes accessed | tf_op | source)
XLA Modules:
  0.0 77.6 jit_solution(12183359350937540534)
XLA Ops:
  0.0 5.6 %pool.1 = (bf16[208,256]{1,0:T(8,128)(2,1)S(1)}, bf16[192,4096]{1,0:T(8,128)(2,1)}, f32[192,128]{1,0:T(8,128)}) custom-call(s32[1,192]{1,0:T(1,128)} %len_ref.1, f32[1,4096]{1,0:T(1,128)} %bitcast.38, bf16[512,4096]{1,0:T(8,128)(2,1)} %enc_hbm.1, bf16[4096,128]{1,0:T(8,128)(2,1)} %wk_hbm.1, bf16[4096,128]{1,0:T(8,128)(2,1)} %wv_hbm.1), custom_call_target="tpu_custom_call" | custom-call | flops 1207959552 | bytes 7864320 | tf_op jit(solution)/shard_map/pool/pallas_call | solution.py:117
  5.6 1.6 %collective-permute-start.1 = (bf16[208,256]{1,0:T(8,128)(2,1)S(1)}, bf16[208,256]{1,0:T(8,128)(2,1)S(1)}, u32[]{:S(2)}, u32[]{:S(2)}) collective-permute-start(bf16[208,256]{1,0:T(8,128)(2,1)S(1)} %get-tuple-element.253.refs_0_), channel_id=1, source_target_pairs={{0,8},{4,12},{8,16},{12,20},{16,24},{20,28},{24,0},{28,4},{32,40},... | collective-permute-start | bytes 319496 | tf_op jit(solution)/shard_map/ppermute | solution.py:589
  7.2 1.8 %collective-permute-start.2 = (bf16[208,256]{1,0:T(8,128)(2,1)S(1)}, bf16[208,256]{1,0:T(8,128)(2,1)S(1)}, u32[]{:S(2)}, u32[]{:S(2)}) collective-permute-start(bf16[208,256]{1,0:T(8,128)(2,1)S(1)} %get-tuple-element.253.refs_0_), channel_id=1, source_target_pairs={{0,24},{4,28},{8,0},{12,4},{16,8},{20,12},{24,16},{28,20},{32,56},... | collective-permute-start | bytes 319496 | tf_op jit(solution)/shard_map/ppermute | solution.py:589
  8.9 1.8 %collective-permute-start.3 = (bf16[208,256]{1,0:T(8,128)(2,1)S(1)}, bf16[208,256]{1,0:T(8,128)(2,1)S(1)}, u32[]{:S(2)}, u32[]{:S(2)}) collective-permute-start(bf16[208,256]{1,0:T(8,128)(2,1)S(1)} %get-tuple-element.253.refs_0_), channel_id=1, source_target_pairs={{0,16},{4,20},{8,24},{12,28},{16,0},{20,4},{24,8},{28,12},{32,48},... | collective-permute-start | bytes 319496 | tf_op jit(solution)/shard_map/ppermute | solution.py:589
  10.8 0.9 %collective-permute-done.1.refs_1_ = bf16[208,256]{1,0:T(8,128)(2,1)S(1)} collective-permute-done((bf16[208,256]{1,0:T(8,128)(2,1)S(1)}, bf16[208,256]{1,0:T(8,128)(2,1)S(1)}, u32[]{:S(2)}, u32[]{:S(2)}) %collective-permute-start.1) | collective-permute-done | bytes 106528 | tf_op jit(solution)/shard_map/ppermute | solution.py:589
  11.6 1.9 %collective-permute-done.2.refs_2_ = bf16[208,256]{1,0:T(8,128)(2,1)S(1)} collective-permute-done((bf16[208,256]{1,0:T(8,128)(2,1)S(1)}, bf16[208,256]{1,0:T(8,128)(2,1)S(1)}, u32[]{:S(2)}, u32[]{:S(2)}) %collective-permute-start.2) | collective-permute-done | bytes 106528 | tf_op jit(solution)/shard_map/ppermute | solution.py:589
  13.5 1.7 %collective-permute-done.3.refs_3_ = bf16[208,256]{1,0:T(8,128)(2,1)S(1)} collective-permute-done((bf16[208,256]{1,0:T(8,128)(2,1)S(1)}, bf16[208,256]{1,0:T(8,128)(2,1)S(1)}, u32[]{:S(2)}, u32[]{:S(2)}) %collective-permute-start.3) | collective-permute-done | bytes 106528 | tf_op jit(solution)/shard_map/ppermute | solution.py:589
  15.2 0.1 pad_add_fusion.index_ref
  15.3 1.2 %collective-permute-done.7.refs_7_ = bf16[208,256]{1,0:T(8,128)(2,1)S(1)} collective-permute-done((bf16[208,256]{1,0:T(8,128)(2,1)S(1)}, bf16[208,256]{1,0:T(8,128)(2,1)S(1)}, u32[]{:S(2)}, u32[]{:S(2)}) %collective-permute-start.7) | collective-permute-done | bytes 106528 | tf_op jit(solution)/shard_map/ppermute | solution.py:589
  16.5 1.5 %compact.1.refs_0_ = bf16[784,256]{1,0:T(8,128)(2,1)S(1)} custom-call(s32[4]{0:T(128)S(1)} %pad_add_fusion.index_ref, bf16[208,256]{1,0:T(8,128)(2,1)S(1)} %get-tuple-element.253.refs_0_, bf16[208,256]{1,0:T(8,128)(2,1)S(1)} %collective-permute-done.1.refs_1_, bf16[208,256]{1,0:T(8,128)(2,1)S(1)} %collective-permute-done.2.refs_2_, ...), custom_call_target="tpu_custom_call" | custom-call | tf_op jit(solution)/shard_map/compact/pallas_call | solution.py:220
  18.0 1.1 %collective-permute-start.8 = (bf16[784,256]{1,0:T(8,128)(2,1)S(1)}, bf16[784,256]{1,0:T(8,128)(2,1)S(1)}, u32[]{:S(2)}, u32[]{:S(2)}) collective-permute-start(bf16[784,256]{1,0:T(8,128)(2,1)S(1)} %compact.1.refs_0_), channel_id=1, source_target_pairs={{0,32},{4,228},{8,40},{12,236},{16,48},{20,244},{24,56},{28,252},{... | collective-permute-start | bytes 1204232 | tf_op jit(solution)/shard_map/ppermute | solution.py:589
  19.1 4.0 %query.1.q_ref = bf16[192,512]{1,0:T(8,128)(2,1)S(1)} custom-call(bf16[192,4096]{1,0:T(8,128)(2,1)} %get-tuple-element.254.x_hbm, f32[192,128]{1,0:T(8,128)} %get-tuple-element.255.scale_ref, bf16[4096,512]{1,0:T(8,128)(2,1)} %wq_hbm.1), custom_call_target="tpu_custom_call" | custom-call | flops 805306368 | bytes 5767168 | tf_op jit(solution)/shard_map/query/pallas_call | solution.py:169
  23.1 4.1 %collective-permute-done.8.refs_1_ = bf16[784,256]{1,0:T(8,128)(2,1)S(1)} collective-permute-done((bf16[784,256]{1,0:T(8,128)(2,1)S(1)}, bf16[784,256]{1,0:T(8,128)(2,1)S(1)}, u32[]{:S(2)}, u32[]{:S(2)}) %collective-permute-start.8) | collective-permute-done | bytes 401440 | tf_op jit(solution)/shard_map/ppermute | solution.py:589
  27.2 9.1 %collective-permute-done.9.refs_2_ = bf16[784,256]{1,0:T(8,128)(2,1)S(1)} collective-permute-done((bf16[784,256]{1,0:T(8,128)(2,1)S(1)}, bf16[784,256]{1,0:T(8,128)(2,1)S(1)}, u32[]{:S(2)}, u32[]{:S(2)}) %collective-permute-start.9) | collective-permute-done | bytes 401440 | tf_op jit(solution)/shard_map/ppermute | solution.py:589
  36.2 0.5 collective-permute-start.13
  36.8 8.6 %collective-permute-done.10.refs_3_ = bf16[784,256]{1,0:T(8,128)(2,1)S(1)} collective-permute-done((bf16[784,256]{1,0:T(8,128)(2,1)S(1)}, bf16[784,256]{1,0:T(8,128)(2,1)S(1)}, u32[]{:S(2)}, u32[]{:S(2)}) %collective-permute-start.10) | collective-permute-done | bytes 401440 | tf_op jit(solution)/shard_map/ppermute | solution.py:589
  45.3 0.3 collective-permute-start.11
  45.6 1.4 %collective-permute-done.14.refs_6_ = bf16[784,256]{1,0:T(8,128)(2,1)S(1)} collective-permute-done((bf16[784,256]{1,0:T(8,128)(2,1)S(1)}, bf16[784,256]{1,0:T(8,128)(2,1)S(1)}, u32[]{:S(2)}, u32[]{:S(2)}) %collective-permute-start.14) | collective-permute-done | bytes 401440 | tf_op jit(solution)/shard_map/ppermute | solution.py:589
  47.1 4.5 %attend_near.1 = (f32[2,384,128]{2,1,0:T(8,128)S(1)}, f32[2,384,128]{2,1,0:T(8,128)S(1)}, f32[2,384,128]{2,1,0:T(8,128)S(1)}, s32[2]{0:T(128)S(1)}) custom-call(s32[4]{0:T(128)S(1)} %pad_add_fusion.index_ref, bf16[192,512]{1,0:T(8,128)(2,1)S(1)} %query.1.q_ref, bf16[784,256]{1,0:T(8,128)(2,1)S(1)} %compact.1.refs_0_, ...), custom_call_target="tpu_custom_call" | custom-call | flops 5435817984 | bytes 8388608 | tf_op jit(solution)/shard_map/attend_near/pallas_call | solution.py:362
  51.5 1.0 %collective-permute-done.11.came = bf16[400,256]{1,0:T(8,128)(2,1)S(1)} collective-permute-done((bf16[400,256]{1,0:T(8,128)(2,1)S(1)}, bf16[400,256]{1,0:T(8,128)(2,1)S(1)}, u32[]{:S(2)}, u32[]{:S(2)}) %collective-permute-start.11) | collective-permute-done | bytes 204832 | tf_op jit(solution)/shard_map/ppermute | solution.py:589
  52.6 1.5 %collective-permute-done.15.swapped = bf16[400,256]{1,0:T(8,128)(2,1)S(1)} collective-permute-done((bf16[400,256]{1,0:T(8,128)(2,1)S(1)}, bf16[400,256]{1,0:T(8,128)(2,1)S(1)}, u32[]{:S(2)}, u32[]{:S(2)}) %collective-permute-start.15) | collective-permute-done | bytes 204832 | tf_op jit(solution)/shard_map/ppermute | solution.py:589
  54.0 3.6 %attend_far.1 = (bf16[192,256]{1,0:T(8,128)(2,1)S(1)}, bf16[192,256]{1,0:T(8,128)(2,1)S(1)}, bf16[192,256]{1,0:T(8,128)(2,1)S(1)}, bf16[192,256]{1,0:T(8,128)(2,1)S(1)}, s32[1]{0:T(128)}) custom-call(s32[4]{0:T(128)S(1)} %pad_add_fusion.index_ref, s32[2]{0:T(128)S(1)} %get-tuple-element.262.info_ref, bf16[192,512]{1,0:T(8,128)(2,1)S(1)} %query.1.q_ref, ...), custom_call_target="tpu_custom_call" | custom-call | tf_op jit(solution)/shard_map/attend_far/pallas_call | solution.py:429
  58.4 1.7 %collective-permute-start.16 = (bf16[192,256]{1,0:T(8,128)(2,1)S(1)}, bf16[192,256]{1,0:T(8,128)(2,1)S(1)}, u32[]{:S(2)}, u32[]{:S(2)}) collective-permute-start(bf16[192,256]{1,0:T(8,128)(2,1)S(1)} %get-tuple-element.273), channel_id=1, source_target_pairs={{0,1},{1,2},{2,3},{3,0},{4,5},{5,6},{6,7},{7,4},{8,9},{9,10},{10,1... | collective-permute-start | bytes 294920 | tf_op jit(solution)/shard_map/ppermute | solution.py:623
  60.0 2.9 %collective-permute-start.17 = (bf16[192,256]{1,0:T(8,128)(2,1)S(1)}, bf16[192,256]{1,0:T(8,128)(2,1)S(1)}, u32[]{:S(2)}, u32[]{:S(2)}) collective-permute-start(bf16[192,256]{1,0:T(8,128)(2,1)S(1)} %get-tuple-element.274), channel_id=1, source_target_pairs={{0,2},{1,3},{2,0},{3,1},{4,6},{5,7},{6,4},{7,5},{8,10},{9,11},{10,... | collective-permute-start | bytes 294920 | tf_op jit(solution)/shard_map/ppermute | solution.py:623
  62.9 1.4 %collective-permute-start.18 = (bf16[192,256]{1,0:T(8,128)(2,1)S(1)}, bf16[192,256]{1,0:T(8,128)(2,1)S(1)}, u32[]{:S(2)}, u32[]{:S(2)}) collective-permute-start(bf16[192,256]{1,0:T(8,128)(2,1)S(1)} %get-tuple-element.275), channel_id=1, source_target_pairs={{0,3},{1,0},{2,1},{3,2},{4,7},{5,4},{6,5},{7,6},{8,11},{9,8},{10,9... | collective-permute-start | bytes 294920 | tf_op jit(solution)/shard_map/ppermute | solution.py:623
  64.3 0.3 collective-permute-done.16.p1
  64.6 3.3 %collective-permute-done.17.p2 = bf16[192,256]{1,0:T(8,128)(2,1)S(1)} collective-permute-done((bf16[192,256]{1,0:T(8,128)(2,1)S(1)}, bf16[192,256]{1,0:T(8,128)(2,1)S(1)}, u32[]{:S(2)}, u32[]{:S(2)}) %collective-permute-start.17) | collective-permute-done | bytes 98336 | tf_op jit(solution)/shard_map/ppermute | solution.py:623
  67.9 0.3 mix.1
  68.2 1.9 %collective-permute-start.19 = (bf16[32,256]{1,0:T(8,128)(2,1)S(1)}, bf16[32,256]{1,0:T(8,128)(2,1)S(1)}, u32[]{:S(2)}, u32[]{:S(2)}) collective-permute-start(bf16[32,256]{1,0:T(8,128)(2,1)S(1)} %get-tuple-element.277), channel_id=1, source_target_pairs={{0,4},{4,8},{8,12},{12,16},{16,20},{20,24},{24,28},{28,32},{32,36}... | collective-permute-start | bytes 49160 | tf_op jit(solution)/shard_map/ppermute | solution.py:626
  70.2 3.6 %convolve.1.given_hbm = bf16[512,256]{1,0:T(8,128)(2,1)} custom-call(bf16[512,256]{1,0:T(8,128)(2,1)S(1)} %get-tuple-element.276.mixed_ref, f32[31,256]{1,0:T(8,128)S(1)} %copy-done.1), custom_call_target="tpu_custom_call" | custom-call | flops 8126464 | bytes 2097152 | tf_op jit(solution)/shard_map/convolve/pallas_call | solution.py:554
  73.7 2.9 %collective-permute-done.19.rim_ref = bf16[32,256]{1,0:T(8,128)(2,1)S(1)} collective-permute-done((bf16[32,256]{1,0:T(8,128)(2,1)S(1)}, bf16[32,256]{1,0:T(8,128)(2,1)S(1)}, u32[]{:S(2)}, u32[]{:S(2)}) %collective-permute-start.19) | collective-permute-done | bytes 16416 | tf_op jit(solution)/shard_map/ppermute | solution.py:626
  76.6 0.8 %first_rows.1 = bf16[512,256]{1,0:T(8,128)(2,1)} custom-call(bf16[512,256]{1,0:T(8,128)(2,1)} %convolve.1.given_hbm, bf16[32,256]{1,0:T(8,128)(2,1)S(1)} %collective-permute-done.19.rim_ref, bf16[512,256]{1,0:T(8,128)(2,1)S(1)} %get-tuple-element.276.mixed_ref, f32[31,256]{1,0:T(8,128)S(1)} %copy-done.1), custom_call_target="tpu_custom_call", output_to_operand_aliasing={{}: (0, {})} | custom-call | tf_op jit(solution)/shard_map/first_rows/pallas_call | solution.py:569
  (23 shorter events, 0.1 us)
Async XLA Ops:
  5.6 6.0 %collective-permute-start.1 = (bf16[208,256]{1,0:T(8,128)(2,1)S(1)}, bf16[208,256]{1,0:T(8,128)(2,1)S(1)}, u32[]{:S(2)}, u32[]{:S(2)}) collective-permute-start(bf16[208,256]{1,0:T(8,128)(2,1)S(1)} %get-tuple-element.253.refs_0_), channel_id=1, source_target_pairs={{0,8},{4,12},{8,16},{12,20},{16,24},{20,28},{24,0},{28,4},{32,40},... | collective-permute-start | bytes 319496 | tf_op jit(solution)/shard_map/ppermute | solution.py:589
  7.2 6.3 %collective-permute-start.2 = (bf16[208,256]{1,0:T(8,128)(2,1)S(1)}, bf16[208,256]{1,0:T(8,128)(2,1)S(1)}, u32[]{:S(2)}, u32[]{:S(2)}) collective-permute-start(bf16[208,256]{1,0:T(8,128)(2,1)S(1)} %get-tuple-element.253.refs_0_), channel_id=1, source_target_pairs={{0,24},{4,28},{8,0},{12,4},{16,8},{20,12},{24,16},{28,20},{32,56},... | collective-permute-start | bytes 319496 | tf_op jit(solution)/shard_map/ppermute | solution.py:589
  8.9 6.2 %collective-permute-start.3 = (bf16[208,256]{1,0:T(8,128)(2,1)S(1)}, bf16[208,256]{1,0:T(8,128)(2,1)S(1)}, u32[]{:S(2)}, u32[]{:S(2)}) collective-permute-start(bf16[208,256]{1,0:T(8,128)(2,1)S(1)} %get-tuple-element.253.refs_0_), channel_id=1, source_target_pairs={{0,16},{4,20},{8,24},{12,28},{16,0},{20,4},{24,8},{28,12},{32,48},... | collective-permute-start | bytes 319496 | tf_op jit(solution)/shard_map/ppermute | solution.py:589
  10.8 4.5 %collective-permute-start.4 = (bf16[208,256]{1,0:T(8,128)(2,1)S(1)}, bf16[208,256]{1,0:T(8,128)(2,1)S(1)}, u32[]{:S(2)}, u32[]{:S(2)}) collective-permute-start(bf16[208,256]{1,0:T(8,128)(2,1)S(1)} %get-tuple-element.253.refs_0_), channel_id=1, source_target_pairs={{0,4},{4,0},{8,12},{12,8},{16,20},{20,16},{24,28},{28,24},{32,36},... | collective-permute-start | bytes 319496 | tf_op jit(solution)/shard_map/ppermute | solution.py:589
  11.6 3.6 %collective-permute-start.5 = (bf16[208,256]{1,0:T(8,128)(2,1)S(1)}, bf16[208,256]{1,0:T(8,128)(2,1)S(1)}, u32[]{:S(2)}, u32[]{:S(2)}) collective-permute-start(bf16[208,256]{1,0:T(8,128)(2,1)S(1)} %collective-permute-done.1.refs_1_), channel_id=1, source_target_pairs={{0,4},{4,0},{8,12},{12,8},{16,20},{20,16},{24,28},{28,24},{32,36},... | collective-permute-start | bytes 319496 | tf_op jit(solution)/shard_map/ppermute | solution.py:589
  13.5 1.8 %collective-permute-start.6 = (bf16[208,256]{1,0:T(8,128)(2,1)S(1)}, bf16[208,256]{1,0:T(8,128)(2,1)S(1)}, u32[]{:S(2)}, u32[]{:S(2)}) collective-permute-start(bf16[208,256]{1,0:T(8,128)(2,1)S(1)} %collective-permute-done.2.refs_2_), channel_id=1, source_target_pairs={{0,4},{4,0},{8,12},{12,8},{16,20},{20,16},{24,28},{28,24},{32,36},... | collective-permute-start | bytes 319496 | tf_op jit(solution)/shard_map/ppermute | solution.py:589
  15.2 1.3 %collective-permute-start.7 = (bf16[208,256]{1,0:T(8,128)(2,1)S(1)}, bf16[208,256]{1,0:T(8,128)(2,1)S(1)}, u32[]{:S(2)}, u32[]{:S(2)}) collective-permute-start(bf16[208,256]{1,0:T(8,128)(2,1)S(1)} %collective-permute-done.3.refs_3_), channel_id=1, source_target_pairs={{0,4},{4,0},{8,12},{12,8},{16,20},{20,16},{24,28},{28,24},{32,36},... | collective-permute-start | bytes 319496 | tf_op jit(solution)/shard_map/ppermute | solution.py:589
  18.0 9.2 %collective-permute-start.8 = (bf16[784,256]{1,0:T(8,128)(2,1)S(1)}, bf16[784,256]{1,0:T(8,128)(2,1)S(1)}, u32[]{:S(2)}, u32[]{:S(2)}) collective-permute-start(bf16[784,256]{1,0:T(8,128)(2,1)S(1)} %compact.1.refs_0_), channel_id=1, source_target_pairs={{0,32},{4,228},{8,40},{12,236},{16,48},{20,244},{24,56},{28,252},{... | collective-permute-start | bytes 1204232 | tf_op jit(solution)/shard_map/ppermute | solution.py:589
  27.2 9.1 %collective-permute-start.9 = (bf16[784,256]{1,0:T(8,128)(2,1)S(1)}, bf16[784,256]{1,0:T(8,128)(2,1)S(1)}, u32[]{:S(2)}, u32[]{:S(2)}) collective-permute-start(bf16[784,256]{1,0:T(8,128)(2,1)S(1)} %collective-permute-done.8.refs_1_), channel_id=1, source_target_pairs={{0,32},{4,228},{8,40},{12,236},{16,48},{20,244},{24,56},{28,252},{... | collective-permute-start | bytes 1204232 | tf_op jit(solution)/shard_map/ppermute | solution.py:589
  36.2 9.1 %collective-permute-start.10 = (bf16[784,256]{1,0:T(8,128)(2,1)S(1)}, bf16[784,256]{1,0:T(8,128)(2,1)S(1)}, u32[]{:S(2)}, u32[]{:S(2)}) collective-permute-start(bf16[784,256]{1,0:T(8,128)(2,1)S(1)} %collective-permute-done.9.refs_2_), channel_id=1, source_target_pairs={{0,32},{4,228},{8,40},{12,236},{16,48},{20,244},{24,56},{28,252},{... | collective-permute-start | bytes 1204232 | tf_op jit(solution)/shard_map/ppermute | solution.py:589
  36.2 9.4 %collective-permute-start.12 = (bf16[784,256]{1,0:T(8,128)(2,1)S(1)}, bf16[784,256]{1,0:T(8,128)(2,1)S(1)}, u32[]{:S(2)}, u32[]{:S(2)}) collective-permute-start(bf16[784,256]{1,0:T(8,128)(2,1)S(1)} %collective-permute-done.8.refs_1_), channel_id=1, source_target_pairs={{0,4},{4,0},{8,12},{12,8},{16,20},{20,16},{24,28},{28,24},{32,36},... | collective-permute-start | bytes 1204232 | tf_op jit(solution)/shard_map/ppermute | solution.py:589
  36.2 9.4 %collective-permute-start.13 = (bf16[784,256]{1,0:T(8,128)(2,1)S(1)}, bf16[784,256]{1,0:T(8,128)(2,1)S(1)}, u32[]{:S(2)}, u32[]{:S(2)}) collective-permute-start(bf16[784,256]{1,0:T(8,128)(2,1)S(1)} %collective-permute-done.9.refs_2_), channel_id=1, source_target_pairs={{0,4},{4,0},{8,12},{12,8},{16,20},{20,16},{24,28},{28,24},{32,36},... | collective-permute-start | bytes 1204232 | tf_op jit(solution)/shard_map/ppermute | solution.py:589
  45.3 1.7 %collective-permute-start.14 = (bf16[784,256]{1,0:T(8,128)(2,1)S(1)}, bf16[784,256]{1,0:T(8,128)(2,1)S(1)}, u32[]{:S(2)}, u32[]{:S(2)}) collective-permute-start(bf16[784,256]{1,0:T(8,128)(2,1)S(1)} %collective-permute-done.10.refs_3_), channel_id=1, source_target_pairs={{0,4},{4,0},{8,12},{12,8},{16,20},{20,16},{24,28},{28,24},{32,36},... | collective-permute-start | bytes 1204232 | tf_op jit(solution)/shard_map/ppermute | solution.py:589
  45.3 7.2 %collective-permute-start.11 = (bf16[400,256]{1,0:T(8,128)(2,1)S(1)}, bf16[400,256]{1,0:T(8,128)(2,1)S(1)}, u32[]{:S(2)}, u32[]{:S(2)}) collective-permute-start(bf16[400,256]{1,0:T(8,128)(2,1)S(1)} %constant_dynamic-slice_fusion.4), channel_id=1, source_target_pairs={{0,32},{4,228},{8,40},{12,236},{16,48},{20,244},{24,56},{28,252},{... | collective-permute-start | bytes 614408 | tf_op jit(solution)/shard_map/ppermute | solution.py:589
  52.6 1.5 %collective-permute-start.15 = (bf16[400,256]{1,0:T(8,128)(2,1)S(1)}, bf16[400,256]{1,0:T(8,128)(2,1)S(1)}, u32[]{:S(2)}, u32[]{:S(2)}) collective-permute-start(bf16[400,256]{1,0:T(8,128)(2,1)S(1)} %collective-permute-done.11.came), channel_id=1, source_target_pairs={{0,4},{4,0},{8,12},{12,8},{16,20},{20,16},{24,28},{28,24},{32,36},... | collective-permute-start | bytes 614408 | tf_op jit(solution)/shard_map/ppermute | solution.py:589
  58.3 9.6 %copy-start = (bf16[512,256]{1,0:T(8,128)(2,1)S(1)}, bf16[512,256]{1,0:T(8,128)(2,1)}, u32[]{:S(2)}) copy-start(bf16[512,256]{1,0:T(8,128)(2,1)} %skip_ref.1) | copy-start | bytes 786436
  58.3 9.6 %copy-start.2 = (s32[1,192]{1,0:T(1,128)S(1)}, s32[1,192]{1,0:T(1,128)}, u32[]{:S(2)}) copy-start(s32[1,192]{1,0:T(1,128)} %len_ref.1) | copy-start | bytes 2308
  58.3 11.8 %copy-start.1 = (f32[31,256]{1,0:T(8,128)S(1)}, f32[31,256]{1,0:T(8,128)}, u32[]{:S(2)}) copy-start(f32[31,256]{1,0:T(8,128)} %taps_ref.3) | copy-start | bytes 95236
  58.4 6.2 %collective-permute-start.16 = (bf16[192,256]{1,0:T(8,128)(2,1)S(1)}, bf16[192,256]{1,0:T(8,128)(2,1)S(1)}, u32[]{:S(2)}, u32[]{:S(2)}) collective-permute-start(bf16[192,256]{1,0:T(8,128)(2,1)S(1)} %get-tuple-element.273), channel_id=1, source_target_pairs={{0,1},{1,2},{2,3},{3,0},{4,5},{5,6},{6,7},{7,4},{8,9},{9,10},{10,1... | collective-permute-start | bytes 294920 | tf_op jit(solution)/shard_map/ppermute | solution.py:623
  60.0 7.9 %collective-permute-start.17 = (bf16[192,256]{1,0:T(8,128)(2,1)S(1)}, bf16[192,256]{1,0:T(8,128)(2,1)S(1)}, u32[]{:S(2)}, u32[]{:S(2)}) collective-permute-start(bf16[192,256]{1,0:T(8,128)(2,1)S(1)} %get-tuple-element.274), channel_id=1, source_target_pairs={{0,2},{1,3},{2,0},{3,1},{4,6},{5,7},{6,4},{7,5},{8,10},{9,11},{10,... | collective-permute-start | bytes 294920 | tf_op jit(solution)/shard_map/ppermute | solution.py:623
  62.9 5.0 %collective-permute-start.18 = (bf16[192,256]{1,0:T(8,128)(2,1)S(1)}, bf16[192,256]{1,0:T(8,128)(2,1)S(1)}, u32[]{:S(2)}, u32[]{:S(2)}) collective-permute-start(bf16[192,256]{1,0:T(8,128)(2,1)S(1)} %get-tuple-element.275), channel_id=1, source_target_pairs={{0,3},{1,0},{2,1},{3,2},{4,7},{5,4},{6,5},{7,6},{8,11},{9,8},{10,9... | collective-permute-start | bytes 294920 | tf_op jit(solution)/shard_map/ppermute | solution.py:623
  68.2 8.4 %collective-permute-start.19 = (bf16[32,256]{1,0:T(8,128)(2,1)S(1)}, bf16[32,256]{1,0:T(8,128)(2,1)S(1)}, u32[]{:S(2)}, u32[]{:S(2)}) collective-permute-start(bf16[32,256]{1,0:T(8,128)(2,1)S(1)} %get-tuple-element.277), channel_id=1, source_target_pairs={{0,4},{4,8},{8,12},{12,16},{16,20},{20,24},{24,28},{28,32},{32,36}... | collective-permute-start | bytes 49160 | tf_op jit(solution)/shard_map/ppermute | solution.py:626

commit v2 on v1

--- a/solution.py
+++ b/solution.py
@@ -13,15 +13,15 @@
 ROWS = CAP + TILE
 NX = 4
 NZ = 8
-HALF = 384
+HALF = 352
 UPPER = HALF + TILE
 PIECE = UPPER + HALF
 QT = 96
 KEYS = 512
 POOL_STEPS = 4
-DEPTH = 2
-FULL = 63
-QUERY_LIMIT = 62
+DEPTH = 4
+FULL = 62
+QUERY_LIMIT = 60
 HALO = 32
 LOG2E = math.log2(math.e)
 NEG = -1e30
@@ -46,7 +46,7 @@
     return lax.broadcasted_iota(jnp.int32, shape, dim)
 
 
-def pool_kernel(len_hbm, gain_hbm, enc_hbm, wk_hbm, wv_hbm, kv_ref, x_hbm, scale_ref, lengths, gain, enc, wkv, x, sems):
+def pool_kernel(len_hbm, gain_hbm, enc_hbm, wk_hbm, wv_hbm, kv_ref, x_ref, scale_ref, lengths, gain, enc, wkv, sems):
     byte_rows, width = enc.shape
     block = width // POOL_STEPS
     small = [
@@ -75,7 +75,6 @@
     hot = jnp.where(iota((CAP, byte_rows), 1).astype(F32) == start, 1.0, 0.0).astype(BF)
     total = jnp.zeros((CAP, 2 * HD), F32)
     squares = jnp.zeros((CAP, HD), F32)
-    leaving = []
     held = None
     for step in range(POOL_STEPS + 1):
         if step < POOL_STEPS:
@@ -94,22 +93,12 @@
                 piece = pooled[:, k * HD : (k + 1) * HD]
                 squares += piece * piece
             held = (pooled * gain[:, part]).astype(BF)
-            x[:, part] = held
-            leaving.append(
-                pltpu.make_async_copy(
-                    x.at[:, pl.ds(step * block, block)],
-                    x_hbm.at[:, pl.ds(step * block, block)],
-                    sems.at[2 + 3 * POOL_STEPS + step],
-                )
-            )
-            leaving[-1].start()
+            x_ref[:, part] = held
     scale = lax.rsqrt(jnp.sum(squares, axis=1, keepdims=True) / width + 1e-5)
     scale_ref[...] = jnp.broadcast_to(scale, scale_ref.shape)
     kv_ref[:CAP, :] = (total * scale).astype(BF)
     count = jnp.sum((lengths[...] > 0).astype(F32), axis=1, keepdims=True)
     kv_ref[CAP:, :] = jnp.broadcast_to(count, (TILE, 2 * HD)).astype(BF)
-    for copy in leaving:
-        copy.wait()
 
 
 def pool(lengths, enc, gain, wk, wv):
@@ -117,7 +106,7 @@
     return pl.pallas_call(
         pool_kernel,
         in_specs=[anywhere()] * 5,
-        out_specs=[vmem(), anywhere(), vmem()],
+        out_specs=[vmem()] * 3,
         out_shape=[
             jax.ShapeDtypeStruct((ROWS, 2 * HD), BF),
             jax.ShapeDtypeStruct((CAP, width), BF),
@@ -128,8 +117,7 @@
             pltpu.VMEM(gain.shape, F32),
             pltpu.VMEM((byte_rows, width), BF),
             pltpu.VMEM((width, 2 * HD), BF),
-            pltpu.VMEM((CAP, width), BF),
-            pltpu.SemaphoreType.DMA((4 * POOL_STEPS + 2,)),
+            pltpu.SemaphoreType.DMA((3 * POOL_STEPS + 2,)),
         ],
         compiler_params=params(FULL),
         cost_estimate=pl.CostEstimate(
@@ -141,26 +129,19 @@
     )(lengths, gain, enc, wk, wv)
 
 
-def query_kernel(x_hbm, scale_ref, wq_hbm, q_ref, x, wq, sems):
+def query_kernel(x_ref, scale_ref, wq_hbm, q_ref, wq, sems):
     width = wq.shape[0]
     block = width // POOL_STEPS
     copies = []
     for step in range(POOL_STEPS):
         part = pl.ds(step * block, block)
-        copies.append(
-            [
-                pltpu.make_async_copy(wq_hbm.at[part], wq.at[part], sems.at[2 * step]),
-                pltpu.make_async_copy(x_hbm.at[:, part], x.at[:, part], sems.at[2 * step + 1]),
-            ]
-        )
-        for copy in copies[-1]:
-            copy.start()
+        copies.append(pltpu.make_async_copy(wq_hbm.at[part], wq.at[part], sems.at[step]))
+        copies[-1].start()
     total = jnp.zeros(q_ref.shape, F32)
     for step in range(POOL_STEPS):
-        for copy in copies[step]:
-            copy.wait()
+        copies[step].wait()
         part = slice(step * block, (step + 1) * block)
-        total += jnp.dot(x[:, part], wq[part, :], preferred_element_type=F32)
+        total += jnp.dot(x_ref[:, part], wq[part, :], preferred_element_type=F32)
     q_ref[...] = (total * (scale_ref[:, :1] * (LOG2E * HD**-0.5))).astype(BF)
 
 
@@ -168,13 +149,12 @@
     width, out = wq.shape
     return pl.pallas_call(
         query_kernel,
-        in_specs=[anywhere(), vmem(), anywhere()],
+        in_specs=[vmem(), vmem(), anywhere()],
         out_specs=vmem(),
         out_shape=jax.ShapeDtypeStruct((CAP, out), BF),
         scratch_shapes=[
-            pltpu.VMEM((CAP, width), BF),
             pltpu.VMEM((width, out), BF),
-            pltpu.SemaphoreType.DMA((2 * POOL_STEPS,)),
+            pltpu.SemaphoreType.DMA((POOL_STEPS,)),
         ],
         compiler_params=params(QUERY_LIMIT),
         cost_estimate=pl.CostEstimate(
@@ -300,15 +280,15 @@
 
 
 def attend_near_kernel(index_ref, q_ref, *refs):
-    pieces, (top, lsum, acc, info_ref) = refs[:7], refs[7:11]
-    keys, values, scores = refs[11:]
+    pieces, (top, lsum, acc, info_ref) = refs[:5], refs[5:9]
+    keys, values, scores = refs[9:]
     z, x, core = index_ref[0], index_ref[1], index_ref[2]
     own = x * 2 + core
 
-    own_piece, came, swapped = pieces[0], pieces[1:4], pieces[4:7]
+    own_piece, came, swapped = pieces[0], pieces[1:3], pieces[3:5]
     upward, downward = (came, swapped), (swapped, came)
-    planes = [(8 - s, [downward[c][s - 1] for c in range(2)]) for s in (1, 2, 3)]
-    planes += [(s, [upward[c][s - 1] for c in range(2)]) for s in (3, 2, 1)]
+    planes = [(8 - s, [downward[c][s - 1] for c in range(2)]) for s in (1, 2)]
+    planes += [(s, [upward[c][s - 1] for c in range(2)]) for s in (2, 1)]
     planes.append((0, [own_piece, own_piece]))
 
     lives, most = [], jnp.int32(0)
@@ -357,7 +337,7 @@
 
 
 def attend_near(index, q, pieces):
-    most = 7 * 2 * HALF + KEYS
+    most = 5 * 2 * HALF + KEYS
     most = (most + KEYS - 1) // KEYS * KEYS
     return pl.pallas_call(
         attend_near_kernel,
@@ -378,6 +358,69 @@
     )(index, q, *pieces)
 
 
+def add_tile(tile, q_ref, given, mine, chunks, keys, values, scores):
+    slots = pl.ds(pl.multiple_of(tile * QT, QT), QT)
+    mine[0][...] = given[0][tile]
+    weigh = softmax_chunks(
+        heads_of(q_ref, slots), None, chunks, chunks, keys, values, scores, *mine
+    )
+    factor = jnp.exp2(given[0][tile] - mine[0][...])
+    mine[1][...] = given[1][tile] * factor
+    mine[2][...] = given[2][tile] * factor
+    lax.fori_loop(0, chunks, weigh, 0)
+
+
+def attend_more_kernel(index_ref, info_ref, q_ref, came, swapped, top, lsum, acc, *refs):
+    results, out_info, (keys, values, scores) = refs[:3], refs[3], refs[4:]
+    z, core = index_ref[0], index_ref[2]
+    first, most = jnp.int32(0), info_ref[0]
+    for back, where in ((5, (swapped, came)), (3, (came, swapped))):
+        live = single(jnp.where(core == 0, table_of(where[0]), table_of(where[1])))
+        most = jnp.maximum(most, live)
+        here = jnp.minimum(live, 2 * HALF)
+        for c in range(2):
+
+            @pl.when((z >= back) & (core == c))
+            def _(ref=where[c], here=here, first=first):
+                place(keys, values, ref, 0, 0, first, here)
+                place(keys, values, ref, UPPER, HALF, first, here)
+
+        first = first + jnp.where(z >= back, (here + TILE - 1) // TILE * TILE, 0)
+    fill(keys, values, first, KEYS, NEG)
+    chunks = (first + KEYS - 1) // KEYS
+    out_info[0] = most
+    out_info[1] = info_ref[1]
+
+    def per_tile(tile, _):
+        mine = [ref.at[tile] for ref in results]
+        add_tile(tile, q_ref, (top, lsum, acc), mine, chunks, keys, values, scores)
+        return 0
+
+    lax.fori_loop(0, (info_ref[1] + QT - 1) // QT, per_tile, 0)
+
+
+def attend_more(index, q, came, swapped, state, info):
+    most = 2 * 2 * HALF + KEYS
+    most = (most + KEYS - 1) // KEYS * KEYS
+    return pl.pallas_call(
+        attend_more_kernel,
+        in_specs=[pl.BlockSpec(memory_space=pltpu.SMEM)] * 2 + [vmem()] * 6,
+        out_specs=[vmem()] * 3 + [pl.BlockSpec(memory_space=pltpu.SMEM)],
+        out_shape=[jax.ShapeDtypeStruct(value.shape, F32) for value in state]
+        + [jax.ShapeDtypeStruct((2,), jnp.int32)],
+        scratch_shapes=[
+            pltpu.VMEM((most, 2 * HD), BF),
+            pltpu.VMEM((most, HD), BF),
+            pltpu.VMEM((most // KEYS, 4 * QT, KEYS), F32),
+        ],
+        compiler_params=params(),
+        cost_estimate=pl.CostEstimate(
+            flops=12 * QT * most * 3 * HD * 2, bytes_accessed=1 << 23, transcendentals=8 * QT * most
+        ),
+        name="attend_more",
+    )(index, info, q, came, swapped, *state)
+
+
 def attend_far_kernel(index_ref, info_ref, q_ref, wout_ref, came, swapped, top, lsum, acc, *refs):
     outs, flag_ref = refs[:4], refs[4]
     keys, values, scores, peak, total, sums = refs[5:]
@@ -400,14 +443,9 @@
 
     def per_tile(tile, _):
         slots = pl.ds(pl.multiple_of(tile * QT, QT), QT)
-        peak[...] = top[tile]
-        weigh = softmax_chunks(
-            heads_of(q_ref, slots), None, chunks, chunks, keys, values, scores, peak, total, sums
+        add_tile(
+            tile, q_ref, (top, lsum, acc), (peak, total, sums), chunks, keys, values, scores
         )
-        factor = jnp.exp2(top[tile] - peak[...])
-        total[...] = lsum[tile] * factor
-        sums[...] = acc[tile] * factor
-        lax.fori_loop(0, chunks, weigh, 0)
         a = (sums[...] / jnp.sum(total[...], axis=1, keepdims=True)).astype(BF)
         a = jnp.concatenate([a[h * QT : (h + 1) * QT, :] for h in range(4)], axis=1)
         for k in range(4):
@@ -610,11 +648,12 @@
     plane = compact(index, column + [swap(v) for v in column])
     first, q = lax.optimization_barrier((round_z(plane), query(x, wq, scale)))
     came = [first]
-    came.append(round_z(came[-1]))
-    came.append(round_z(came[-1]))
-    far = round_z(lax.dynamic_slice_in_dim(came[-1], (seq % 2) * HALF, UPPER, 0))
+    came.append(round_z(first))
     near = attend_near(index, q, [plane] + came + [swap(piece) for piece in came])
-    far, (*state, info) = lax.optimization_barrier((far, near))
+    third, (*state, info) = lax.optimization_barrier((round_z(came[-1]), near))
+    far = round_z(lax.dynamic_slice_in_dim(third, (seq % 2) * HALF, UPPER, 0))
+    more = attend_more(index, q, third, swap(third), state, info)
+    far, (*state, info) = lax.optimization_barrier((far, more))
     parts, crowded = attend_far(index, info, q, wout, far, swap(far), state)
     parts = lax.cond(
         crowded > 0, lambda _: attend_any(kv, q, span_len, wout, y), lambda given: given, parts

time: 78.7 us -> 75.2 us (0.956)
  waiting for transfers between devices: 37.8 us -> 35.1 us
    ppermute x15, waiting for transfers between devices: 31.3 us -> 28.6 us  [seq_permute(): return lax.ppermute(value, 'seq', pairs)]
    pallas_call x2 -> x3, Pallas kernels: 9.59 us -> 11.1 us  [the longest x1 4.71 us: pool(): pl.pallas_call(pool_kernel, in_specs=[anywhere()] * 5, out_specs=[vmem()]...]
    pallas_call x1, Pallas kernels: 3.65 us -> 2.38 us  [attend_far(): pl.pallas_call(attend_far_kernel, in_specs=[pl.BlockSpec(memory_space=plt...]
  transfers between devices with their start and end apart: 19 -> 19, of which waited for: 13 -> 14; matrix products, arithmetic and copies ran while one was open for 0% -> 0% of each run, Pallas kernels for 15% -> 19%
where the time goes in v2:
time: 75.2 us; the launch traced here: 73.9 us
  waiting for transfers between devices  35.1 us (47%)
  Pallas kernels  23.6 us (31%)
  starting transfers between devices  14.2 us (19%)
  between operations  0.97 us (1%)
    ppermute x15, waiting for transfers between devices, seq_permute(): return lax.ppermute(value, 'seq', pairs)  28.6 us
    ppermute x15, starting transfers between devices, seq_permute(): return lax.ppermute(value, 'seq', pairs)  6.33 us
    ppermute x3, starting transfers between devices, per_device(): lax.ppermute(parts[k], 'section', [(i, (i + k) % 4) for i in range(4)])  5.9 us
    pallas_call x1, Pallas kernels, pool(): pl.pallas_call(pool_kernel, in_specs=[anywhere()] * 5, out_specs=[vmem()]...  4.71 us
    pallas_call x1, Pallas kernels, query(): pl.pallas_call(query_kernel, in_specs=[vmem(), vmem(), anywhere()], out_s...  4.11 us
    pallas_call x1, Pallas kernels, attend_near(): pl.pallas_call(attend_near_kernel, in_specs=[pl.BlockSpec(memory_space=pl...  3.9 us
    ppermute x3, waiting for transfers between devices, per_device(): lax.ppermute(parts[k], 'section', [(i, (i + k) % 4) for i in range(4)])  3.61 us
    pallas_call x1, Pallas kernels, convolve(): pl.pallas_call(conv_kernel, in_specs=[vmem()] * 2, out_specs=vmem(), out_...  3.56 us
  transfers between devices with their start and end apart: 19, of which 14 were waited for; matrix products, arithmetic and copies ran while one was open for 0% of the time, Pallas kernels for 19%

profile of v2, /device:TPU:128, one launch (start us, length us, event | category | flops | bytes accessed | tf_op | source)
XLA Modules:
  0.0 73.9 jit_solution(3164540165562410630)
XLA Ops:
  0.0 4.7 %pool.1 = (bf16[208,256]{1,0:T(8,128)(2,1)S(1)}, bf16[192,4096]{1,0:T(8,128)(2,1)}, f32[192,128]{1,0:T(8,128)}) custom-call(s32[1,192]{1,0:T(1,128)} %len_ref.1, f32[1,4096]{1,0:T(1,128)} %bitcast.38, bf16[512,4096]{1,0:T(8,128)(2,1)} %enc_hbm.1, bf16[4096,128]{1,0:T(8,128)(2,1)} %wk_hbm.1, bf16[4096,128]{1,0:T(8,128)(2,1)} %wv_hbm.1), custom_call_target="tpu_custom_call" | custom-call | flops 1207959552 | bytes 7864320 | tf_op jit(solution)/shard_map/pool/pallas_call | solution.py:106
  4.7 1.6 %collective-permute-start.1 = (bf16[208,256]{1,0:T(8,128)(2,1)S(1)}, bf16[208,256]{1,0:T(8,128)(2,1)S(1)}, u32[]{:S(2)}, u32[]{:S(2)}) collective-permute-start(bf16[208,256]{1,0:T(8,128)(2,1)S(1)} %get-tuple-element.262.refs_0_), channel_id=1, source_target_pairs={{0,8},{4,12},{8,16},{12,20},{16,24},{20,28},{24,0},{28,4},{32,40},... | collective-permute-start | bytes 319496 | tf_op jit(solution)/shard_map/ppermute | solution.py:627
  6.3 1.7 %collective-permute-start.2 = (bf16[208,256]{1,0:T(8,128)(2,1)S(1)}, bf16[208,256]{1,0:T(8,128)(2,1)S(1)}, u32[]{:S(2)}, u32[]{:S(2)}) collective-permute-start(bf16[208,256]{1,0:T(8,128)(2,1)S(1)} %get-tuple-element.262.refs_0_), channel_id=1, source_target_pairs={{0,24},{4,28},{8,0},{12,4},{16,8},{20,12},{24,16},{28,20},{32,56},... | collective-permute-start | bytes 319496 | tf_op jit(solution)/shard_map/ppermute | solution.py:627
  8.0 1.8 %collective-permute-start.3 = (bf16[208,256]{1,0:T(8,128)(2,1)S(1)}, bf16[208,256]{1,0:T(8,128)(2,1)S(1)}, u32[]{:S(2)}, u32[]{:S(2)}) collective-permute-start(bf16[208,256]{1,0:T(8,128)(2,1)S(1)} %get-tuple-element.262.refs_0_), channel_id=1, source_target_pairs={{0,16},{4,20},{8,24},{12,28},{16,0},{20,4},{24,8},{28,12},{32,48},... | collective-permute-start | bytes 319496 | tf_op jit(solution)/shard_map/ppermute | solution.py:627
  9.8 0.9 %collective-permute-done.1.refs_1_ = bf16[208,256]{1,0:T(8,128)(2,1)S(1)} collective-permute-done((bf16[208,256]{1,0:T(8,128)(2,1)S(1)}, bf16[208,256]{1,0:T(8,128)(2,1)S(1)}, u32[]{:S(2)}, u32[]{:S(2)}) %collective-permute-start.1) | collective-permute-done | bytes 106528 | tf_op jit(solution)/shard_map/ppermute | solution.py:627
  10.7 1.9 %collective-permute-done.2.refs_2_ = bf16[208,256]{1,0:T(8,128)(2,1)S(1)} collective-permute-done((bf16[208,256]{1,0:T(8,128)(2,1)S(1)}, bf16[208,256]{1,0:T(8,128)(2,1)S(1)}, u32[]{:S(2)}, u32[]{:S(2)}) %collective-permute-start.2) | collective-permute-done | bytes 106528 | tf_op jit(solution)/shard_map/ppermute | solution.py:627
  12.6 1.7 %collective-permute-done.3.refs_3_ = bf16[208,256]{1,0:T(8,128)(2,1)S(1)} collective-permute-done((bf16[208,256]{1,0:T(8,128)(2,1)S(1)}, bf16[208,256]{1,0:T(8,128)(2,1)S(1)}, u32[]{:S(2)}, u32[]{:S(2)}) %collective-permute-start.3) | collective-permute-done | bytes 106528 | tf_op jit(solution)/shard_map/ppermute | solution.py:627
  14.3 1.2 %collective-permute-done.7.refs_7_ = bf16[208,256]{1,0:T(8,128)(2,1)S(1)} collective-permute-done((bf16[208,256]{1,0:T(8,128)(2,1)S(1)}, bf16[208,256]{1,0:T(8,128)(2,1)S(1)}, u32[]{:S(2)}, u32[]{:S(2)}) %collective-permute-start.7) | collective-permute-done | bytes 106528 | tf_op jit(solution)/shard_map/ppermute | solution.py:627
  15.6 1.5 %compact.1.refs_0_ = bf16[720,256]{1,0:T(8,128)(2,1)S(1)} custom-call(s32[4]{0:T(128)S(1)} %pad_add_fusion.index_ref, bf16[208,256]{1,0:T(8,128)(2,1)S(1)} %get-tuple-element.262.refs_0_, bf16[208,256]{1,0:T(8,128)(2,1)S(1)} %collective-permute-done.1.refs_1_, bf16[208,256]{1,0:T(8,128)(2,1)S(1)} %collective-permute-done.2.refs_2_, ...), custom_call_target="tpu_custom_call" | custom-call | tf_op jit(solution)/shard_map/compact/pallas_call | solution.py:200
  17.0 1.1 %collective-permute-start.8 = (bf16[720,256]{1,0:T(8,128)(2,1)S(1)}, bf16[720,256]{1,0:T(8,128)(2,1)S(1)}, u32[]{:S(2)}, u32[]{:S(2)}) collective-permute-start(bf16[720,256]{1,0:T(8,128)(2,1)S(1)} %compact.1.refs_0_), channel_id=1, source_target_pairs={{0,32},{4,228},{8,40},{12,236},{16,48},{20,244},{24,56},{28,252},{... | collective-permute-start | bytes 1105928 | tf_op jit(solution)/shard_map/ppermute | solution.py:627
  18.1 4.1 %query.1.q_ref = bf16[192,512]{1,0:T(8,128)(2,1)S(1)} custom-call(bf16[192,4096]{1,0:T(8,128)(2,1)} %get-tuple-element.263.x_ref, f32[192,128]{1,0:T(8,128)} %get-tuple-element.264.scale_ref, bf16[4096,512]{1,0:T(8,128)(2,1)} %wq_hbm.1), custom_call_target="tpu_custom_call" | custom-call | flops 805306368 | bytes 5767168 | tf_op jit(solution)/shard_map/query/pallas_call | solution.py:150
  22.3 3.6 %collective-permute-done.8.refs_1_ = bf16[720,256]{1,0:T(8,128)(2,1)S(1)} collective-permute-done((bf16[720,256]{1,0:T(8,128)(2,1)S(1)}, bf16[720,256]{1,0:T(8,128)(2,1)S(1)}, u32[]{:S(2)}, u32[]{:S(2)}) %collective-permute-start.8) | collective-permute-done | bytes 368672 | tf_op jit(solution)/shard_map/ppermute | solution.py:627
  25.8 8.7 %collective-permute-done.9.refs_2_ = bf16[720,256]{1,0:T(8,128)(2,1)S(1)} collective-permute-done((bf16[720,256]{1,0:T(8,128)(2,1)S(1)}, bf16[720,256]{1,0:T(8,128)(2,1)S(1)}, u32[]{:S(2)}, u32[]{:S(2)}) %collective-permute-start.9) | collective-permute-done | bytes 368672 | tf_op jit(solution)/shard_map/ppermute | solution.py:627
  34.6 1.7 %collective-permute-done.12.refs_4_ = bf16[720,256]{1,0:T(8,128)(2,1)S(1)} collective-permute-done((bf16[720,256]{1,0:T(8,128)(2,1)S(1)}, bf16[720,256]{1,0:T(8,128)(2,1)S(1)}, u32[]{:S(2)}, u32[]{:S(2)}) %collective-permute-start.12) | collective-permute-done | bytes 368672 | tf_op jit(solution)/shard_map/ppermute | solution.py:627
  36.3 3.9 %attend_near.1 = (f32[2,384,128]{2,1,0:T(8,128)S(1)}, f32[2,384,128]{2,1,0:T(8,128)S(1)}, f32[2,384,128]{2,1,0:T(8,128)S(1)}, s32[2]{0:T(128)S(1)}) custom-call(s32[4]{0:T(128)S(1)} %pad_add_fusion.index_ref, bf16[192,512]{1,0:T(8,128)(2,1)S(1)} %query.1.q_ref, bf16[720,256]{1,0:T(8,128)(2,1)S(1)} %compact.1.refs_0_, ...), custom_call_target="tpu_custom_call" | custom-call | flops 3623878656 | bytes 8388608 | tf_op jit(solution)/shard_map/attend_near/pallas_call | solution.py:342
  40.2 3.1 %collective-permute-done.10.came = bf16[720,256]{1,0:T(8,128)(2,1)S(1)} collective-permute-done((bf16[720,256]{1,0:T(8,128)(2,1)S(1)}, bf16[720,256]{1,0:T(8,128)(2,1)S(1)}, u32[]{:S(2)}, u32[]{:S(2)}) %collective-permute-start.10) | collective-permute-done | bytes 368672 | tf_op jit(solution)/shard_map/ppermute | solution.py:627
  43.3 0.1 collective-permute-start.13
  43.4 1.6 %collective-permute-done.14.swapped = bf16[720,256]{1,0:T(8,128)(2,1)S(1)} collective-permute-done((bf16[720,256]{1,0:T(8,128)(2,1)S(1)}, bf16[720,256]{1,0:T(8,128)(2,1)S(1)}, u32[]{:S(2)}, u32[]{:S(2)}) %collective-permute-start.14) | collective-permute-done | bytes 368672 | tf_op jit(solution)/shard_map/ppermute | solution.py:627
  45.0 2.3 %attend_more.1 = (f32[2,384,128]{2,1,0:T(8,128)S(1)}, f32[2,384,128]{2,1,0:T(8,128)S(1)}, f32[2,384,128]{2,1,0:T(8,128)S(1)}, s32[2]{0:T(128)S(1)}) custom-call(s32[4]{0:T(128)S(1)} %pad_add_fusion.index_ref, s32[2]{0:T(128)S(1)} %get-tuple-element.272.info_ref, bf16[192,512]{1,0:T(8,128)(2,1)S(1)} %query.1.q_ref, ...), custom_call_target="tpu_custom_call" | custom-call | flops 1811939328 | bytes 8388608 | tf_op jit(solution)/shard_map/attend_more/pallas_call | solution.py:405
  47.3 2.9 %collective-permute-done.13.came = bf16[368,256]{1,0:T(8,128)(2,1)S(1)} collective-permute-done((bf16[368,256]{1,0:T(8,128)(2,1)S(1)}, bf16[368,256]{1,0:T(8,128)(2,1)S(1)}, u32[]{:S(2)}, u32[]{:S(2)}) %collective-permute-start.13) | collective-permute-done | bytes 188448 | tf_op jit(solution)/shard_map/ppermute | solution.py:627
  50.2 1.4 %collective-permute-done.15.swapped = bf16[368,256]{1,0:T(8,128)(2,1)S(1)} collective-permute-done((bf16[368,256]{1,0:T(8,128)(2,1)S(1)}, bf16[368,256]{1,0:T(8,128)(2,1)S(1)}, u32[]{:S(2)}, u32[]{:S(2)}) %collective-permute-start.15) | collective-permute-done | bytes 188448 | tf_op jit(solution)/shard_map/ppermute | solution.py:627
  51.6 2.4 %attend_far.1 = (bf16[192,256]{1,0:T(8,128)(2,1)S(1)}, bf16[192,256]{1,0:T(8,128)(2,1)S(1)}, bf16[192,256]{1,0:T(8,128)(2,1)S(1)}, bf16[192,256]{1,0:T(8,128)(2,1)S(1)}, s32[1]{0:T(128)}) custom-call(s32[4]{0:T(128)S(1)} %pad_add_fusion.index_ref, s32[2]{0:T(128)S(1)} %get-tuple-element.280.info_ref, bf16[192,512]{1,0:T(8,128)(2,1)S(1)} %query.1.q_ref, ...), custom_call_target="tpu_custom_call" | custom-call | tf_op jit(solution)/shard_map/attend_far/pallas_call | solution.py:467
  54.7 1.6 %collective-permute-start.16 = (bf16[192,256]{1,0:T(8,128)(2,1)S(1)}, bf16[192,256]{1,0:T(8,128)(2,1)S(1)}, u32[]{:S(2)}, u32[]{:S(2)}) collective-permute-start(bf16[192,256]{1,0:T(8,128)(2,1)S(1)} %get-tuple-element.291), channel_id=1, source_target_pairs={{0,1},{1,2},{2,3},{3,0},{4,5},{5,6},{6,7},{7,4},{8,9},{9,10},{10,1... | collective-permute-start | bytes 294920 | tf_op jit(solution)/shard_map/ppermute | solution.py:662
  56.4 2.9 %collective-permute-start.17 = (bf16[192,256]{1,0:T(8,128)(2,1)S(1)}, bf16[192,256]{1,0:T(8,128)(2,1)S(1)}, u32[]{:S(2)}, u32[]{:S(2)}) collective-permute-start(bf16[192,256]{1,0:T(8,128)(2,1)S(1)} %get-tuple-element.292), channel_id=1, source_target_pairs={{0,2},{1,3},{2,0},{3,1},{4,6},{5,7},{6,4},{7,5},{8,10},{9,11},{10,... | collective-permute-start | bytes 294920 | tf_op jit(solution)/shard_map/ppermute | solution.py:662
  59.3 1.3 %collective-permute-start.18 = (bf16[192,256]{1,0:T(8,128)(2,1)S(1)}, bf16[192,256]{1,0:T(8,128)(2,1)S(1)}, u32[]{:S(2)}, u32[]{:S(2)}) collective-permute-start(bf16[192,256]{1,0:T(8,128)(2,1)S(1)} %get-tuple-element.293), channel_id=1, source_target_pairs={{0,3},{1,0},{2,1},{3,2},{4,7},{5,4},{6,5},{7,6},{8,11},{9,8},{10,9... | collective-permute-start | bytes 294920 | tf_op jit(solution)/shard_map/ppermute | solution.py:662
  60.6 0.3 collective-permute-done.16.p1
  60.9 3.3 %collective-permute-done.17.p2 = bf16[192,256]{1,0:T(8,128)(2,1)S(1)} collective-permute-done((bf16[192,256]{1,0:T(8,128)(2,1)S(1)}, bf16[192,256]{1,0:T(8,128)(2,1)S(1)}, u32[]{:S(2)}, u32[]{:S(2)}) %collective-permute-start.17) | collective-permute-done | bytes 98336 | tf_op jit(solution)/shard_map/ppermute | solution.py:662
  64.2 0.3 mix.1
  64.6 1.9 %collective-permute-start.19 = (bf16[32,256]{1,0:T(8,128)(2,1)S(1)}, bf16[32,256]{1,0:T(8,128)(2,1)S(1)}, u32[]{:S(2)}, u32[]{:S(2)}) collective-permute-start(bf16[32,256]{1,0:T(8,128)(2,1)S(1)} %get-tuple-element.295), channel_id=1, source_target_pairs={{0,4},{4,8},{8,12},{12,16},{16,20},{20,24},{24,28},{28,32},{32,36}... | collective-permute-start | bytes 49160 | tf_op jit(solution)/shard_map/ppermute | solution.py:665
  66.5 3.6 %convolve.1.given_hbm = bf16[512,256]{1,0:T(8,128)(2,1)} custom-call(bf16[512,256]{1,0:T(8,128)(2,1)S(1)} %get-tuple-element.294.mixed_ref, f32[31,256]{1,0:T(8,128)S(1)} %copy-done.1), custom_call_target="tpu_custom_call" | custom-call | flops 8126464 | bytes 2097152 | tf_op jit(solution)/shard_map/convolve/pallas_call | solution.py:592
  70.1 2.9 %collective-permute-done.19.rim_ref = bf16[32,256]{1,0:T(8,128)(2,1)S(1)} collective-permute-done((bf16[32,256]{1,0:T(8,128)(2,1)S(1)}, bf16[32,256]{1,0:T(8,128)(2,1)S(1)}, u32[]{:S(2)}, u32[]{:S(2)}) %collective-permute-start.19) | collective-permute-done | bytes 16416 | tf_op jit(solution)/shard_map/ppermute | solution.py:665
  72.9 0.8 %first_rows.1 = bf16[512,256]{1,0:T(8,128)(2,1)} custom-call(bf16[512,256]{1,0:T(8,128)(2,1)} %convolve.1.given_hbm, bf16[32,256]{1,0:T(8,128)(2,1)S(1)} %collective-permute-done.19.rim_ref, bf16[512,256]{1,0:T(8,128)(2,1)S(1)} %get-tuple-element.294.mixed_ref, f32[31,256]{1,0:T(8,128)S(1)} %copy-done.1), custom_call_target="tpu_custom_call", output_to_operand_aliasing={{}: (0, {})} | custom-call | tf_op jit(solution)/shard_map/first_rows/pallas_call | solution.py:607
  (26 shorter events, 0.2 us)
Async XLA Ops:
  4.7 6.0 %collective-permute-start.1 = (bf16[208,256]{1,0:T(8,128)(2,1)S(1)}, bf16[208,256]{1,0:T(8,128)(2,1)S(1)}, u32[]{:S(2)}, u32[]{:S(2)}) collective-permute-start(bf16[208,256]{1,0:T(8,128)(2,1)S(1)} %get-tuple-element.262.refs_0_), channel_id=1, source_target_pairs={{0,8},{4,12},{8,16},{12,20},{16,24},{20,28},{24,0},{28,4},{32,40},... | collective-permute-start | bytes 319496 | tf_op jit(solution)/shard_map/ppermute | solution.py:627
  6.3 6.3 %collective-permute-start.2 = (bf16[208,256]{1,0:T(8,128)(2,1)S(1)}, bf16[208,256]{1,0:T(8,128)(2,1)S(1)}, u32[]{:S(2)}, u32[]{:S(2)}) collective-permute-start(bf16[208,256]{1,0:T(8,128)(2,1)S(1)} %get-tuple-element.262.refs_0_), channel_id=1, source_target_pairs={{0,24},{4,28},{8,0},{12,4},{16,8},{20,12},{24,16},{28,20},{32,56},... | collective-permute-start | bytes 319496 | tf_op jit(solution)/shard_map/ppermute | solution.py:627
  8.0 6.2 %collective-permute-start.3 = (bf16[208,256]{1,0:T(8,128)(2,1)S(1)}, bf16[208,256]{1,0:T(8,128)(2,1)S(1)}, u32[]{:S(2)}, u32[]{:S(2)}) collective-permute-start(bf16[208,256]{1,0:T(8,128)(2,1)S(1)} %get-tuple-element.262.refs_0_), channel_id=1, source_target_pairs={{0,16},{4,20},{8,24},{12,28},{16,0},{20,4},{24,8},{28,12},{32,48},... | collective-permute-start | bytes 319496 | tf_op jit(solution)/shard_map/ppermute | solution.py:627
  9.8 4.5 %collective-permute-start.4 = (bf16[208,256]{1,0:T(8,128)(2,1)S(1)}, bf16[208,256]{1,0:T(8,128)(2,1)S(1)}, u32[]{:S(2)}, u32[]{:S(2)}) collective-permute-start(bf16[208,256]{1,0:T(8,128)(2,1)S(1)} %get-tuple-element.262.refs_0_), channel_id=1, source_target_pairs={{0,4},{4,0},{8,12},{12,8},{16,20},{20,16},{24,28},{28,24},{32,36},... | collective-permute-start | bytes 319496 | tf_op jit(solution)/shard_map/ppermute | solution.py:627
  10.7 3.6 %collective-permute-start.5 = (bf16[208,256]{1,0:T(8,128)(2,1)S(1)}, bf16[208,256]{1,0:T(8,128)(2,1)S(1)}, u32[]{:S(2)}, u32[]{:S(2)}) collective-permute-start(bf16[208,256]{1,0:T(8,128)(2,1)S(1)} %collective-permute-done.1.refs_1_), channel_id=1, source_target_pairs={{0,4},{4,0},{8,12},{12,8},{16,20},{20,16},{24,28},{28,24},{32,36},... | collective-permute-start | bytes 319496 | tf_op jit(solution)/shard_map/ppermute | solution.py:627
  12.6 1.8 %collective-permute-start.6 = (bf16[208,256]{1,0:T(8,128)(2,1)S(1)}, bf16[208,256]{1,0:T(8,128)(2,1)S(1)}, u32[]{:S(2)}, u32[]{:S(2)}) collective-permute-start(bf16[208,256]{1,0:T(8,128)(2,1)S(1)} %collective-permute-done.2.refs_2_), channel_id=1, source_target_pairs={{0,4},{4,0},{8,12},{12,8},{16,20},{20,16},{24,28},{28,24},{32,36},... | collective-permute-start | bytes 319496 | tf_op jit(solution)/shard_map/ppermute | solution.py:627
  14.2 1.3 %collective-permute-start.7 = (bf16[208,256]{1,0:T(8,128)(2,1)S(1)}, bf16[208,256]{1,0:T(8,128)(2,1)S(1)}, u32[]{:S(2)}, u32[]{:S(2)}) collective-permute-start(bf16[208,256]{1,0:T(8,128)(2,1)S(1)} %collective-permute-done.3.refs_3_), channel_id=1, source_target_pairs={{0,4},{4,0},{8,12},{12,8},{16,20},{20,16},{24,28},{28,24},{32,36},... | collective-permute-start | bytes 319496 | tf_op jit(solution)/shard_map/ppermute | solution.py:627
  17.0 8.8 %collective-permute-start.8 = (bf16[720,256]{1,0:T(8,128)(2,1)S(1)}, bf16[720,256]{1,0:T(8,128)(2,1)S(1)}, u32[]{:S(2)}, u32[]{:S(2)}) collective-permute-start(bf16[720,256]{1,0:T(8,128)(2,1)S(1)} %compact.1.refs_0_), channel_id=1, source_target_pairs={{0,32},{4,228},{8,40},{12,236},{16,48},{20,244},{24,56},{28,252},{... | collective-permute-start | bytes 1105928 | tf_op jit(solution)/shard_map/ppermute | solution.py:627
  25.8 8.7 %collective-permute-start.9 = (bf16[720,256]{1,0:T(8,128)(2,1)S(1)}, bf16[720,256]{1,0:T(8,128)(2,1)S(1)}, u32[]{:S(2)}, u32[]{:S(2)}) collective-permute-start(bf16[720,256]{1,0:T(8,128)(2,1)S(1)} %collective-permute-done.8.refs_1_), channel_id=1, source_target_pairs={{0,32},{4,228},{8,40},{12,236},{16,48},{20,244},{24,56},{28,252},{... | collective-permute-start | bytes 1105928 | tf_op jit(solution)/shard_map/ppermute | solution.py:627
  25.8 8.7 %collective-permute-start.11 = (bf16[720,256]{1,0:T(8,128)(2,1)S(1)}, bf16[720,256]{1,0:T(8,128)(2,1)S(1)}, u32[]{:S(2)}, u32[]{:S(2)}) collective-permute-start(bf16[720,256]{1,0:T(8,128)(2,1)S(1)} %collective-permute-done.8.refs_1_), channel_id=1, source_target_pairs={{0,4},{4,0},{8,12},{12,8},{16,20},{20,16},{24,28},{28,24},{32,36},... | collective-permute-start | bytes 1105928 | tf_op jit(solution)/shard_map/ppermute | solution.py:627
  34.6 1.7 %collective-permute-start.12 = (bf16[720,256]{1,0:T(8,128)(2,1)S(1)}, bf16[720,256]{1,0:T(8,128)(2,1)S(1)}, u32[]{:S(2)}, u32[]{:S(2)}) collective-permute-start(bf16[720,256]{1,0:T(8,128)(2,1)S(1)} %collective-permute-done.9.refs_2_), channel_id=1, source_target_pairs={{0,4},{4,0},{8,12},{12,8},{16,20},{20,16},{24,28},{28,24},{32,36},... | collective-permute-start | bytes 1105928 | tf_op jit(solution)/shard_map/ppermute | solution.py:627
  34.6 8.7 %collective-permute-start.10 = (bf16[720,256]{1,0:T(8,128)(2,1)S(1)}, bf16[720,256]{1,0:T(8,128)(2,1)S(1)}, u32[]{:S(2)}, u32[]{:S(2)}) collective-permute-start(bf16[720,256]{1,0:T(8,128)(2,1)S(1)} %collective-permute-done.9.refs_2_), channel_id=1, source_target_pairs={{0,32},{4,228},{8,40},{12,236},{16,48},{20,244},{24,56},{28,252},{... | collective-permute-start | bytes 1105928 | tf_op jit(solution)/shard_map/ppermute | solution.py:627
  40.2 11.5 %copy-start.3 = (bf16[512,1024]{1,0:T(8,128)(2,1)S(1)}, bf16[512,1024]{1,0:T(8,128)(2,1)}, u32[]{:S(2)}) copy-start(bf16[512,1024]{1,0:T(8,128)(2,1)} %wout_ref.1) | copy-start | bytes 3145732
  43.3 1.7 %collective-permute-start.14 = (bf16[720,256]{1,0:T(8,128)(2,1)S(1)}, bf16[720,256]{1,0:T(8,128)(2,1)S(1)}, u32[]{:S(2)}, u32[]{:S(2)}) collective-permute-start(bf16[720,256]{1,0:T(8,128)(2,1)S(1)} %collective-permute-done.10.came), channel_id=1, source_target_pairs={{0,4},{4,0},{8,12},{12,8},{16,20},{20,16},{24,28},{28,24},{32,36},... | collective-permute-start | bytes 1105928 | tf_op jit(solution)/shard_map/ppermute | solution.py:627
  43.3 6.9 %collective-permute-start.13 = (bf16[368,256]{1,0:T(8,128)(2,1)S(1)}, bf16[368,256]{1,0:T(8,128)(2,1)S(1)}, u32[]{:S(2)}, u32[]{:S(2)}) collective-permute-start(bf16[368,256]{1,0:T(8,128)(2,1)S(1)} %constant_dynamic-slice_fusion.4), channel_id=1, source_target_pairs={{0,32},{4,228},{8,40},{12,236},{16,48},{20,244},{24,56},{28,252},{... | collective-permute-start | bytes 565256 | tf_op jit(solution)/shard_map/ppermute | solution.py:627
  50.2 1.4 %collective-permute-start.15 = (bf16[368,256]{1,0:T(8,128)(2,1)S(1)}, bf16[368,256]{1,0:T(8,128)(2,1)S(1)}, u32[]{:S(2)}, u32[]{:S(2)}) collective-permute-start(bf16[368,256]{1,0:T(8,128)(2,1)S(1)} %collective-permute-done.13.came), channel_id=1, source_target_pairs={{0,4},{4,0},{8,12},{12,8},{16,20},{20,16},{24,28},{28,24},{32,36},... | collective-permute-start | bytes 565256 | tf_op jit(solution)/shard_map/ppermute | solution.py:627
  54.7 9.6 %copy-start = (bf16[512,256]{1,0:T(8,128)(2,1)S(1)}, bf16[512,256]{1,0:T(8,128)(2,1)}, u32[]{:S(2)}) copy-start(bf16[512,256]{1,0:T(8,128)(2,1)} %skip_ref.1) | copy-start | bytes 786436
  54.7 9.6 %copy-start.2 = (s32[1,192]{1,0:T(1,128)S(1)}, s32[1,192]{1,0:T(1,128)}, u32[]{:S(2)}) copy-start(s32[1,192]{1,0:T(1,128)} %len_ref.1) | copy-start | bytes 2308
  54.7 11.8 %copy-start.1 = (f32[31,256]{1,0:T(8,128)S(1)}, f32[31,256]{1,0:T(8,128)}, u32[]{:S(2)}) copy-start(f32[31,256]{1,0:T(8,128)} %taps_ref.3) | copy-start | bytes 95236
  54.7 6.2 %collective-permute-start.16 = (bf16[192,256]{1,0:T(8,128)(2,1)S(1)}, bf16[192,256]{1,0:T(8,128)(2,1)S(1)}, u32[]{:S(2)}, u32[]{:S(2)}) collective-permute-start(bf16[192,256]{1,0:T(8,128)(2,1)S(1)} %get-tuple-element.291), channel_id=1, source_target_pairs={{0,1},{1,2},{2,3},{3,0},{4,5},{5,6},{6,7},{7,4},{8,9},{9,10},{10,1... | collective-permute-start | bytes 294920 | tf_op jit(solution)/shard_map/ppermute | solution.py:662
  56.4 7.9 %collective-permute-start.17 = (bf16[192,256]{1,0:T(8,128)(2,1)S(1)}, bf16[192,256]{1,0:T(8,128)(2,1)S(1)}, u32[]{:S(2)}, u32[]{:S(2)}) collective-permute-start(bf16[192,256]{1,0:T(8,128)(2,1)S(1)} %get-tuple-element.292), channel_id=1, source_target_pairs={{0,2},{1,3},{2,0},{3,1},{4,6},{5,7},{6,4},{7,5},{8,10},{9,11},{10,... | collective-permute-start | bytes 294920 | tf_op jit(solution)/shard_map/ppermute | solution.py:662
  59.3 5.0 %collective-permute-start.18 = (bf16[192,256]{1,0:T(8,128)(2,1)S(1)}, bf16[192,256]{1,0:T(8,128)(2,1)S(1)}, u32[]{:S(2)}, u32[]{:S(2)}) collective-permute-start(bf16[192,256]{1,0:T(8,128)(2,1)S(1)} %get-tuple-element.293), channel_id=1, source_target_pairs={{0,3},{1,0},{2,1},{3,2},{4,7},{5,4},{6,5},{7,6},{8,11},{9,8},{10,9... | collective-permute-start | bytes 294920 | tf_op jit(solution)/shard_map/ppermute | solution.py:662
  64.6 8.4 %collective-permute-start.19 = (bf16[32,256]{1,0:T(8,128)(2,1)S(1)}, bf16[32,256]{1,0:T(8,128)(2,1)S(1)}, u32[]{:S(2)}, u32[]{:S(2)}) collective-permute-start(bf16[32,256]{1,0:T(8,128)(2,1)S(1)} %get-tuple-element.295), channel_id=1, source_target_pairs={{0,4},{4,8},{8,12},{12,16},{16,20},{20,24},{24,28},{28,32},{32,36}... | collective-permute-start | bytes 49160 | tf_op jit(solution)/shard_map/ppermute | solution.py:665

commit v3 on v2

--- a/solution.py
+++ b/solution.py
@@ -564,17 +564,19 @@
     byte_rows, channels = mixed_ref.shape
     ext[:HALO, :] = jnp.zeros((HALO, channels), F32)
     ext[HALO:, :] = mixed_ref[...].astype(F32)
-    block = 64
-
-    def per_block(i, _):
-        first = pl.multiple_of(i * block, block)
+    block = 128
+    lags = taps_ref.shape[0]
+
+    for first in range(0, byte_rows, block):
         for low in range(0, channels, 128):
             part = slice(low, low + 128)
-            window = ext[pl.ds(first, block + HALO), part]
-            out_ref[pl.ds(first, block), part] = filtered(window, taps_ref[:, part])
-        return 0
-
-    lax.fori_loop(0, byte_rows // block, per_block, 0)
+            total = jnp.zeros((block, 128), F32)
+            for lag in range(lags):
+                start = first + HALO - lag
+                total += taps_ref[lag : lag + 1, part] * ext[start : start + block, part]
+            here = ext[first + HALO : first + HALO + block, part]
+            silu = total / (1.0 + jnp.exp(-total))
+            out_ref[first : first + block, part] = (here + silu).astype(BF)
 
 
 def rim_kernel(given_hbm, rim_ref, mixed_ref, taps_ref, out_hbm, rows, sem):
@@ -644,7 +646,8 @@
     y = lax.axis_index("section")
     index = jnp.stack([seq // (2 * NX), (seq // 2) % NX, seq % 2, y]).astype(jnp.int32)
     kv, x, scale = pool(span_len, enc, gain.reshape(1, -1), wk, wv)
-    column = [kv, along_x(kv, 1), along_x(kv, -1), along_x(kv, 2)]
+    across = along_x(kv, 2)
+    column = [kv, along_x(kv, 1), along_x(kv, -1), across]
     plane = compact(index, column + [swap(v) for v in column])
     first, q = lax.optimization_barrier((round_z(plane), query(x, wq, scale)))
     came = [first]
@@ -659,7 +662,7 @@
         crowded > 0, lambda _: attend_any(kv, q, span_len, wout, y), lambda given: given, parts
     )
     sent = [
-        lax.ppermute(parts[k], "section", [(i, (i + k) % 4) for i in range(4)]) for k in (1, 2, 3)
+        lax.ppermute(parts[k], "section", [(i, (i + k) % 4) for i in range(4)]) for k in (2, 1, 3)
     ]
     mixed, tail = mix(span_len, skip, [parts[0]] + sent)
     rim = lax.ppermute(tail, "seq", [(i, i + 1) for i in range(2 * NX * NZ - 1)])

time: 75.2 us -> 74.5 us (level); the launches traced: 73.9 us -> 74.1 us
  starting transfers between devices: 14.2 us -> 15 us
    ppermute x3, waiting for transfers between devices: 3.61 us -> 2.59 us  [per_device(): lax.ppermute(parts[k], 'section', [(i, (i + k) % 4) for i in range(4)])]
  transfers between devices with their start and end apart: 19 -> 19, of which waited for: 14 -> 14; matrix products, arithmetic and copies ran while one was open for 0% -> 0% of each run, Pallas kernels for 19% -> 18%
where the time goes in v3:
time: 74.5 us; the launch traced here: 74.1 us
  waiting for transfers between devices  34.6 us (46%)
  Pallas kernels  23.5 us (32%)
  starting transfers between devices  15 us (20%)
  between operations  0.99 us (1%)
    ppermute x15, waiting for transfers between devices, seq_permute(): return lax.ppermute(value, 'seq', pairs)  28.6 us
    ppermute x3, starting transfers between devices, per_device(): lax.ppermute(parts[k], 'section', [(i, (i + k) % 4) for i in range(4)])  6.52 us
    ppermute x15, starting transfers between devices, seq_permute(): return lax.ppermute(value, 'seq', pairs)  6.33 us
    pallas_call x1, Pallas kernels, pool(): pl.pallas_call(pool_kernel, in_specs=[anywhere()] * 5, out_specs=[vmem()]...  4.71 us
    pallas_call x1, Pallas kernels, query(): pl.pallas_call(query_kernel, in_specs=[vmem(), vmem(), anywhere()], out_s...  4.11 us
    ppermute x1, waiting for transfers between devices, per_device(): lax.ppermute(tail, 'seq', [(i, i + 1) for i in range(2 * NX * NZ - 1)])  3.36 us
    pallas_call x1, Pallas kernels, attend_near(): pl.pallas_call(attend_near_kernel, in_specs=[pl.BlockSpec(memory_space=pl...  3.31 us
    pallas_call x1, Pallas kernels, attend_far(): pl.pallas_call(attend_far_kernel, in_specs=[pl.BlockSpec(memory_space=plt...  2.96 us
  transfers between devices with their start and end apart: 19, of which 14 were waited for; matrix products, arithmetic and copies ran while one was open for 0% of the time, Pallas kernels for 18%

profile of v3, /device:TPU:128, one launch (start us, length us, event | category | flops | bytes accessed | tf_op | source)
XLA Modules:
  0.0 74.1 jit_solution(17530839518699663399)
XLA Ops:
  0.0 4.7 %pool.1 = (bf16[208,256]{1,0:T(8,128)(2,1)S(1)}, bf16[192,4096]{1,0:T(8,128)(2,1)}, f32[192,128]{1,0:T(8,128)}) custom-call(s32[1,192]{1,0:T(1,128)} %len_ref.1, f32[1,4096]{1,0:T(1,128)} %bitcast.38, bf16[512,4096]{1,0:T(8,128)(2,1)} %enc_hbm.1, bf16[4096,128]{1,0:T(8,128)(2,1)} %wk_hbm.1, bf16[4096,128]{1,0:T(8,128)(2,1)} %wv_hbm.1), custom_call_target="tpu_custom_call" | custom-call | flops 1207959552 | bytes 7864320 | tf_op jit(solution)/shard_map/pool/pallas_call | solution.py:106
  4.7 1.6 %collective-permute-start.1 = (bf16[208,256]{1,0:T(8,128)(2,1)S(1)}, bf16[208,256]{1,0:T(8,128)(2,1)S(1)}, u32[]{:S(2)}, u32[]{:S(2)}) collective-permute-start(bf16[208,256]{1,0:T(8,128)(2,1)S(1)} %get-tuple-element.262.refs_0_), channel_id=1, source_target_pairs={{0,8},{4,12},{8,16},{12,20},{16,24},{20,28},{24,0},{28,4},{32,40},... | collective-permute-start | bytes 319496 | tf_op jit(solution)/shard_map/ppermute | solution.py:629
  6.3 1.7 %collective-permute-start.2 = (bf16[208,256]{1,0:T(8,128)(2,1)S(1)}, bf16[208,256]{1,0:T(8,128)(2,1)S(1)}, u32[]{:S(2)}, u32[]{:S(2)}) collective-permute-start(bf16[208,256]{1,0:T(8,128)(2,1)S(1)} %get-tuple-element.262.refs_0_), channel_id=1, source_target_pairs={{0,24},{4,28},{8,0},{12,4},{16,8},{20,12},{24,16},{28,20},{32,56},... | collective-permute-start | bytes 319496 | tf_op jit(solution)/shard_map/ppermute | solution.py:629
  8.0 1.8 %collective-permute-start.3 = (bf16[208,256]{1,0:T(8,128)(2,1)S(1)}, bf16[208,256]{1,0:T(8,128)(2,1)S(1)}, u32[]{:S(2)}, u32[]{:S(2)}) collective-permute-start(bf16[208,256]{1,0:T(8,128)(2,1)S(1)} %get-tuple-element.262.refs_0_), channel_id=1, source_target_pairs={{0,16},{4,20},{8,24},{12,28},{16,0},{20,4},{24,8},{28,12},{32,48},... | collective-permute-start | bytes 319496 | tf_op jit(solution)/shard_map/ppermute | solution.py:629
  9.8 0.9 %collective-permute-done.1.refs_1_ = bf16[208,256]{1,0:T(8,128)(2,1)S(1)} collective-permute-done((bf16[208,256]{1,0:T(8,128)(2,1)S(1)}, bf16[208,256]{1,0:T(8,128)(2,1)S(1)}, u32[]{:S(2)}, u32[]{:S(2)}) %collective-permute-start.1) | collective-permute-done | bytes 106528 | tf_op jit(solution)/shard_map/ppermute | solution.py:629
  10.7 1.9 %collective-permute-done.2.refs_2_ = bf16[208,256]{1,0:T(8,128)(2,1)S(1)} collective-permute-done((bf16[208,256]{1,0:T(8,128)(2,1)S(1)}, bf16[208,256]{1,0:T(8,128)(2,1)S(1)}, u32[]{:S(2)}, u32[]{:S(2)}) %collective-permute-start.2) | collective-permute-done | bytes 106528 | tf_op jit(solution)/shard_map/ppermute | solution.py:629
  12.6 1.7 %collective-permute-done.3.refs_3_ = bf16[208,256]{1,0:T(8,128)(2,1)S(1)} collective-permute-done((bf16[208,256]{1,0:T(8,128)(2,1)S(1)}, bf16[208,256]{1,0:T(8,128)(2,1)S(1)}, u32[]{:S(2)}, u32[]{:S(2)}) %collective-permute-start.3) | collective-permute-done | bytes 106528 | tf_op jit(solution)/shard_map/ppermute | solution.py:629
  14.3 1.2 %collective-permute-done.7.refs_7_ = bf16[208,256]{1,0:T(8,128)(2,1)S(1)} collective-permute-done((bf16[208,256]{1,0:T(8,128)(2,1)S(1)}, bf16[208,256]{1,0:T(8,128)(2,1)S(1)}, u32[]{:S(2)}, u32[]{:S(2)}) %collective-permute-start.7) | collective-permute-done | bytes 106528 | tf_op jit(solution)/shard_map/ppermute | solution.py:629
  15.6 1.5 %compact.1.refs_0_ = bf16[720,256]{1,0:T(8,128)(2,1)S(1)} custom-call(s32[4]{0:T(128)S(1)} %pad_add_fusion.index_ref, bf16[208,256]{1,0:T(8,128)(2,1)S(1)} %get-tuple-element.262.refs_0_, bf16[208,256]{1,0:T(8,128)(2,1)S(1)} %collective-permute-done.1.refs_1_, bf16[208,256]{1,0:T(8,128)(2,1)S(1)} %collective-permute-done.2.refs_2_, ...), custom_call_target="tpu_custom_call" | custom-call | tf_op jit(solution)/shard_map/compact/pallas_call | solution.py:200
  17.0 1.1 %collective-permute-start.8 = (bf16[720,256]{1,0:T(8,128)(2,1)S(1)}, bf16[720,256]{1,0:T(8,128)(2,1)S(1)}, u32[]{:S(2)}, u32[]{:S(2)}) collective-permute-start(bf16[720,256]{1,0:T(8,128)(2,1)S(1)} %compact.1.refs_0_), channel_id=1, source_target_pairs={{0,32},{4,228},{8,40},{12,236},{16,48},{20,244},{24,56},{28,252},{... | collective-permute-start | bytes 1105928 | tf_op jit(solution)/shard_map/ppermute | solution.py:629
  18.1 4.1 %query.1.q_ref = bf16[192,512]{1,0:T(8,128)(2,1)S(1)} custom-call(bf16[192,4096]{1,0:T(8,128)(2,1)} %get-tuple-element.263.x_ref, f32[192,128]{1,0:T(8,128)} %get-tuple-element.264.scale_ref, bf16[4096,512]{1,0:T(8,128)(2,1)} %wq_hbm.1), custom_call_target="tpu_custom_call" | custom-call | flops 805306368 | bytes 5767168 | tf_op jit(solution)/shard_map/query/pallas_call | solution.py:150
  22.3 3.6 %collective-permute-done.8.refs_1_ = bf16[720,256]{1,0:T(8,128)(2,1)S(1)} collective-permute-done((bf16[720,256]{1,0:T(8,128)(2,1)S(1)}, bf16[720,256]{1,0:T(8,128)(2,1)S(1)}, u32[]{:S(2)}, u32[]{:S(2)}) %collective-permute-start.8) | collective-permute-done | bytes 368672 | tf_op jit(solution)/shard_map/ppermute | solution.py:629
  25.8 8.7 %collective-permute-done.9.refs_2_ = bf16[720,256]{1,0:T(8,128)(2,1)S(1)} collective-permute-done((bf16[720,256]{1,0:T(8,128)(2,1)S(1)}, bf16[720,256]{1,0:T(8,128)(2,1)S(1)}, u32[]{:S(2)}, u32[]{:S(2)}) %collective-permute-start.9) | collective-permute-done | bytes 368672 | tf_op jit(solution)/shard_map/ppermute | solution.py:629
  34.6 1.7 %collective-permute-done.12.refs_4_ = bf16[720,256]{1,0:T(8,128)(2,1)S(1)} collective-permute-done((bf16[720,256]{1,0:T(8,128)(2,1)S(1)}, bf16[720,256]{1,0:T(8,128)(2,1)S(1)}, u32[]{:S(2)}, u32[]{:S(2)}) %collective-permute-start.12) | collective-permute-done | bytes 368672 | tf_op jit(solution)/shard_map/ppermute | solution.py:629
  36.3 3.3 %attend_near.1 = (f32[2,384,128]{2,1,0:T(8,128)S(1)}, f32[2,384,128]{2,1,0:T(8,128)S(1)}, f32[2,384,128]{2,1,0:T(8,128)S(1)}, s32[2]{0:T(128)S(1)}) custom-call(s32[4]{0:T(128)S(1)} %pad_add_fusion.index_ref, bf16[192,512]{1,0:T(8,128)(2,1)S(1)} %query.1.q_ref, bf16[720,256]{1,0:T(8,128)(2,1)S(1)} %compact.1.refs_0_, ...), custom_call_target="tpu_custom_call" | custom-call | flops 3623878656 | bytes 8388608 | tf_op jit(solution)/shard_map/attend_near/pallas_call | solution.py:342
  39.6 3.7 %collective-permute-done.10.came = bf16[720,256]{1,0:T(8,128)(2,1)S(1)} collective-permute-done((bf16[720,256]{1,0:T(8,128)(2,1)S(1)}, bf16[720,256]{1,0:T(8,128)(2,1)S(1)}, u32[]{:S(2)}, u32[]{:S(2)}) %collective-permute-start.10) | collective-permute-done | bytes 368672 | tf_op jit(solution)/shard_map/ppermute | solution.py:629
  43.3 0.1 collective-permute-start.13
  43.4 1.6 %collective-permute-done.14.swapped = bf16[720,256]{1,0:T(8,128)(2,1)S(1)} collective-permute-done((bf16[720,256]{1,0:T(8,128)(2,1)S(1)}, bf16[720,256]{1,0:T(8,128)(2,1)S(1)}, u32[]{:S(2)}, u32[]{:S(2)}) %collective-permute-start.14) | collective-permute-done | bytes 368672 | tf_op jit(solution)/shard_map/ppermute | solution.py:629
  45.0 2.9 %attend_more.1 = (f32[2,384,128]{2,1,0:T(8,128)S(1)}, f32[2,384,128]{2,1,0:T(8,128)S(1)}, f32[2,384,128]{2,1,0:T(8,128)S(1)}, s32[2]{0:T(128)S(1)}) custom-call(s32[4]{0:T(128)S(1)} %pad_add_fusion.index_ref, s32[2]{0:T(128)S(1)} %get-tuple-element.272.info_ref, bf16[192,512]{1,0:T(8,128)(2,1)S(1)} %query.1.q_ref, ...), custom_call_target="tpu_custom_call" | custom-call | flops 1811939328 | bytes 8388608 | tf_op jit(solution)/shard_map/attend_more/pallas_call | solution.py:405
  47.9 2.3 %collective-permute-done.13.came = bf16[368,256]{1,0:T(8,128)(2,1)S(1)} collective-permute-done((bf16[368,256]{1,0:T(8,128)(2,1)S(1)}, bf16[368,256]{1,0:T(8,128)(2,1)S(1)}, u32[]{:S(2)}, u32[]{:S(2)}) %collective-permute-start.13) | collective-permute-done | bytes 188448 | tf_op jit(solution)/shard_map/ppermute | solution.py:629
  50.2 1.4 %collective-permute-done.15.swapped = bf16[368,256]{1,0:T(8,128)(2,1)S(1)} collective-permute-done((bf16[368,256]{1,0:T(8,128)(2,1)S(1)}, bf16[368,256]{1,0:T(8,128)(2,1)S(1)}, u32[]{:S(2)}, u32[]{:S(2)}) %collective-permute-start.15) | collective-permute-done | bytes 188448 | tf_op jit(solution)/shard_map/ppermute | solution.py:629
  51.6 3.0 %attend_far.1 = (bf16[192,256]{1,0:T(8,128)(2,1)S(1)}, bf16[192,256]{1,0:T(8,128)(2,1)S(1)}, bf16[192,256]{1,0:T(8,128)(2,1)S(1)}, bf16[192,256]{1,0:T(8,128)(2,1)S(1)}, s32[1]{0:T(128)}) custom-call(s32[4]{0:T(128)S(1)} %pad_add_fusion.index_ref, s32[2]{0:T(128)S(1)} %get-tuple-element.280.info_ref, bf16[192,512]{1,0:T(8,128)(2,1)S(1)} %query.1.q_ref, ...), custom_call_target="tpu_custom_call" | custom-call | tf_op jit(solution)/shard_map/attend_far/pallas_call | solution.py:467
  55.3 3.3 %collective-permute-start.16 = (bf16[192,256]{1,0:T(8,128)(2,1)S(1)}, bf16[192,256]{1,0:T(8,128)(2,1)S(1)}, u32[]{:S(2)}, u32[]{:S(2)}) collective-permute-start(bf16[192,256]{1,0:T(8,128)(2,1)S(1)} %get-tuple-element.291), channel_id=1, source_target_pairs={{0,2},{1,3},{2,0},{3,1},{4,6},{5,7},{6,4},{7,5},{8,10},{9,11},{10,... | collective-permute-start | bytes 294920 | tf_op jit(solution)/shard_map/ppermute | solution.py:665
  58.6 0.7 collective-permute-start.17
  59.2 2.6 %collective-permute-start.18 = (bf16[192,256]{1,0:T(8,128)(2,1)S(1)}, bf16[192,256]{1,0:T(8,128)(2,1)S(1)}, u32[]{:S(2)}, u32[]{:S(2)}) collective-permute-start(bf16[192,256]{1,0:T(8,128)(2,1)S(1)} %get-tuple-element.293), channel_id=1, source_target_pairs={{0,3},{1,0},{2,1},{3,2},{4,7},{5,4},{6,5},{7,6},{8,11},{9,8},{10,9... | collective-permute-start | bytes 294920 | tf_op jit(solution)/shard_map/ppermute | solution.py:665
  61.8 0.2 collective-permute-done.16.p1
  62.0 2.4 %collective-permute-done.17.p2 = bf16[192,256]{1,0:T(8,128)(2,1)S(1)} collective-permute-done((bf16[192,256]{1,0:T(8,128)(2,1)S(1)}, bf16[192,256]{1,0:T(8,128)(2,1)S(1)}, u32[]{:S(2)}, u32[]{:S(2)}) %collective-permute-start.17) | collective-permute-done | bytes 98336 | tf_op jit(solution)/shard_map/ppermute | solution.py:665
  64.4 0.3 mix.1
  64.7 2.1 %collective-permute-start.19 = (bf16[32,256]{1,0:T(8,128)(2,1)S(1)}, bf16[32,256]{1,0:T(8,128)(2,1)S(1)}, u32[]{:S(2)}, u32[]{:S(2)}) collective-permute-start(bf16[32,256]{1,0:T(8,128)(2,1)S(1)} %get-tuple-element.295), channel_id=1, source_target_pairs={{0,4},{4,8},{8,12},{12,16},{16,20},{20,24},{24,28},{28,32},{32,36}... | collective-permute-start | bytes 49160 | tf_op jit(solution)/shard_map/ppermute | solution.py:668
  66.9 2.9 %convolve.1.given_hbm = bf16[512,256]{1,0:T(8,128)(2,1)} custom-call(bf16[512,256]{1,0:T(8,128)(2,1)S(1)} %get-tuple-element.294.mixed_ref, f32[31,256]{1,0:T(8,128)S(1)} %copy-done.1), custom_call_target="tpu_custom_call" | custom-call | flops 8126464 | bytes 2097152 | tf_op jit(solution)/shard_map/convolve/pallas_call | solution.py:594
  69.8 3.4 %collective-permute-done.19.rim_ref = bf16[32,256]{1,0:T(8,128)(2,1)S(1)} collective-permute-done((bf16[32,256]{1,0:T(8,128)(2,1)S(1)}, bf16[32,256]{1,0:T(8,128)(2,1)S(1)}, u32[]{:S(2)}, u32[]{:S(2)}) %collective-permute-start.19) | collective-permute-done | bytes 16416 | tf_op jit(solution)/shard_map/ppermute | solution.py:668
  73.1 0.8 %first_rows.1 = bf16[512,256]{1,0:T(8,128)(2,1)} custom-call(bf16[512,256]{1,0:T(8,128)(2,1)} %convolve.1.given_hbm, bf16[32,256]{1,0:T(8,128)(2,1)S(1)} %collective-permute-done.19.rim_ref, bf16[512,256]{1,0:T(8,128)(2,1)S(1)} %get-tuple-element.294.mixed_ref, f32[31,256]{1,0:T(8,128)S(1)} %copy-done.1), custom_call_target="tpu_custom_call", output_to_operand_aliasing={{}: (0, {})} | custom-call | tf_op jit(solution)/shard_map/first_rows/pallas_call | solution.py:609
  (26 shorter events, 0.2 us)
Async XLA Ops:
  4.7 6.0 %collective-permute-start.1 = (bf16[208,256]{1,0:T(8,128)(2,1)S(1)}, bf16[208,256]{1,0:T(8,128)(2,1)S(1)}, u32[]{:S(2)}, u32[]{:S(2)}) collective-permute-start(bf16[208,256]{1,0:T(8,128)(2,1)S(1)} %get-tuple-element.262.refs_0_), channel_id=1, source_target_pairs={{0,8},{4,12},{8,16},{12,20},{16,24},{20,28},{24,0},{28,4},{32,40},... | collective-permute-start | bytes 319496 | tf_op jit(solution)/shard_map/ppermute | solution.py:629
  6.3 6.3 %collective-permute-start.2 = (bf16[208,256]{1,0:T(8,128)(2,1)S(1)}, bf16[208,256]{1,0:T(8,128)(2,1)S(1)}, u32[]{:S(2)}, u32[]{:S(2)}) collective-permute-start(bf16[208,256]{1,0:T(8,128)(2,1)S(1)} %get-tuple-element.262.refs_0_), channel_id=1, source_target_pairs={{0,24},{4,28},{8,0},{12,4},{16,8},{20,12},{24,16},{28,20},{32,56},... | collective-permute-start | bytes 319496 | tf_op jit(solution)/shard_map/ppermute | solution.py:629
  8.0 6.2 %collective-permute-start.3 = (bf16[208,256]{1,0:T(8,128)(2,1)S(1)}, bf16[208,256]{1,0:T(8,128)(2,1)S(1)}, u32[]{:S(2)}, u32[]{:S(2)}) collective-permute-start(bf16[208,256]{1,0:T(8,128)(2,1)S(1)} %get-tuple-element.262.refs_0_), channel_id=1, source_target_pairs={{0,16},{4,20},{8,24},{12,28},{16,0},{20,4},{24,8},{28,12},{32,48},... | collective-permute-start | bytes 319496 | tf_op jit(solution)/shard_map/ppermute | solution.py:629
  9.8 4.5 %collective-permute-start.4 = (bf16[208,256]{1,0:T(8,128)(2,1)S(1)}, bf16[208,256]{1,0:T(8,128)(2,1)S(1)}, u32[]{:S(2)}, u32[]{:S(2)}) collective-permute-start(bf16[208,256]{1,0:T(8,128)(2,1)S(1)} %get-tuple-element.262.refs_0_), channel_id=1, source_target_pairs={{0,4},{4,0},{8,12},{12,8},{16,20},{20,16},{24,28},{28,24},{32,36},... | collective-permute-start | bytes 319496 | tf_op jit(solution)/shard_map/ppermute | solution.py:629
  10.7 3.6 %collective-permute-start.5 = (bf16[208,256]{1,0:T(8,128)(2,1)S(1)}, bf16[208,256]{1,0:T(8,128)(2,1)S(1)}, u32[]{:S(2)}, u32[]{:S(2)}) collective-permute-start(bf16[208,256]{1,0:T(8,128)(2,1)S(1)} %collective-permute-done.1.refs_1_), channel_id=1, source_target_pairs={{0,4},{4,0},{8,12},{12,8},{16,20},{20,16},{24,28},{28,24},{32,36},... | collective-permute-start | bytes 319496 | tf_op jit(solution)/shard_map/ppermute | solution.py:629
  12.6 1.8 %collective-permute-start.6 = (bf16[208,256]{1,0:T(8,128)(2,1)S(1)}, bf16[208,256]{1,0:T(8,128)(2,1)S(1)}, u32[]{:S(2)}, u32[]{:S(2)}) collective-permute-start(bf16[208,256]{1,0:T(8,128)(2,1)S(1)} %collective-permute-done.2.refs_2_), channel_id=1, source_target_pairs={{0,4},{4,0},{8,12},{12,8},{16,20},{20,16},{24,28},{28,24},{32,36},... | collective-permute-start | bytes 319496 | tf_op jit(solution)/shard_map/ppermute | solution.py:629
  14.2 1.3 %collective-permute-start.7 = (bf16[208,256]{1,0:T(8,128)(2,1)S(1)}, bf16[208,256]{1,0:T(8,128)(2,1)S(1)}, u32[]{:S(2)}, u32[]{:S(2)}) collective-permute-start(bf16[208,256]{1,0:T(8,128)(2,1)S(1)} %collective-permute-done.3.refs_3_), channel_id=1, source_target_pairs={{0,4},{4,0},{8,12},{12,8},{16,20},{20,16},{24,28},{28,24},{32,36},... | collective-permute-start | bytes 319496 | tf_op jit(solution)/shard_map/ppermute | solution.py:629
  17.0 8.8 %collective-permute-start.8 = (bf16[720,256]{1,0:T(8,128)(2,1)S(1)}, bf16[720,256]{1,0:T(8,128)(2,1)S(1)}, u32[]{:S(2)}, u32[]{:S(2)}) collective-permute-start(bf16[720,256]{1,0:T(8,128)(2,1)S(1)} %compact.1.refs_0_), channel_id=1, source_target_pairs={{0,32},{4,228},{8,40},{12,236},{16,48},{20,244},{24,56},{28,252},{... | collective-permute-start | bytes 1105928 | tf_op jit(solution)/shard_map/ppermute | solution.py:629
  25.8 8.7 %collective-permute-start.9 = (bf16[720,256]{1,0:T(8,128)(2,1)S(1)}, bf16[720,256]{1,0:T(8,128)(2,1)S(1)}, u32[]{:S(2)}, u32[]{:S(2)}) collective-permute-start(bf16[720,256]{1,0:T(8,128)(2,1)S(1)} %collective-permute-done.8.refs_1_), channel_id=1, source_target_pairs={{0,32},{4,228},{8,40},{12,236},{16,48},{20,244},{24,56},{28,252},{... | collective-permute-start | bytes 1105928 | tf_op jit(solution)/shard_map/ppermute | solution.py:629
  25.8 8.7 %collective-permute-start.11 = (bf16[720,256]{1,0:T(8,128)(2,1)S(1)}, bf16[720,256]{1,0:T(8,128)(2,1)S(1)}, u32[]{:S(2)}, u32[]{:S(2)}) collective-permute-start(bf16[720,256]{1,0:T(8,128)(2,1)S(1)} %collective-permute-done.8.refs_1_), channel_id=1, source_target_pairs={{0,4},{4,0},{8,12},{12,8},{16,20},{20,16},{24,28},{28,24},{32,36},... | collective-permute-start | bytes 1105928 | tf_op jit(solution)/shard_map/ppermute | solution.py:629
  34.6 1.7 %collective-permute-start.12 = (bf16[720,256]{1,0:T(8,128)(2,1)S(1)}, bf16[720,256]{1,0:T(8,128)(2,1)S(1)}, u32[]{:S(2)}, u32[]{:S(2)}) collective-permute-start(bf16[720,256]{1,0:T(8,128)(2,1)S(1)} %collective-permute-done.9.refs_2_), channel_id=1, source_target_pairs={{0,4},{4,0},{8,12},{12,8},{16,20},{20,16},{24,28},{28,24},{32,36},... | collective-permute-start | bytes 1105928 | tf_op jit(solution)/shard_map/ppermute | solution.py:629
  34.6 8.7 %collective-permute-start.10 = (bf16[720,256]{1,0:T(8,128)(2,1)S(1)}, bf16[720,256]{1,0:T(8,128)(2,1)S(1)}, u32[]{:S(2)}, u32[]{:S(2)}) collective-permute-start(bf16[720,256]{1,0:T(8,128)(2,1)S(1)} %collective-permute-done.9.refs_2_), channel_id=1, source_target_pairs={{0,32},{4,228},{8,40},{12,236},{16,48},{20,244},{24,56},{28,252},{... | collective-permute-start | bytes 1105928 | tf_op jit(solution)/shard_map/ppermute | solution.py:629
  39.6 12.0 %copy-start.3 = (bf16[512,1024]{1,0:T(8,128)(2,1)S(1)}, bf16[512,1024]{1,0:T(8,128)(2,1)}, u32[]{:S(2)}) copy-start(bf16[512,1024]{1,0:T(8,128)(2,1)} %wout_ref.1) | copy-start | bytes 3145732
  43.3 1.7 %collective-permute-start.14 = (bf16[720,256]{1,0:T(8,128)(2,1)S(1)}, bf16[720,256]{1,0:T(8,128)(2,1)S(1)}, u32[]{:S(2)}, u32[]{:S(2)}) collective-permute-start(bf16[720,256]{1,0:T(8,128)(2,1)S(1)} %collective-permute-done.10.came), channel_id=1, source_target_pairs={{0,4},{4,0},{8,12},{12,8},{16,20},{20,16},{24,28},{28,24},{32,36},... | collective-permute-start | bytes 1105928 | tf_op jit(solution)/shard_map/ppermute | solution.py:629
  43.3 6.9 %collective-permute-start.13 = (bf16[368,256]{1,0:T(8,128)(2,1)S(1)}, bf16[368,256]{1,0:T(8,128)(2,1)S(1)}, u32[]{:S(2)}, u32[]{:S(2)}) collective-permute-start(bf16[368,256]{1,0:T(8,128)(2,1)S(1)} %constant_dynamic-slice_fusion.4), channel_id=1, source_target_pairs={{0,32},{4,228},{8,40},{12,236},{16,48},{20,244},{24,56},{28,252},{... | collective-permute-start | bytes 565256 | tf_op jit(solution)/shard_map/ppermute | solution.py:629
  50.2 1.4 %collective-permute-start.15 = (bf16[368,256]{1,0:T(8,128)(2,1)S(1)}, bf16[368,256]{1,0:T(8,128)(2,1)S(1)}, u32[]{:S(2)}, u32[]{:S(2)}) collective-permute-start(bf16[368,256]{1,0:T(8,128)(2,1)S(1)} %collective-permute-done.13.came), channel_id=1, source_target_pairs={{0,4},{4,0},{8,12},{12,8},{16,20},{20,16},{24,28},{28,24},{32,36},... | collective-permute-start | bytes 565256 | tf_op jit(solution)/shard_map/ppermute | solution.py:629
  55.2 9.2 %copy-start = (bf16[512,256]{1,0:T(8,128)(2,1)S(1)}, bf16[512,256]{1,0:T(8,128)(2,1)}, u32[]{:S(2)}) copy-start(bf16[512,256]{1,0:T(8,128)(2,1)} %skip_ref.1) | copy-start | bytes 786436
  55.3 9.2 %copy-start.2 = (s32[1,192]{1,0:T(1,128)S(1)}, s32[1,192]{1,0:T(1,128)}, u32[]{:S(2)}) copy-start(s32[1,192]{1,0:T(1,128)} %len_ref.1) | copy-start | bytes 2308
  55.3 11.6 %copy-start.1 = (f32[31,256]{1,0:T(8,128)S(1)}, f32[31,256]{1,0:T(8,128)}, u32[]{:S(2)}) copy-start(f32[31,256]{1,0:T(8,128)} %taps_ref.3) | copy-start | bytes 95236
  55.3 6.7 %collective-permute-start.16 = (bf16[192,256]{1,0:T(8,128)(2,1)S(1)}, bf16[192,256]{1,0:T(8,128)(2,1)S(1)}, u32[]{:S(2)}, u32[]{:S(2)}) collective-permute-start(bf16[192,256]{1,0:T(8,128)(2,1)S(1)} %get-tuple-element.291), channel_id=1, source_target_pairs={{0,2},{1,3},{2,0},{3,1},{4,6},{5,7},{6,4},{7,5},{8,10},{9,11},{10,... | collective-permute-start | bytes 294920 | tf_op jit(solution)/shard_map/ppermute | solution.py:665
  58.6 5.8 %collective-permute-start.17 = (bf16[192,256]{1,0:T(8,128)(2,1)S(1)}, bf16[192,256]{1,0:T(8,128)(2,1)S(1)}, u32[]{:S(2)}, u32[]{:S(2)}) collective-permute-start(bf16[192,256]{1,0:T(8,128)(2,1)S(1)} %get-tuple-element.292), channel_id=1, source_target_pairs={{0,1},{1,2},{2,3},{3,0},{4,5},{5,6},{6,7},{7,4},{8,9},{9,10},{10,1... | collective-permute-start | bytes 294920 | tf_op jit(solution)/shard_map/ppermute | solution.py:665
  59.2 5.2 %collective-permute-start.18 = (bf16[192,256]{1,0:T(8,128)(2,1)S(1)}, bf16[192,256]{1,0:T(8,128)(2,1)S(1)}, u32[]{:S(2)}, u32[]{:S(2)}) collective-permute-start(bf16[192,256]{1,0:T(8,128)(2,1)S(1)} %get-tuple-element.293), channel_id=1, source_target_pairs={{0,3},{1,0},{2,1},{3,2},{4,7},{5,4},{6,5},{7,6},{8,11},{9,8},{10,9... | collective-permute-start | bytes 294920 | tf_op jit(solution)/shard_map/ppermute | solution.py:665
  64.7 8.4 %collective-permute-start.19 = (bf16[32,256]{1,0:T(8,128)(2,1)S(1)}, bf16[32,256]{1,0:T(8,128)(2,1)S(1)}, u32[]{:S(2)}, u32[]{:S(2)}) collective-permute-start(bf16[32,256]{1,0:T(8,128)(2,1)S(1)} %get-tuple-element.295), channel_id=1, source_target_pairs={{0,4},{4,8},{8,12},{12,16},{16,20},{20,24},{24,28},{28,32},{32,36}... | collective-permute-start | bytes 49160 | tf_op jit(solution)/shard_map/ppermute | solution.py:668

commit v4 on v3

--- a/solution.py
+++ b/solution.py
@@ -18,8 +18,8 @@
 PIECE = UPPER + HALF
 QT = 96
 KEYS = 512
-POOL_STEPS = 4
-DEPTH = 4
+POOL_STEPS = 8
+DEPTH = 8
 FULL = 62
 QUERY_LIMIT = 60
 HALO = 32

time: 74.5 us -> 75.1 us (level)
  transfers between devices with their start and end apart: 19 -> 19, of which waited for: 14 -> 14; matrix products, arithmetic and copies ran while one was open for 0% -> 0% of each run, Pallas kernels for 18% -> 17%
where the time goes in v4:
time: 75.1 us; the launch traced here: 74.8 us
  waiting for transfers between devices  34.7 us (46%)
  Pallas kernels  24.1 us (32%)
  starting transfers between devices  15 us (20%)
  between operations  0.99 us (1%)
    ppermute x15, waiting for transfers between devices, seq_permute(): return lax.ppermute(value, 'seq', pairs)  28.7 us
    ppermute x3, starting transfers between devices, per_device(): lax.ppermute(parts[k], 'section', [(i, (i + k) % 4) for i in range(4)])  6.52 us
    ppermute x15, starting transfers between devices, seq_permute(): return lax.ppermute(value, 'seq', pairs)  6.34 us
    pallas_call x1, Pallas kernels, pool(): pl.pallas_call(pool_kernel, in_specs=[anywhere()] * 5, out_specs=[vmem()]...  5.45 us
    pallas_call x1, Pallas kernels, query(): pl.pallas_call(query_kernel, in_specs=[vmem(), vmem(), anywhere()], out_s...  3.98 us
    pallas_call x1, Pallas kernels, attend_near(): pl.pallas_call(attend_near_kernel, in_specs=[pl.BlockSpec(memory_space=pl...  3.91 us
    ppermute x1, waiting for transfers between devices, per_device(): lax.ppermute(tail, 'seq', [(i, i + 1) for i in range(2 * NX * NZ - 1)])  3.36 us
    pallas_call x1, Pallas kernels, attend_far(): pl.pallas_call(attend_far_kernel, in_specs=[pl.BlockSpec(memory_space=plt...  2.97 us
  transfers between devices with their start and end apart: 19, of which 14 were waited for; matrix products, arithmetic and copies ran while one was open for 0% of the time, Pallas kernels for 17%

profile of v4, /device:TPU:128, one launch (start us, length us, event | category | flops | bytes accessed | tf_op | source)
XLA Modules:
  0.0 74.8 jit_solution(5603282721071139430)
XLA Ops:
  0.0 5.5 %pool.1 = (bf16[208,256]{1,0:T(8,128)(2,1)S(1)}, bf16[192,4096]{1,0:T(8,128)(2,1)}, f32[192,128]{1,0:T(8,128)}) custom-call(s32[1,192]{1,0:T(1,128)} %len_ref.1, f32[1,4096]{1,0:T(1,128)} %bitcast.38, bf16[512,4096]{1,0:T(8,128)(2,1)} %enc_hbm.1, bf16[4096,128]{1,0:T(8,128)(2,1)} %wk_hbm.1, bf16[4096,128]{1,0:T(8,128)(2,1)} %wv_hbm.1), custom_call_target="tpu_custom_call" | custom-call | flops 1207959552 | bytes 7864320 | tf_op jit(solution)/shard_map/pool/pallas_call | solution.py:106
  5.5 1.6 %collective-permute-start.1 = (bf16[208,256]{1,0:T(8,128)(2,1)S(1)}, bf16[208,256]{1,0:T(8,128)(2,1)S(1)}, u32[]{:S(2)}, u32[]{:S(2)}) collective-permute-start(bf16[208,256]{1,0:T(8,128)(2,1)S(1)} %get-tuple-element.262.refs_0_), channel_id=1, source_target_pairs={{0,8},{4,12},{8,16},{12,20},{16,24},{20,28},{24,0},{28,4},{32,40},... | collective-permute-start | bytes 319496 | tf_op jit(solution)/shard_map/ppermute | solution.py:629
  7.0 1.7 %collective-permute-start.2 = (bf16[208,256]{1,0:T(8,128)(2,1)S(1)}, bf16[208,256]{1,0:T(8,128)(2,1)S(1)}, u32[]{:S(2)}, u32[]{:S(2)}) collective-permute-start(bf16[208,256]{1,0:T(8,128)(2,1)S(1)} %get-tuple-element.262.refs_0_), channel_id=1, source_target_pairs={{0,24},{4,28},{8,0},{12,4},{16,8},{20,12},{24,16},{28,20},{32,56},... | collective-permute-start | bytes 319496 | tf_op jit(solution)/shard_map/ppermute | solution.py:629
  8.8 1.8 %collective-permute-start.3 = (bf16[208,256]{1,0:T(8,128)(2,1)S(1)}, bf16[208,256]{1,0:T(8,128)(2,1)S(1)}, u32[]{:S(2)}, u32[]{:S(2)}) collective-permute-start(bf16[208,256]{1,0:T(8,128)(2,1)S(1)} %get-tuple-element.262.refs_0_), channel_id=1, source_target_pairs={{0,16},{4,20},{8,24},{12,28},{16,0},{20,4},{24,8},{28,12},{32,48},... | collective-permute-start | bytes 319496 | tf_op jit(solution)/shard_map/ppermute | solution.py:629
  10.6 0.9 %collective-permute-done.1.refs_1_ = bf16[208,256]{1,0:T(8,128)(2,1)S(1)} collective-permute-done((bf16[208,256]{1,0:T(8,128)(2,1)S(1)}, bf16[208,256]{1,0:T(8,128)(2,1)S(1)}, u32[]{:S(2)}, u32[]{:S(2)}) %collective-permute-start.1) | collective-permute-done | bytes 106528 | tf_op jit(solution)/shard_map/ppermute | solution.py:629
  11.5 1.8 %collective-permute-done.2.refs_2_ = bf16[208,256]{1,0:T(8,128)(2,1)S(1)} collective-permute-done((bf16[208,256]{1,0:T(8,128)(2,1)S(1)}, bf16[208,256]{1,0:T(8,128)(2,1)S(1)}, u32[]{:S(2)}, u32[]{:S(2)}) %collective-permute-start.2) | collective-permute-done | bytes 106528 | tf_op jit(solution)/shard_map/ppermute | solution.py:629
  13.3 1.7 %collective-permute-done.3.refs_3_ = bf16[208,256]{1,0:T(8,128)(2,1)S(1)} collective-permute-done((bf16[208,256]{1,0:T(8,128)(2,1)S(1)}, bf16[208,256]{1,0:T(8,128)(2,1)S(1)}, u32[]{:S(2)}, u32[]{:S(2)}) %collective-permute-start.3) | collective-permute-done | bytes 106528 | tf_op jit(solution)/shard_map/ppermute | solution.py:629
  15.1 1.2 %collective-permute-done.7.refs_7_ = bf16[208,256]{1,0:T(8,128)(2,1)S(1)} collective-permute-done((bf16[208,256]{1,0:T(8,128)(2,1)S(1)}, bf16[208,256]{1,0:T(8,128)(2,1)S(1)}, u32[]{:S(2)}, u32[]{:S(2)}) %collective-permute-start.7) | collective-permute-done | bytes 106528 | tf_op jit(solution)/shard_map/ppermute | solution.py:629
  16.3 1.5 %compact.1.refs_0_ = bf16[720,256]{1,0:T(8,128)(2,1)S(1)} custom-call(s32[4]{0:T(128)S(1)} %pad_add_fusion.index_ref, bf16[208,256]{1,0:T(8,128)(2,1)S(1)} %get-tuple-element.262.refs_0_, bf16[208,256]{1,0:T(8,128)(2,1)S(1)} %collective-permute-done.1.refs_1_, bf16[208,256]{1,0:T(8,128)(2,1)S(1)} %collective-permute-done.2.refs_2_, ...), custom_call_target="tpu_custom_call" | custom-call | tf_op jit(solution)/shard_map/compact/pallas_call | solution.py:200
  17.8 1.1 %collective-permute-start.8 = (bf16[720,256]{1,0:T(8,128)(2,1)S(1)}, bf16[720,256]{1,0:T(8,128)(2,1)S(1)}, u32[]{:S(2)}, u32[]{:S(2)}) collective-permute-start(bf16[720,256]{1,0:T(8,128)(2,1)S(1)} %compact.1.refs_0_), channel_id=1, source_target_pairs={{0,32},{4,228},{8,40},{12,236},{16,48},{20,244},{24,56},{28,252},{... | collective-permute-start | bytes 1105928 | tf_op jit(solution)/shard_map/ppermute | solution.py:629
  18.9 4.0 %query.1.q_ref = bf16[192,512]{1,0:T(8,128)(2,1)S(1)} custom-call(bf16[192,4096]{1,0:T(8,128)(2,1)} %get-tuple-element.263.x_ref, f32[192,128]{1,0:T(8,128)} %get-tuple-element.264.scale_ref, bf16[4096,512]{1,0:T(8,128)(2,1)} %wq_hbm.1), custom_call_target="tpu_custom_call" | custom-call | flops 805306368 | bytes 5767168 | tf_op jit(solution)/shard_map/query/pallas_call | solution.py:150
  22.9 3.7 %collective-permute-done.8.refs_1_ = bf16[720,256]{1,0:T(8,128)(2,1)S(1)} collective-permute-done((bf16[720,256]{1,0:T(8,128)(2,1)S(1)}, bf16[720,256]{1,0:T(8,128)(2,1)S(1)}, u32[]{:S(2)}, u32[]{:S(2)}) %collective-permute-start.8) | collective-permute-done | bytes 368672 | tf_op jit(solution)/shard_map/ppermute | solution.py:629
  26.6 8.7 %collective-permute-done.9.refs_2_ = bf16[720,256]{1,0:T(8,128)(2,1)S(1)} collective-permute-done((bf16[720,256]{1,0:T(8,128)(2,1)S(1)}, bf16[720,256]{1,0:T(8,128)(2,1)S(1)}, u32[]{:S(2)}, u32[]{:S(2)}) %collective-permute-start.9) | collective-permute-done | bytes 368672 | tf_op jit(solution)/shard_map/ppermute | solution.py:629
  35.3 1.7 %collective-permute-done.12.refs_4_ = bf16[720,256]{1,0:T(8,128)(2,1)S(1)} collective-permute-done((bf16[720,256]{1,0:T(8,128)(2,1)S(1)}, bf16[720,256]{1,0:T(8,128)(2,1)S(1)}, u32[]{:S(2)}, u32[]{:S(2)}) %collective-permute-start.12) | collective-permute-done | bytes 368672 | tf_op jit(solution)/shard_map/ppermute | solution.py:629
  37.0 3.9 %attend_near.1 = (f32[2,384,128]{2,1,0:T(8,128)S(1)}, f32[2,384,128]{2,1,0:T(8,128)S(1)}, f32[2,384,128]{2,1,0:T(8,128)S(1)}, s32[2]{0:T(128)S(1)}) custom-call(s32[4]{0:T(128)S(1)} %pad_add_fusion.index_ref, bf16[192,512]{1,0:T(8,128)(2,1)S(1)} %query.1.q_ref, bf16[720,256]{1,0:T(8,128)(2,1)S(1)} %compact.1.refs_0_, ...), custom_call_target="tpu_custom_call" | custom-call | flops 3623878656 | bytes 8388608 | tf_op jit(solution)/shard_map/attend_near/pallas_call | solution.py:342
  40.9 3.1 %collective-permute-done.10.came = bf16[720,256]{1,0:T(8,128)(2,1)S(1)} collective-permute-done((bf16[720,256]{1,0:T(8,128)(2,1)S(1)}, bf16[720,256]{1,0:T(8,128)(2,1)S(1)}, u32[]{:S(2)}, u32[]{:S(2)}) %collective-permute-start.10) | collective-permute-done | bytes 368672 | tf_op jit(solution)/shard_map/ppermute | solution.py:629
  44.1 0.1 collective-permute-start.13
  44.1 1.6 %collective-permute-done.14.swapped = bf16[720,256]{1,0:T(8,128)(2,1)S(1)} collective-permute-done((bf16[720,256]{1,0:T(8,128)(2,1)S(1)}, bf16[720,256]{1,0:T(8,128)(2,1)S(1)}, u32[]{:S(2)}, u32[]{:S(2)}) %collective-permute-start.14) | collective-permute-done | bytes 368672 | tf_op jit(solution)/shard_map/ppermute | solution.py:629
  45.7 2.3 %attend_more.1 = (f32[2,384,128]{2,1,0:T(8,128)S(1)}, f32[2,384,128]{2,1,0:T(8,128)S(1)}, f32[2,384,128]{2,1,0:T(8,128)S(1)}, s32[2]{0:T(128)S(1)}) custom-call(s32[4]{0:T(128)S(1)} %pad_add_fusion.index_ref, s32[2]{0:T(128)S(1)} %get-tuple-element.272.info_ref, bf16[192,512]{1,0:T(8,128)(2,1)S(1)} %query.1.q_ref, ...), custom_call_target="tpu_custom_call" | custom-call | flops 1811939328 | bytes 8388608 | tf_op jit(solution)/shard_map/attend_more/pallas_call | solution.py:405
  48.0 2.9 %collective-permute-done.13.came = bf16[368,256]{1,0:T(8,128)(2,1)S(1)} collective-permute-done((bf16[368,256]{1,0:T(8,128)(2,1)S(1)}, bf16[368,256]{1,0:T(8,128)(2,1)S(1)}, u32[]{:S(2)}, u32[]{:S(2)}) %collective-permute-start.13) | collective-permute-done | bytes 188448 | tf_op jit(solution)/shard_map/ppermute | solution.py:629
  50.9 1.4 %collective-permute-done.15.swapped = bf16[368,256]{1,0:T(8,128)(2,1)S(1)} collective-permute-done((bf16[368,256]{1,0:T(8,128)(2,1)S(1)}, bf16[368,256]{1,0:T(8,128)(2,1)S(1)}, u32[]{:S(2)}, u32[]{:S(2)}) %collective-permute-start.15) | collective-permute-done | bytes 188448 | tf_op jit(solution)/shard_map/ppermute | solution.py:629
  52.4 3.0 %attend_far.1 = (bf16[192,256]{1,0:T(8,128)(2,1)S(1)}, bf16[192,256]{1,0:T(8,128)(2,1)S(1)}, bf16[192,256]{1,0:T(8,128)(2,1)S(1)}, bf16[192,256]{1,0:T(8,128)(2,1)S(1)}, s32[1]{0:T(128)}) custom-call(s32[4]{0:T(128)S(1)} %pad_add_fusion.index_ref, s32[2]{0:T(128)S(1)} %get-tuple-element.280.info_ref, bf16[192,512]{1,0:T(8,128)(2,1)S(1)} %query.1.q_ref, ...), custom_call_target="tpu_custom_call" | custom-call | tf_op jit(solution)/shard_map/attend_far/pallas_call | solution.py:467
  56.0 3.3 %collective-permute-start.16 = (bf16[192,256]{1,0:T(8,128)(2,1)S(1)}, bf16[192,256]{1,0:T(8,128)(2,1)S(1)}, u32[]{:S(2)}, u32[]{:S(2)}) collective-permute-start(bf16[192,256]{1,0:T(8,128)(2,1)S(1)} %get-tuple-element.291), channel_id=1, source_target_pairs={{0,2},{1,3},{2,0},{3,1},{4,6},{5,7},{6,4},{7,5},{8,10},{9,11},{10,... | collective-permute-start | bytes 294920 | tf_op jit(solution)/shard_map/ppermute | solution.py:665
  59.3 0.7 collective-permute-start.17
  60.0 2.6 %collective-permute-start.18 = (bf16[192,256]{1,0:T(8,128)(2,1)S(1)}, bf16[192,256]{1,0:T(8,128)(2,1)S(1)}, u32[]{:S(2)}, u32[]{:S(2)}) collective-permute-start(bf16[192,256]{1,0:T(8,128)(2,1)S(1)} %get-tuple-element.293), channel_id=1, source_target_pairs={{0,3},{1,0},{2,1},{3,2},{4,7},{5,4},{6,5},{7,6},{8,11},{9,8},{10,9... | collective-permute-start | bytes 294920 | tf_op jit(solution)/shard_map/ppermute | solution.py:665
  62.5 0.1 collective-permute-done.16.p1
  62.7 2.4 %collective-permute-done.17.p2 = bf16[192,256]{1,0:T(8,128)(2,1)S(1)} collective-permute-done((bf16[192,256]{1,0:T(8,128)(2,1)S(1)}, bf16[192,256]{1,0:T(8,128)(2,1)S(1)}, u32[]{:S(2)}, u32[]{:S(2)}) %collective-permute-start.17) | collective-permute-done | bytes 98336 | tf_op jit(solution)/shard_map/ppermute | solution.py:665
  65.1 0.3 mix.1
  65.5 2.1 %collective-permute-start.19 = (bf16[32,256]{1,0:T(8,128)(2,1)S(1)}, bf16[32,256]{1,0:T(8,128)(2,1)S(1)}, u32[]{:S(2)}, u32[]{:S(2)}) collective-permute-start(bf16[32,256]{1,0:T(8,128)(2,1)S(1)} %get-tuple-element.295), channel_id=1, source_target_pairs={{0,4},{4,8},{8,12},{12,16},{16,20},{20,24},{24,28},{28,32},{32,36}... | collective-permute-start | bytes 49160 | tf_op jit(solution)/shard_map/ppermute | solution.py:668
  67.6 2.9 %convolve.1.given_hbm = bf16[512,256]{1,0:T(8,128)(2,1)} custom-call(bf16[512,256]{1,0:T(8,128)(2,1)S(1)} %get-tuple-element.294.mixed_ref, f32[31,256]{1,0:T(8,128)S(1)} %copy-done.1), custom_call_target="tpu_custom_call" | custom-call | flops 8126464 | bytes 2097152 | tf_op jit(solution)/shard_map/convolve/pallas_call | solution.py:594
  70.5 3.4 %collective-permute-done.19.rim_ref = bf16[32,256]{1,0:T(8,128)(2,1)S(1)} collective-permute-done((bf16[32,256]{1,0:T(8,128)(2,1)S(1)}, bf16[32,256]{1,0:T(8,128)(2,1)S(1)}, u32[]{:S(2)}, u32[]{:S(2)}) %collective-permute-start.19) | collective-permute-done | bytes 16416 | tf_op jit(solution)/shard_map/ppermute | solution.py:668
  73.9 0.8 %first_rows.1 = bf16[512,256]{1,0:T(8,128)(2,1)} custom-call(bf16[512,256]{1,0:T(8,128)(2,1)} %convolve.1.given_hbm, bf16[32,256]{1,0:T(8,128)(2,1)S(1)} %collective-permute-done.19.rim_ref, bf16[512,256]{1,0:T(8,128)(2,1)S(1)} %get-tuple-element.294.mixed_ref, f32[31,256]{1,0:T(8,128)S(1)} %copy-done.1), custom_call_target="tpu_custom_call", output_to_operand_aliasing={{}: (0, {})} | custom-call | tf_op jit(solution)/shard_map/first_rows/pallas_call | solution.py:609
  (26 shorter events, 0.2 us)
Async XLA Ops:
  5.5 6.0 %collective-permute-start.1 = (bf16[208,256]{1,0:T(8,128)(2,1)S(1)}, bf16[208,256]{1,0:T(8,128)(2,1)S(1)}, u32[]{:S(2)}, u32[]{:S(2)}) collective-permute-start(bf16[208,256]{1,0:T(8,128)(2,1)S(1)} %get-tuple-element.262.refs_0_), channel_id=1, source_target_pairs={{0,8},{4,12},{8,16},{12,20},{16,24},{20,28},{24,0},{28,4},{32,40},... | collective-permute-start | bytes 319496 | tf_op jit(solution)/shard_map/ppermute | solution.py:629
  7.0 6.3 %collective-permute-start.2 = (bf16[208,256]{1,0:T(8,128)(2,1)S(1)}, bf16[208,256]{1,0:T(8,128)(2,1)S(1)}, u32[]{:S(2)}, u32[]{:S(2)}) collective-permute-start(bf16[208,256]{1,0:T(8,128)(2,1)S(1)} %get-tuple-element.262.refs_0_), channel_id=1, source_target_pairs={{0,24},{4,28},{8,0},{12,4},{16,8},{20,12},{24,16},{28,20},{32,56},... | collective-permute-start | bytes 319496 | tf_op jit(solution)/shard_map/ppermute | solution.py:629
  8.8 6.2 %collective-permute-start.3 = (bf16[208,256]{1,0:T(8,128)(2,1)S(1)}, bf16[208,256]{1,0:T(8,128)(2,1)S(1)}, u32[]{:S(2)}, u32[]{:S(2)}) collective-permute-start(bf16[208,256]{1,0:T(8,128)(2,1)S(1)} %get-tuple-element.262.refs_0_), channel_id=1, source_target_pairs={{0,16},{4,20},{8,24},{12,28},{16,0},{20,4},{24,8},{28,12},{32,48},... | collective-permute-start | bytes 319496 | tf_op jit(solution)/shard_map/ppermute | solution.py:629
  10.6 4.5 %collective-permute-start.4 = (bf16[208,256]{1,0:T(8,128)(2,1)S(1)}, bf16[208,256]{1,0:T(8,128)(2,1)S(1)}, u32[]{:S(2)}, u32[]{:S(2)}) collective-permute-start(bf16[208,256]{1,0:T(8,128)(2,1)S(1)} %get-tuple-element.262.refs_0_), channel_id=1, source_target_pairs={{0,4},{4,0},{8,12},{12,8},{16,20},{20,16},{24,28},{28,24},{32,36},... | collective-permute-start | bytes 319496 | tf_op jit(solution)/shard_map/ppermute | solution.py:629
  11.5 3.6 %collective-permute-start.5 = (bf16[208,256]{1,0:T(8,128)(2,1)S(1)}, bf16[208,256]{1,0:T(8,128)(2,1)S(1)}, u32[]{:S(2)}, u32[]{:S(2)}) collective-permute-start(bf16[208,256]{1,0:T(8,128)(2,1)S(1)} %collective-permute-done.1.refs_1_), channel_id=1, source_target_pairs={{0,4},{4,0},{8,12},{12,8},{16,20},{20,16},{24,28},{28,24},{32,36},... | collective-permute-start | bytes 319496 | tf_op jit(solution)/shard_map/ppermute | solution.py:629
  13.3 1.8 %collective-permute-start.6 = (bf16[208,256]{1,0:T(8,128)(2,1)S(1)}, bf16[208,256]{1,0:T(8,128)(2,1)S(1)}, u32[]{:S(2)}, u32[]{:S(2)}) collective-permute-start(bf16[208,256]{1,0:T(8,128)(2,1)S(1)} %collective-permute-done.2.refs_2_), channel_id=1, source_target_pairs={{0,4},{4,0},{8,12},{12,8},{16,20},{20,16},{24,28},{28,24},{32,36},... | collective-permute-start | bytes 319496 | tf_op jit(solution)/shard_map/ppermute | solution.py:629
  15.0 1.3 %collective-permute-start.7 = (bf16[208,256]{1,0:T(8,128)(2,1)S(1)}, bf16[208,256]{1,0:T(8,128)(2,1)S(1)}, u32[]{:S(2)}, u32[]{:S(2)}) collective-permute-start(bf16[208,256]{1,0:T(8,128)(2,1)S(1)} %collective-permute-done.3.refs_3_), channel_id=1, source_target_pairs={{0,4},{4,0},{8,12},{12,8},{16,20},{20,16},{24,28},{28,24},{32,36},... | collective-permute-start | bytes 319496 | tf_op jit(solution)/shard_map/ppermute | solution.py:629
  17.8 8.8 %collective-permute-start.8 = (bf16[720,256]{1,0:T(8,128)(2,1)S(1)}, bf16[720,256]{1,0:T(8,128)(2,1)S(1)}, u32[]{:S(2)}, u32[]{:S(2)}) collective-permute-start(bf16[720,256]{1,0:T(8,128)(2,1)S(1)} %compact.1.refs_0_), channel_id=1, source_target_pairs={{0,32},{4,228},{8,40},{12,236},{16,48},{20,244},{24,56},{28,252},{... | collective-permute-start | bytes 1105928 | tf_op jit(solution)/shard_map/ppermute | solution.py:629
  26.6 8.7 %collective-permute-start.9 = (bf16[720,256]{1,0:T(8,128)(2,1)S(1)}, bf16[720,256]{1,0:T(8,128)(2,1)S(1)}, u32[]{:S(2)}, u32[]{:S(2)}) collective-permute-start(bf16[720,256]{1,0:T(8,128)(2,1)S(1)} %collective-permute-done.8.refs_1_), channel_id=1, source_target_pairs={{0,32},{4,228},{8,40},{12,236},{16,48},{20,244},{24,56},{28,252},{... | collective-permute-start | bytes 1105928 | tf_op jit(solution)/shard_map/ppermute | solution.py:629
  26.6 8.7 %collective-permute-start.11 = (bf16[720,256]{1,0:T(8,128)(2,1)S(1)}, bf16[720,256]{1,0:T(8,128)(2,1)S(1)}, u32[]{:S(2)}, u32[]{:S(2)}) collective-permute-start(bf16[720,256]{1,0:T(8,128)(2,1)S(1)} %collective-permute-done.8.refs_1_), channel_id=1, source_target_pairs={{0,4},{4,0},{8,12},{12,8},{16,20},{20,16},{24,28},{28,24},{32,36},... | collective-permute-start | bytes 1105928 | tf_op jit(solution)/shard_map/ppermute | solution.py:629
  35.3 1.7 %collective-permute-start.12 = (bf16[720,256]{1,0:T(8,128)(2,1)S(1)}, bf16[720,256]{1,0:T(8,128)(2,1)S(1)}, u32[]{:S(2)}, u32[]{:S(2)}) collective-permute-start(bf16[720,256]{1,0:T(8,128)(2,1)S(1)} %collective-permute-done.9.refs_2_), channel_id=1, source_target_pairs={{0,4},{4,0},{8,12},{12,8},{16,20},{20,16},{24,28},{28,24},{32,36},... | collective-permute-start | bytes 1105928 | tf_op jit(solution)/shard_map/ppermute | solution.py:629
  35.3 8.7 %collective-permute-start.10 = (bf16[720,256]{1,0:T(8,128)(2,1)S(1)}, bf16[720,256]{1,0:T(8,128)(2,1)S(1)}, u32[]{:S(2)}, u32[]{:S(2)}) collective-permute-start(bf16[720,256]{1,0:T(8,128)(2,1)S(1)} %collective-permute-done.9.refs_2_), channel_id=1, source_target_pairs={{0,32},{4,228},{8,40},{12,236},{16,48},{20,244},{24,56},{28,252},{... | collective-permute-start | bytes 1105928 | tf_op jit(solution)/shard_map/ppermute | solution.py:629
  40.9 11.4 %copy-start.3 = (bf16[512,1024]{1,0:T(8,128)(2,1)S(1)}, bf16[512,1024]{1,0:T(8,128)(2,1)}, u32[]{:S(2)}) copy-start(bf16[512,1024]{1,0:T(8,128)(2,1)} %wout_ref.1) | copy-start | bytes 3145732
  44.0 1.7 %collective-permute-start.14 = (bf16[720,256]{1,0:T(8,128)(2,1)S(1)}, bf16[720,256]{1,0:T(8,128)(2,1)S(1)}, u32[]{:S(2)}, u32[]{:S(2)}) collective-permute-start(bf16[720,256]{1,0:T(8,128)(2,1)S(1)} %collective-permute-done.10.came), channel_id=1, source_target_pairs={{0,4},{4,0},{8,12},{12,8},{16,20},{20,16},{24,28},{28,24},{32,36},... | collective-permute-start | bytes 1105928 | tf_op jit(solution)/shard_map/ppermute | solution.py:629
  44.1 6.9 %collective-permute-start.13 = (bf16[368,256]{1,0:T(8,128)(2,1)S(1)}, bf16[368,256]{1,0:T(8,128)(2,1)S(1)}, u32[]{:S(2)}, u32[]{:S(2)}) collective-permute-start(bf16[368,256]{1,0:T(8,128)(2,1)S(1)} %constant_dynamic-slice_fusion.4), channel_id=1, source_target_pairs={{0,32},{4,228},{8,40},{12,236},{16,48},{20,244},{24,56},{28,252},{... | collective-permute-start | bytes 565256 | tf_op jit(solution)/shard_map/ppermute | solution.py:629
  50.9 1.4 %collective-permute-start.15 = (bf16[368,256]{1,0:T(8,128)(2,1)S(1)}, bf16[368,256]{1,0:T(8,128)(2,1)S(1)}, u32[]{:S(2)}, u32[]{:S(2)}) collective-permute-start(bf16[368,256]{1,0:T(8,128)(2,1)S(1)} %collective-permute-done.13.came), channel_id=1, source_target_pairs={{0,4},{4,0},{8,12},{12,8},{16,20},{20,16},{24,28},{28,24},{32,36},... | collective-permute-start | bytes 565256 | tf_op jit(solution)/shard_map/ppermute | solution.py:629
  56.0 9.2 %copy-start = (bf16[512,256]{1,0:T(8,128)(2,1)S(1)}, bf16[512,256]{1,0:T(8,128)(2,1)}, u32[]{:S(2)}) copy-start(bf16[512,256]{1,0:T(8,128)(2,1)} %skip_ref.1) | copy-start | bytes 786436
  56.0 9.2 %copy-start.2 = (s32[1,192]{1,0:T(1,128)S(1)}, s32[1,192]{1,0:T(1,128)}, u32[]{:S(2)}) copy-start(s32[1,192]{1,0:T(1,128)} %len_ref.1) | copy-start | bytes 2308
  56.0 11.6 %copy-start.1 = (f32[31,256]{1,0:T(8,128)S(1)}, f32[31,256]{1,0:T(8,128)}, u32[]{:S(2)}) copy-start(f32[31,256]{1,0:T(8,128)} %taps_ref.3) | copy-start | bytes 95236
  56.0 6.7 %collective-permute-start.16 = (bf16[192,256]{1,0:T(8,128)(2,1)S(1)}, bf16[192,256]{1,0:T(8,128)(2,1)S(1)}, u32[]{:S(2)}, u32[]{:S(2)}) collective-permute-start(bf16[192,256]{1,0:T(8,128)(2,1)S(1)} %get-tuple-element.291), channel_id=1, source_target_pairs={{0,2},{1,3},{2,0},{3,1},{4,6},{5,7},{6,4},{7,5},{8,10},{9,11},{10,... | collective-permute-start | bytes 294920 | tf_op jit(solution)/shard_map/ppermute | solution.py:665
  59.3 5.8 %collective-permute-start.17 = (bf16[192,256]{1,0:T(8,128)(2,1)S(1)}, bf16[192,256]{1,0:T(8,128)(2,1)S(1)}, u32[]{:S(2)}, u32[]{:S(2)}) collective-permute-start(bf16[192,256]{1,0:T(8,128)(2,1)S(1)} %get-tuple-element.292), channel_id=1, source_target_pairs={{0,1},{1,2},{2,3},{3,0},{4,5},{5,6},{6,7},{7,4},{8,9},{9,10},{10,1... | collective-permute-start | bytes 294920 | tf_op jit(solution)/shard_map/ppermute | solution.py:665
  60.0 5.2 %collective-permute-start.18 = (bf16[192,256]{1,0:T(8,128)(2,1)S(1)}, bf16[192,256]{1,0:T(8,128)(2,1)S(1)}, u32[]{:S(2)}, u32[]{:S(2)}) collective-permute-start(bf16[192,256]{1,0:T(8,128)(2,1)S(1)} %get-tuple-element.293), channel_id=1, source_target_pairs={{0,3},{1,0},{2,1},{3,2},{4,7},{5,4},{6,5},{7,6},{8,11},{9,8},{10,9... | collective-permute-start | bytes 294920 | tf_op jit(solution)/shard_map/ppermute | solution.py:665
  65.5 8.4 %collective-permute-start.19 = (bf16[32,256]{1,0:T(8,128)(2,1)S(1)}, bf16[32,256]{1,0:T(8,128)(2,1)S(1)}, u32[]{:S(2)}, u32[]{:S(2)}) collective-permute-start(bf16[32,256]{1,0:T(8,128)(2,1)S(1)} %get-tuple-element.295), channel_id=1, source_target_pairs={{0,4},{4,8},{8,12},{12,16},{16,20},{20,24},{24,28},{28,32},{32,36}... | collective-permute-start | bytes 49160 | tf_op jit(solution)/shard_map/ppermute | solution.py:668

commit v5 on v3

--- a/solution.py
+++ b/solution.py
@@ -187,12 +187,12 @@
     for i in range(8):
         table += jnp.where(sub == order[i], counts[i], 0.0)
     out_ref[HALF:UPPER, :] = table.astype(BF)
+    target = jnp.concatenate(targets, axis=1)
+    rows = jnp.concatenate([ref[:CAP, :] for ref in blocks], axis=0)
     for half in range(2):
-        row = (iota((HALF, CAP), 0) + half * HALF).astype(F32)
-        total = jnp.zeros((HALF, 2 * HD), F32)
-        for i in range(8):
-            hot = jnp.where(row == targets[i], 1.0, 0.0).astype(BF)
-            total += jnp.dot(hot, blocks[i][:CAP, :], preferred_element_type=F32)
+        row = (iota((HALF, 8 * CAP), 0) + half * HALF).astype(F32)
+        hot = jnp.where(row == target, 1.0, 0.0).astype(BF)
+        total = jnp.dot(hot, rows, preferred_element_type=F32)
         out_ref[half * UPPER : half * UPPER + HALF, :] = total.astype(BF)
 
 

time: 74.5 us -> 74.1 us (level)
  transfers between devices with their start and end apart: 19 -> 19, of which waited for: 14 -> 14; matrix products, arithmetic and copies ran while one was open for 0% -> 0% of each run, Pallas kernels for 18% -> 19%
where the time goes in v5:
time: 74.1 us; the launch traced here: 73.4 us
  waiting for transfers between devices  34.2 us (46%)
  Pallas kernels  23.3 us (31%)
  starting transfers between devices  14.8 us (20%)
  between operations  0.97 us (1%)
    ppermute x15, waiting for transfers between devices, seq_permute(): return lax.ppermute(value, 'seq', pairs)  28 us
    ppermute x3, starting transfers between devices, per_device(): lax.ppermute(parts[k], 'section', [(i, (i + k) % 4) for i in range(4)])  6.51 us
    ppermute x15, starting transfers between devices, seq_permute(): return lax.ppermute(value, 'seq', pairs)  6.33 us
    pallas_call x1, Pallas kernels, pool(): pl.pallas_call(pool_kernel, in_specs=[anywhere()] * 5, out_specs=[vmem()]...  4.71 us
    pallas_call x1, Pallas kernels, query(): pl.pallas_call(query_kernel, in_specs=[vmem(), vmem(), anywhere()], out_s...  4.09 us
    pallas_call x1, Pallas kernels, attend_near(): pl.pallas_call(attend_near_kernel, in_specs=[pl.BlockSpec(memory_space=pl...  3.91 us
    ppermute x1, waiting for transfers between devices, per_device(): lax.ppermute(tail, 'seq', [(i, i + 1) for i in range(2 * NX * NZ - 1)])  3.58 us
    pallas_call x1, Pallas kernels, attend_more(): pl.pallas_call(attend_more_kernel, in_specs=[pl.BlockSpec(memory_space=pl...  2.89 us
  transfers between devices with their start and end apart: 19, of which 14 were waited for; matrix products, arithmetic and copies ran while one was open for 0% of the time, Pallas kernels for 19%

profile of v5, /device:TPU:128, one launch (start us, length us, event | category | flops | bytes accessed | tf_op | source)
XLA Modules:
  0.0 73.4 jit_solution(7155418057466277688)
XLA Ops:
  0.0 4.7 %pool.1 = (bf16[208,256]{1,0:T(8,128)(2,1)S(1)}, bf16[192,4096]{1,0:T(8,128)(2,1)}, f32[192,128]{1,0:T(8,128)}) custom-call(s32[1,192]{1,0:T(1,128)} %len_ref.1, f32[1,4096]{1,0:T(1,128)} %bitcast.38, bf16[512,4096]{1,0:T(8,128)(2,1)} %enc_hbm.1, bf16[4096,128]{1,0:T(8,128)(2,1)} %wk_hbm.1, bf16[4096,128]{1,0:T(8,128)(2,1)} %wv_hbm.1), custom_call_target="tpu_custom_call" | custom-call | flops 1207959552 | bytes 7864320 | tf_op jit(solution)/shard_map/pool/pallas_call | solution.py:106
  4.7 1.6 %collective-permute-start.1 = (bf16[208,256]{1,0:T(8,128)(2,1)S(1)}, bf16[208,256]{1,0:T(8,128)(2,1)S(1)}, u32[]{:S(2)}, u32[]{:S(2)}) collective-permute-start(bf16[208,256]{1,0:T(8,128)(2,1)S(1)} %get-tuple-element.262.refs_0_), channel_id=1, source_target_pairs={{0,8},{4,12},{8,16},{12,20},{16,24},{20,28},{24,0},{28,4},{32,40},... | collective-permute-start | bytes 319496 | tf_op jit(solution)/shard_map/ppermute | solution.py:629
  6.3 1.7 %collective-permute-start.2 = (bf16[208,256]{1,0:T(8,128)(2,1)S(1)}, bf16[208,256]{1,0:T(8,128)(2,1)S(1)}, u32[]{:S(2)}, u32[]{:S(2)}) collective-permute-start(bf16[208,256]{1,0:T(8,128)(2,1)S(1)} %get-tuple-element.262.refs_0_), channel_id=1, source_target_pairs={{0,24},{4,28},{8,0},{12,4},{16,8},{20,12},{24,16},{28,20},{32,56},... | collective-permute-start | bytes 319496 | tf_op jit(solution)/shard_map/ppermute | solution.py:629
  8.0 1.8 %collective-permute-start.3 = (bf16[208,256]{1,0:T(8,128)(2,1)S(1)}, bf16[208,256]{1,0:T(8,128)(2,1)S(1)}, u32[]{:S(2)}, u32[]{:S(2)}) collective-permute-start(bf16[208,256]{1,0:T(8,128)(2,1)S(1)} %get-tuple-element.262.refs_0_), channel_id=1, source_target_pairs={{0,16},{4,20},{8,24},{12,28},{16,0},{20,4},{24,8},{28,12},{32,48},... | collective-permute-start | bytes 319496 | tf_op jit(solution)/shard_map/ppermute | solution.py:629
  9.8 0.9 %collective-permute-done.1.refs_1_ = bf16[208,256]{1,0:T(8,128)(2,1)S(1)} collective-permute-done((bf16[208,256]{1,0:T(8,128)(2,1)S(1)}, bf16[208,256]{1,0:T(8,128)(2,1)S(1)}, u32[]{:S(2)}, u32[]{:S(2)}) %collective-permute-start.1) | collective-permute-done | bytes 106528 | tf_op jit(solution)/shard_map/ppermute | solution.py:629
  10.7 1.9 %collective-permute-done.2.refs_2_ = bf16[208,256]{1,0:T(8,128)(2,1)S(1)} collective-permute-done((bf16[208,256]{1,0:T(8,128)(2,1)S(1)}, bf16[208,256]{1,0:T(8,128)(2,1)S(1)}, u32[]{:S(2)}, u32[]{:S(2)}) %collective-permute-start.2) | collective-permute-done | bytes 106528 | tf_op jit(solution)/shard_map/ppermute | solution.py:629
  12.6 1.7 %collective-permute-done.3.refs_3_ = bf16[208,256]{1,0:T(8,128)(2,1)S(1)} collective-permute-done((bf16[208,256]{1,0:T(8,128)(2,1)S(1)}, bf16[208,256]{1,0:T(8,128)(2,1)S(1)}, u32[]{:S(2)}, u32[]{:S(2)}) %collective-permute-start.3) | collective-permute-done | bytes 106528 | tf_op jit(solution)/shard_map/ppermute | solution.py:629
  14.3 1.2 %collective-permute-done.7.refs_7_ = bf16[208,256]{1,0:T(8,128)(2,1)S(1)} collective-permute-done((bf16[208,256]{1,0:T(8,128)(2,1)S(1)}, bf16[208,256]{1,0:T(8,128)(2,1)S(1)}, u32[]{:S(2)}, u32[]{:S(2)}) %collective-permute-start.7) | collective-permute-done | bytes 106528 | tf_op jit(solution)/shard_map/ppermute | solution.py:629
  15.6 1.3 %compact.1.refs_0_ = bf16[720,256]{1,0:T(8,128)(2,1)S(1)} custom-call(s32[4]{0:T(128)S(1)} %pad_add_fusion.index_ref, bf16[208,256]{1,0:T(8,128)(2,1)S(1)} %get-tuple-element.262.refs_0_, bf16[208,256]{1,0:T(8,128)(2,1)S(1)} %collective-permute-done.1.refs_1_, bf16[208,256]{1,0:T(8,128)(2,1)S(1)} %collective-permute-done.2.refs_2_, ...), custom_call_target="tpu_custom_call" | custom-call | tf_op jit(solution)/shard_map/compact/pallas_call | solution.py:200
  16.9 1.1 %collective-permute-start.8 = (bf16[720,256]{1,0:T(8,128)(2,1)S(1)}, bf16[720,256]{1,0:T(8,128)(2,1)S(1)}, u32[]{:S(2)}, u32[]{:S(2)}) collective-permute-start(bf16[720,256]{1,0:T(8,128)(2,1)S(1)} %compact.1.refs_0_), channel_id=1, source_target_pairs={{0,32},{4,228},{8,40},{12,236},{16,48},{20,244},{24,56},{28,252},{... | collective-permute-start | bytes 1105928 | tf_op jit(solution)/shard_map/ppermute | solution.py:629
  18.0 4.1 %query.1.q_ref = bf16[192,512]{1,0:T(8,128)(2,1)S(1)} custom-call(bf16[192,4096]{1,0:T(8,128)(2,1)} %get-tuple-element.263.x_ref, f32[192,128]{1,0:T(8,128)} %get-tuple-element.264.scale_ref, bf16[4096,512]{1,0:T(8,128)(2,1)} %wq_hbm.1), custom_call_target="tpu_custom_call" | custom-call | flops 805306368 | bytes 5767168 | tf_op jit(solution)/shard_map/query/pallas_call | solution.py:150
  22.1 3.6 %collective-permute-done.8.refs_1_ = bf16[720,256]{1,0:T(8,128)(2,1)S(1)} collective-permute-done((bf16[720,256]{1,0:T(8,128)(2,1)S(1)}, bf16[720,256]{1,0:T(8,128)(2,1)S(1)}, u32[]{:S(2)}, u32[]{:S(2)}) %collective-permute-start.8) | collective-permute-done | bytes 368672 | tf_op jit(solution)/shard_map/ppermute | solution.py:629
  25.7 8.7 %collective-permute-done.9.refs_2_ = bf16[720,256]{1,0:T(8,128)(2,1)S(1)} collective-permute-done((bf16[720,256]{1,0:T(8,128)(2,1)S(1)}, bf16[720,256]{1,0:T(8,128)(2,1)S(1)}, u32[]{:S(2)}, u32[]{:S(2)}) %collective-permute-start.9) | collective-permute-done | bytes 368672 | tf_op jit(solution)/shard_map/ppermute | solution.py:629
  34.4 1.7 %collective-permute-done.12.refs_4_ = bf16[720,256]{1,0:T(8,128)(2,1)S(1)} collective-permute-done((bf16[720,256]{1,0:T(8,128)(2,1)S(1)}, bf16[720,256]{1,0:T(8,128)(2,1)S(1)}, u32[]{:S(2)}, u32[]{:S(2)}) %collective-permute-start.12) | collective-permute-done | bytes 368672 | tf_op jit(solution)/shard_map/ppermute | solution.py:629
  36.1 3.9 %attend_near.1 = (f32[2,384,128]{2,1,0:T(8,128)S(1)}, f32[2,384,128]{2,1,0:T(8,128)S(1)}, f32[2,384,128]{2,1,0:T(8,128)S(1)}, s32[2]{0:T(128)S(1)}) custom-call(s32[4]{0:T(128)S(1)} %pad_add_fusion.index_ref, bf16[192,512]{1,0:T(8,128)(2,1)S(1)} %query.1.q_ref, bf16[720,256]{1,0:T(8,128)(2,1)S(1)} %compact.1.refs_0_, ...), custom_call_target="tpu_custom_call" | custom-call | flops 3623878656 | bytes 8388608 | tf_op jit(solution)/shard_map/attend_near/pallas_call | solution.py:342
  40.0 3.1 %collective-permute-done.10.came = bf16[720,256]{1,0:T(8,128)(2,1)S(1)} collective-permute-done((bf16[720,256]{1,0:T(8,128)(2,1)S(1)}, bf16[720,256]{1,0:T(8,128)(2,1)S(1)}, u32[]{:S(2)}, u32[]{:S(2)}) %collective-permute-start.10) | collective-permute-done | bytes 368672 | tf_op jit(solution)/shard_map/ppermute | solution.py:629
  43.2 0.1 collective-permute-start.13
  43.3 1.6 %collective-permute-done.14.swapped = bf16[720,256]{1,0:T(8,128)(2,1)S(1)} collective-permute-done((bf16[720,256]{1,0:T(8,128)(2,1)S(1)}, bf16[720,256]{1,0:T(8,128)(2,1)S(1)}, u32[]{:S(2)}, u32[]{:S(2)}) %collective-permute-start.14) | collective-permute-done | bytes 368672 | tf_op jit(solution)/shard_map/ppermute | solution.py:629
  44.8 2.9 %attend_more.1 = (f32[2,384,128]{2,1,0:T(8,128)S(1)}, f32[2,384,128]{2,1,0:T(8,128)S(1)}, f32[2,384,128]{2,1,0:T(8,128)S(1)}, s32[2]{0:T(128)S(1)}) custom-call(s32[4]{0:T(128)S(1)} %pad_add_fusion.index_ref, s32[2]{0:T(128)S(1)} %get-tuple-element.272.info_ref, bf16[192,512]{1,0:T(8,128)(2,1)S(1)} %query.1.q_ref, ...), custom_call_target="tpu_custom_call" | custom-call | flops 1811939328 | bytes 8388608 | tf_op jit(solution)/shard_map/attend_more/pallas_call | solution.py:405
  47.7 2.3 %collective-permute-done.13.came = bf16[368,256]{1,0:T(8,128)(2,1)S(1)} collective-permute-done((bf16[368,256]{1,0:T(8,128)(2,1)S(1)}, bf16[368,256]{1,0:T(8,128)(2,1)S(1)}, u32[]{:S(2)}, u32[]{:S(2)}) %collective-permute-start.13) | collective-permute-done | bytes 188448 | tf_op jit(solution)/shard_map/ppermute | solution.py:629
  50.1 1.4 %collective-permute-done.15.swapped = bf16[368,256]{1,0:T(8,128)(2,1)S(1)} collective-permute-done((bf16[368,256]{1,0:T(8,128)(2,1)S(1)}, bf16[368,256]{1,0:T(8,128)(2,1)S(1)}, u32[]{:S(2)}, u32[]{:S(2)}) %collective-permute-start.15) | collective-permute-done | bytes 188448 | tf_op jit(solution)/shard_map/ppermute | solution.py:629
  51.5 2.4 %attend_far.1 = (bf16[192,256]{1,0:T(8,128)(2,1)S(1)}, bf16[192,256]{1,0:T(8,128)(2,1)S(1)}, bf16[192,256]{1,0:T(8,128)(2,1)S(1)}, bf16[192,256]{1,0:T(8,128)(2,1)S(1)}, s32[1]{0:T(128)}) custom-call(s32[4]{0:T(128)S(1)} %pad_add_fusion.index_ref, s32[2]{0:T(128)S(1)} %get-tuple-element.280.info_ref, bf16[192,512]{1,0:T(8,128)(2,1)S(1)} %query.1.q_ref, ...), custom_call_target="tpu_custom_call" | custom-call | tf_op jit(solution)/shard_map/attend_far/pallas_call | solution.py:467
  54.6 3.3 %collective-permute-start.16 = (bf16[192,256]{1,0:T(8,128)(2,1)S(1)}, bf16[192,256]{1,0:T(8,128)(2,1)S(1)}, u32[]{:S(2)}, u32[]{:S(2)}) collective-permute-start(bf16[192,256]{1,0:T(8,128)(2,1)S(1)} %get-tuple-element.291), channel_id=1, source_target_pairs={{0,2},{1,3},{2,0},{3,1},{4,6},{5,7},{6,4},{7,5},{8,10},{9,11},{10,... | collective-permute-start | bytes 294920 | tf_op jit(solution)/shard_map/ppermute | solution.py:665
  57.8 0.7 collective-permute-start.17
  58.5 2.6 %collective-permute-start.18 = (bf16[192,256]{1,0:T(8,128)(2,1)S(1)}, bf16[192,256]{1,0:T(8,128)(2,1)S(1)}, u32[]{:S(2)}, u32[]{:S(2)}) collective-permute-start(bf16[192,256]{1,0:T(8,128)(2,1)S(1)} %get-tuple-element.293), channel_id=1, source_target_pairs={{0,3},{1,0},{2,1},{3,2},{4,7},{5,4},{6,5},{7,6},{8,11},{9,8},{10,9... | collective-permute-start | bytes 294920 | tf_op jit(solution)/shard_map/ppermute | solution.py:665
  61.1 0.2 collective-permute-done.16.p1
  61.2 2.4 %collective-permute-done.17.p2 = bf16[192,256]{1,0:T(8,128)(2,1)S(1)} collective-permute-done((bf16[192,256]{1,0:T(8,128)(2,1)S(1)}, bf16[192,256]{1,0:T(8,128)(2,1)S(1)}, u32[]{:S(2)}, u32[]{:S(2)}) %collective-permute-start.17) | collective-permute-done | bytes 98336 | tf_op jit(solution)/shard_map/ppermute | solution.py:665
  63.7 0.3 mix.1
  64.0 1.9 %collective-permute-start.19 = (bf16[32,256]{1,0:T(8,128)(2,1)S(1)}, bf16[32,256]{1,0:T(8,128)(2,1)S(1)}, u32[]{:S(2)}, u32[]{:S(2)}) collective-permute-start(bf16[32,256]{1,0:T(8,128)(2,1)S(1)} %get-tuple-element.295), channel_id=1, source_target_pairs={{0,4},{4,8},{8,12},{12,16},{16,20},{20,24},{24,28},{28,32},{32,36}... | collective-permute-start | bytes 49160 | tf_op jit(solution)/shard_map/ppermute | solution.py:668
  66.0 2.9 %convolve.1.given_hbm = bf16[512,256]{1,0:T(8,128)(2,1)} custom-call(bf16[512,256]{1,0:T(8,128)(2,1)S(1)} %get-tuple-element.294.mixed_ref, f32[31,256]{1,0:T(8,128)S(1)} %copy-done.1), custom_call_target="tpu_custom_call" | custom-call | flops 8126464 | bytes 2097152 | tf_op jit(solution)/shard_map/convolve/pallas_call | solution.py:594
  68.8 3.6 %collective-permute-done.19.rim_ref = bf16[32,256]{1,0:T(8,128)(2,1)S(1)} collective-permute-done((bf16[32,256]{1,0:T(8,128)(2,1)S(1)}, bf16[32,256]{1,0:T(8,128)(2,1)S(1)}, u32[]{:S(2)}, u32[]{:S(2)}) %collective-permute-start.19) | collective-permute-done | bytes 16416 | tf_op jit(solution)/shard_map/ppermute | solution.py:668
  72.4 0.8 %first_rows.1 = bf16[512,256]{1,0:T(8,128)(2,1)} custom-call(bf16[512,256]{1,0:T(8,128)(2,1)} %convolve.1.given_hbm, bf16[32,256]{1,0:T(8,128)(2,1)S(1)} %collective-permute-done.19.rim_ref, bf16[512,256]{1,0:T(8,128)(2,1)S(1)} %get-tuple-element.294.mixed_ref, f32[31,256]{1,0:T(8,128)S(1)} %copy-done.1), custom_call_target="tpu_custom_call", output_to_operand_aliasing={{}: (0, {})} | custom-call | tf_op jit(solution)/shard_map/first_rows/pallas_call | solution.py:609
  (26 shorter events, 0.2 us)
Async XLA Ops:
  4.7 6.0 %collective-permute-start.1 = (bf16[208,256]{1,0:T(8,128)(2,1)S(1)}, bf16[208,256]{1,0:T(8,128)(2,1)S(1)}, u32[]{:S(2)}, u32[]{:S(2)}) collective-permute-start(bf16[208,256]{1,0:T(8,128)(2,1)S(1)} %get-tuple-element.262.refs_0_), channel_id=1, source_target_pairs={{0,8},{4,12},{8,16},{12,20},{16,24},{20,28},{24,0},{28,4},{32,40},... | collective-permute-start | bytes 319496 | tf_op jit(solution)/shard_map/ppermute | solution.py:629
  6.3 6.3 %collective-permute-start.2 = (bf16[208,256]{1,0:T(8,128)(2,1)S(1)}, bf16[208,256]{1,0:T(8,128)(2,1)S(1)}, u32[]{:S(2)}, u32[]{:S(2)}) collective-permute-start(bf16[208,256]{1,0:T(8,128)(2,1)S(1)} %get-tuple-element.262.refs_0_), channel_id=1, source_target_pairs={{0,24},{4,28},{8,0},{12,4},{16,8},{20,12},{24,16},{28,20},{32,56},... | collective-permute-start | bytes 319496 | tf_op jit(solution)/shard_map/ppermute | solution.py:629
  8.0 6.2 %collective-permute-start.3 = (bf16[208,256]{1,0:T(8,128)(2,1)S(1)}, bf16[208,256]{1,0:T(8,128)(2,1)S(1)}, u32[]{:S(2)}, u32[]{:S(2)}) collective-permute-start(bf16[208,256]{1,0:T(8,128)(2,1)S(1)} %get-tuple-element.262.refs_0_), channel_id=1, source_target_pairs={{0,16},{4,20},{8,24},{12,28},{16,0},{20,4},{24,8},{28,12},{32,48},... | collective-permute-start | bytes 319496 | tf_op jit(solution)/shard_map/ppermute | solution.py:629
  9.8 4.5 %collective-permute-start.4 = (bf16[208,256]{1,0:T(8,128)(2,1)S(1)}, bf16[208,256]{1,0:T(8,128)(2,1)S(1)}, u32[]{:S(2)}, u32[]{:S(2)}) collective-permute-start(bf16[208,256]{1,0:T(8,128)(2,1)S(1)} %get-tuple-element.262.refs_0_), channel_id=1, source_target_pairs={{0,4},{4,0},{8,12},{12,8},{16,20},{20,16},{24,28},{28,24},{32,36},... | collective-permute-start | bytes 319496 | tf_op jit(solution)/shard_map/ppermute | solution.py:629
  10.7 3.6 %collective-permute-start.5 = (bf16[208,256]{1,0:T(8,128)(2,1)S(1)}, bf16[208,256]{1,0:T(8,128)(2,1)S(1)}, u32[]{:S(2)}, u32[]{:S(2)}) collective-permute-start(bf16[208,256]{1,0:T(8,128)(2,1)S(1)} %collective-permute-done.1.refs_1_), channel_id=1, source_target_pairs={{0,4},{4,0},{8,12},{12,8},{16,20},{20,16},{24,28},{28,24},{32,36},... | collective-permute-start | bytes 319496 | tf_op jit(solution)/shard_map/ppermute | solution.py:629
  12.6 1.8 %collective-permute-start.6 = (bf16[208,256]{1,0:T(8,128)(2,1)S(1)}, bf16[208,256]{1,0:T(8,128)(2,1)S(1)}, u32[]{:S(2)}, u32[]{:S(2)}) collective-permute-start(bf16[208,256]{1,0:T(8,128)(2,1)S(1)} %collective-permute-done.2.refs_2_), channel_id=1, source_target_pairs={{0,4},{4,0},{8,12},{12,8},{16,20},{20,16},{24,28},{28,24},{32,36},... | collective-permute-start | bytes 319496 | tf_op jit(solution)/shard_map/ppermute | solution.py:629
  14.2 1.3 %collective-permute-start.7 = (bf16[208,256]{1,0:T(8,128)(2,1)S(1)}, bf16[208,256]{1,0:T(8,128)(2,1)S(1)}, u32[]{:S(2)}, u32[]{:S(2)}) collective-permute-start(bf16[208,256]{1,0:T(8,128)(2,1)S(1)} %collective-permute-done.3.refs_3_), channel_id=1, source_target_pairs={{0,4},{4,0},{8,12},{12,8},{16,20},{20,16},{24,28},{28,24},{32,36},... | collective-permute-start | bytes 319496 | tf_op jit(solution)/shard_map/ppermute | solution.py:629
  16.9 8.8 %collective-permute-start.8 = (bf16[720,256]{1,0:T(8,128)(2,1)S(1)}, bf16[720,256]{1,0:T(8,128)(2,1)S(1)}, u32[]{:S(2)}, u32[]{:S(2)}) collective-permute-start(bf16[720,256]{1,0:T(8,128)(2,1)S(1)} %compact.1.refs_0_), channel_id=1, source_target_pairs={{0,32},{4,228},{8,40},{12,236},{16,48},{20,244},{24,56},{28,252},{... | collective-permute-start | bytes 1105928 | tf_op jit(solution)/shard_map/ppermute | solution.py:629
  25.7 8.7 %collective-permute-start.9 = (bf16[720,256]{1,0:T(8,128)(2,1)S(1)}, bf16[720,256]{1,0:T(8,128)(2,1)S(1)}, u32[]{:S(2)}, u32[]{:S(2)}) collective-permute-start(bf16[720,256]{1,0:T(8,128)(2,1)S(1)} %collective-permute-done.8.refs_1_), channel_id=1, source_target_pairs={{0,32},{4,228},{8,40},{12,236},{16,48},{20,244},{24,56},{28,252},{... | collective-permute-start | bytes 1105928 | tf_op jit(solution)/shard_map/ppermute | solution.py:629
  25.7 8.7 %collective-permute-start.11 = (bf16[720,256]{1,0:T(8,128)(2,1)S(1)}, bf16[720,256]{1,0:T(8,128)(2,1)S(1)}, u32[]{:S(2)}, u32[]{:S(2)}) collective-permute-start(bf16[720,256]{1,0:T(8,128)(2,1)S(1)} %collective-permute-done.8.refs_1_), channel_id=1, source_target_pairs={{0,4},{4,0},{8,12},{12,8},{16,20},{20,16},{24,28},{28,24},{32,36},... | collective-permute-start | bytes 1105928 | tf_op jit(solution)/shard_map/ppermute | solution.py:629
  34.4 1.7 %collective-permute-start.12 = (bf16[720,256]{1,0:T(8,128)(2,1)S(1)}, bf16[720,256]{1,0:T(8,128)(2,1)S(1)}, u32[]{:S(2)}, u32[]{:S(2)}) collective-permute-start(bf16[720,256]{1,0:T(8,128)(2,1)S(1)} %collective-permute-done.9.refs_2_), channel_id=1, source_target_pairs={{0,4},{4,0},{8,12},{12,8},{16,20},{20,16},{24,28},{28,24},{32,36},... | collective-permute-start | bytes 1105928 | tf_op jit(solution)/shard_map/ppermute | solution.py:629
  34.4 8.7 %collective-permute-start.10 = (bf16[720,256]{1,0:T(8,128)(2,1)S(1)}, bf16[720,256]{1,0:T(8,128)(2,1)S(1)}, u32[]{:S(2)}, u32[]{:S(2)}) collective-permute-start(bf16[720,256]{1,0:T(8,128)(2,1)S(1)} %collective-permute-done.9.refs_2_), channel_id=1, source_target_pairs={{0,32},{4,228},{8,40},{12,236},{16,48},{20,244},{24,56},{28,252},{... | collective-permute-start | bytes 1105928 | tf_op jit(solution)/shard_map/ppermute | solution.py:629
  40.0 11.4 %copy-start.3 = (bf16[512,1024]{1,0:T(8,128)(2,1)S(1)}, bf16[512,1024]{1,0:T(8,128)(2,1)}, u32[]{:S(2)}) copy-start(bf16[512,1024]{1,0:T(8,128)(2,1)} %wout_ref.1) | copy-start | bytes 3145732
  43.2 1.7 %collective-permute-start.14 = (bf16[720,256]{1,0:T(8,128)(2,1)S(1)}, bf16[720,256]{1,0:T(8,128)(2,1)S(1)}, u32[]{:S(2)}, u32[]{:S(2)}) collective-permute-start(bf16[720,256]{1,0:T(8,128)(2,1)S(1)} %collective-permute-done.10.came), channel_id=1, source_target_pairs={{0,4},{4,0},{8,12},{12,8},{16,20},{20,16},{24,28},{28,24},{32,36},... | collective-permute-start | bytes 1105928 | tf_op jit(solution)/shard_map/ppermute | solution.py:629
  43.2 6.9 %collective-permute-start.13 = (bf16[368,256]{1,0:T(8,128)(2,1)S(1)}, bf16[368,256]{1,0:T(8,128)(2,1)S(1)}, u32[]{:S(2)}, u32[]{:S(2)}) collective-permute-start(bf16[368,256]{1,0:T(8,128)(2,1)S(1)} %constant_dynamic-slice_fusion.4), channel_id=1, source_target_pairs={{0,32},{4,228},{8,40},{12,236},{16,48},{20,244},{24,56},{28,252},{... | collective-permute-start | bytes 565256 | tf_op jit(solution)/shard_map/ppermute | solution.py:629
  50.0 1.4 %collective-permute-start.15 = (bf16[368,256]{1,0:T(8,128)(2,1)S(1)}, bf16[368,256]{1,0:T(8,128)(2,1)S(1)}, u32[]{:S(2)}, u32[]{:S(2)}) collective-permute-start(bf16[368,256]{1,0:T(8,128)(2,1)S(1)} %collective-permute-done.13.came), channel_id=1, source_target_pairs={{0,4},{4,0},{8,12},{12,8},{16,20},{20,16},{24,28},{28,24},{32,36},... | collective-permute-start | bytes 565256 | tf_op jit(solution)/shard_map/ppermute | solution.py:629
  54.5 9.2 %copy-start = (bf16[512,256]{1,0:T(8,128)(2,1)S(1)}, bf16[512,256]{1,0:T(8,128)(2,1)}, u32[]{:S(2)}) copy-start(bf16[512,256]{1,0:T(8,128)(2,1)} %skip_ref.1) | copy-start | bytes 786436
  54.5 9.1 %copy-start.2 = (s32[1,192]{1,0:T(1,128)S(1)}, s32[1,192]{1,0:T(1,128)}, u32[]{:S(2)}) copy-start(s32[1,192]{1,0:T(1,128)} %len_ref.1) | copy-start | bytes 2308
  54.5 11.4 %copy-start.1 = (f32[31,256]{1,0:T(8,128)S(1)}, f32[31,256]{1,0:T(8,128)}, u32[]{:S(2)}) copy-start(f32[31,256]{1,0:T(8,128)} %taps_ref.3) | copy-start | bytes 95236
  54.6 6.7 %collective-permute-start.16 = (bf16[192,256]{1,0:T(8,128)(2,1)S(1)}, bf16[192,256]{1,0:T(8,128)(2,1)S(1)}, u32[]{:S(2)}, u32[]{:S(2)}) collective-permute-start(bf16[192,256]{1,0:T(8,128)(2,1)S(1)} %get-tuple-element.291), channel_id=1, source_target_pairs={{0,2},{1,3},{2,0},{3,1},{4,6},{5,7},{6,4},{7,5},{8,10},{9,11},{10,... | collective-permute-start | bytes 294920 | tf_op jit(solution)/shard_map/ppermute | solution.py:665
  57.8 5.8 %collective-permute-start.17 = (bf16[192,256]{1,0:T(8,128)(2,1)S(1)}, bf16[192,256]{1,0:T(8,128)(2,1)S(1)}, u32[]{:S(2)}, u32[]{:S(2)}) collective-permute-start(bf16[192,256]{1,0:T(8,128)(2,1)S(1)} %get-tuple-element.292), channel_id=1, source_target_pairs={{0,1},{1,2},{2,3},{3,0},{4,5},{5,6},{6,7},{7,4},{8,9},{9,10},{10,1... | collective-permute-start | bytes 294920 | tf_op jit(solution)/shard_map/ppermute | solution.py:665
  58.5 5.2 %collective-permute-start.18 = (bf16[192,256]{1,0:T(8,128)(2,1)S(1)}, bf16[192,256]{1,0:T(8,128)(2,1)S(1)}, u32[]{:S(2)}, u32[]{:S(2)}) collective-permute-start(bf16[192,256]{1,0:T(8,128)(2,1)S(1)} %get-tuple-element.293), channel_id=1, source_target_pairs={{0,3},{1,0},{2,1},{3,2},{4,7},{5,4},{6,5},{7,6},{8,11},{9,8},{10,9... | collective-permute-start | bytes 294920 | tf_op jit(solution)/shard_map/ppermute | solution.py:665
  64.0 8.4 %collective-permute-start.19 = (bf16[32,256]{1,0:T(8,128)(2,1)S(1)}, bf16[32,256]{1,0:T(8,128)(2,1)S(1)}, u32[]{:S(2)}, u32[]{:S(2)}) collective-permute-start(bf16[32,256]{1,0:T(8,128)(2,1)S(1)} %get-tuple-element.295), channel_id=1, source_target_pairs={{0,4},{4,8},{8,12},{12,16},{16,20},{20,24},{24,28},{28,32},{32,36}... | collective-permute-start | bytes 49160 | tf_op jit(solution)/shard_map/ppermute | solution.py:668
